TPU v7x, 512 devices: a whole 4x8x8 slice. The times are simulated.
512 devices in a mesh: head: 32 (over x, y_lo, core), ctx: 16 (over z, y_hi).
Axes of the slice: x: 4, y: 8 (y_hi: 2, y_lo: 4; y = y_hi * 4 + y_lo), z: 8, core: 2. Of those that a mesh axis runs over, the one named last changes fastest.
Arguments:
- queries: bfloat16 [8192, 8192], P(('head', 'ctx')), may hold values from -6 to 6
- keys: bfloat16 [8192, 8192], P(('head', 'ctx')), may hold values from -6 to 6
- values: bfloat16 [8192, 8192], P(('head', 'ctx')), may hold values from -6 to 6
- doc_lengths: int32 [8], replicated, may hold values from 1 to 4096, 8192 in all
- slab_owner: int32 [512], replicated, may hold values from 0 to 15, as said below
Outputs:
- context: bfloat16 [8192, 8192], P('ctx', 'head')
Inputs may be any that keep to these rules, and one draw needn't show every extreme that they name: `doc_lengths`: the 8 lengths sum to 8192 and the longest is exactly 4096. `slab_owner`: slab h * 16 + c lies on the device of head index h and ctx index c. Every owner receives exactly 32 slabs. Of the 32 slabs that share one ctx index, at most 4 go to one owner, and for every ctx index some owner receives exactly 4 of them.
All inputs are finite; a program needn't handle non-finite values.
Results may differ from a plain program's by a relative error of at most 0.0065.
Values may be sent and summed in bfloat16 or wider, within the bound.
No kernel may reach another device: no remote copies, remote signals or barrier semaphores. Data moves between devices by JAX's collectives and lax.ppermute only.
A program may use at most 64 MiB of HBM per device.

v0:
```python
import jax
import jax.numpy as jnp
from jax import lax
from jax.sharding import PartitionSpec as P

DH = 128


def from_behind(block, axis, distance):
    devices = range(lax.axis_size(axis))
    route = [((i - distance) % len(devices), i) for i in devices]
    return lax.ppermute(block, axis, route)


def slab_tables(slab_owner, n_head, n_ctx):
    slab_index = jnp.arange(n_head * n_ctx, dtype=jnp.int32)
    earlier = slab_index[None, :] < slab_index[:, None]
    same_owner = slab_owner[:, None] == slab_owner[None, :]
    owner_rank = jnp.sum((same_owner & earlier).astype(jnp.int32), axis=1)
    owner_grid = slab_owner.reshape(n_head, n_ctx)
    head_index = jnp.arange(n_head, dtype=jnp.int32)
    lower_head = head_index[None, :] < head_index[:, None]
    same_column = owner_grid[:, None, :] == owner_grid[None, :, :]
    send_rank = jnp.sum((same_column & lower_head[:, :, None]).astype(jnp.int32), axis=1)
    return (owner_rank, owner_grid, send_rank)


def attend(running, query, query_pos, query_doc, key_value, first_row, positions, documents):
    head_count = running[0].shape[0]
    key_count = key_value.shape[1]
    key_pos = lax.dynamic_slice_in_dim(positions, first_row, key_count)
    key_doc = lax.dynamic_slice_in_dim(documents, first_row, key_count)
    allowed = (query_doc[:, None] == key_doc[None, :]) & (key_pos[None, :] <= query_pos[:, None])
    old_high, old_denom, old_weighted = running
    query_three = query.reshape(query.shape[0], head_count, DH)
    key_three = key_value[0].reshape(key_count, head_count, DH)
    value_three = key_value[1].reshape(key_count, head_count, DH)
    scores = jnp.einsum(
        "qhd,khd->hqk", query_three, key_three, preferred_element_type=jnp.float32
    ) * DH ** (-0.5)
    scores = jnp.where(allowed[None], scores, -1e30)
    new_high = jnp.maximum(old_high, jnp.max(scores, axis=2))
    weights = jnp.where(allowed[None], jnp.exp(scores - new_high[:, :, None]), 0.0)
    rescale = jnp.exp(old_high - new_high)
    new_denom = old_denom * rescale + jnp.sum(weights, axis=2)
    new_weighted = old_weighted * rescale[:, :, None] + jnp.einsum(
        "hqk,khd->hqd",
        weights.astype(jnp.bfloat16),
        value_three,
        preferred_element_type=jnp.float32,
    )
    return (new_high, new_denom, new_weighted)


def empty_state(head_count, rows):
    return (
        jnp.full((head_count, rows), -1e30, jnp.float32),
        jnp.zeros((head_count, rows), jnp.float32),
        jnp.zeros((head_count, rows, DH), jnp.float32),
    )


def per_device(queries, keys, values, doc_lengths, slab_owner):
    n_head = lax.axis_size("head")
    n_ctx = lax.axis_size("ctx")
    owner_self = lax.axis_index("ctx")
    slab_rows = queries.shape[0]
    tok_dev = slab_rows * n_head
    group = n_head // n_ctx
    capacity = 2 * group
    owner_rank, owner_grid, send_rank = slab_tables(slab_owner, n_head, n_ctx)
    slab_index = jnp.arange(n_head * n_ctx, dtype=jnp.int32)
    owner_index = jnp.arange(n_ctx, dtype=jnp.int32)
    rank_index = jnp.arange(n_head, dtype=jnp.int32)
    row_offsets = jnp.arange(slab_rows, dtype=jnp.int32)
    spread = (
        lax.all_to_all(queries, "head", split_axis=1, concat_axis=0, tiled=True),
        lax.all_to_all(keys, "head", split_axis=1, concat_axis=0, tiled=True),
        lax.all_to_all(values, "head", split_axis=1, concat_axis=0, tiled=True),
    )
    row_width = spread[0].shape[1]
    head_count = row_width // DH
    target = lax.dynamic_index_in_dim(owner_grid, owner_self, 1, keepdims=False)
    target_rank = lax.dynamic_index_in_dim(send_rank, owner_self, 1, keepdims=False)
    slot_index = jnp.arange(capacity, dtype=jnp.int32)
    picked = (target[None, None, :] == owner_index[:, None, None]) & (
        target_rank[None, None, :] == slot_index[None, :, None]
    )
    source_slab = jnp.sum(jnp.where(picked, rank_index[None, None, :], 0), axis=2) + n_head * (
        1 - jnp.any(picked, axis=2).astype(jnp.int32)
    )
    source_slab = source_slab.reshape(-1)
    mine = (slab_owner[None, :] == owner_self) & (owner_rank[None, :] == rank_index[:, None])
    slot_all = slab_index % n_ctx * capacity + send_rank.reshape(-1)
    slot_of = jnp.sum(jnp.where(mine, slot_all[None, :], 0), axis=1)

    def pack_rows(block):
        padded = jnp.concatenate(
            [
                block.reshape(n_head, slab_rows, row_width),
                jnp.zeros((1, slab_rows, row_width), block.dtype),
            ],
            axis=0,
        )
        return jnp.take(padded, source_slab, axis=0).reshape(
            n_ctx * capacity * slab_rows, row_width
        )

    def unpack_rows(block):
        return jnp.take(
            block.reshape(n_ctx * capacity, slab_rows, row_width), slot_of, axis=0
        ).reshape(tok_dev, row_width)

    arrived = (
        lax.all_to_all(pack_rows(spread[0]), "ctx", split_axis=0, concat_axis=0, tiled=True),
        lax.all_to_all(pack_rows(spread[1]), "ctx", split_axis=0, concat_axis=0, tiled=True),
        lax.all_to_all(pack_rows(spread[2]), "ctx", split_axis=0, concat_axis=0, tiled=True),
    )
    query = unpack_rows(arrived[0])
    key_value = jnp.stack([unpack_rows(arrived[1]), unpack_rows(arrived[2])])
    placed = (slab_owner[None, None, :] == owner_index[:, None, None]) & (
        owner_rank[None, None, :] == rank_index[None, :, None]
    )
    slab_at = jnp.sum(jnp.where(placed, slab_index[None, None, :], 0), axis=2)
    positions = (slab_at[:, :, None] * slab_rows + row_offsets[None, None, :]).reshape(-1)
    doc_ends = jnp.cumsum(doc_lengths)[:-1]
    documents = jnp.sum((positions[:, None] >= doc_ends[None, :]).astype(jnp.int32), axis=1)
    query_pos = lax.dynamic_slice_in_dim(positions, owner_self * tok_dev, tok_dev)
    query_doc = lax.dynamic_slice_in_dim(documents, owner_self * tok_dev, tok_dev)

    def cycle_hop(hop_index, carried):
        running, moving = carried
        source = (owner_self - hop_index) % n_ctx
        running = attend(
            running, query, query_pos, query_doc, moving, source * tok_dev, positions, documents
        )
        moving = from_behind(moving, "ctx", 1)
        return (running, moving)

    running, moving = lax.fori_loop(
        0, n_ctx - 1, cycle_hop, (empty_state(head_count, tok_dev), key_value)
    )
    source = (owner_self - (n_ctx - 1)) % n_ctx
    running = attend(
        running, query, query_pos, query_doc, moving, source * tok_dev, positions, documents
    )
    highest, denominator, weighted = running
    attended = weighted / denominator[:, :, None]
    attended = attended.transpose(1, 0, 2).reshape(tok_dev, row_width).astype(jnp.bfloat16)
    return attended


def solution(mesh):
    return jax.shard_map(
        per_device,
        mesh=mesh,
        in_specs=(
            P(("head", "ctx"), None),
            P(("head", "ctx"), None),
            P(("head", "ctx"), None),
            P(),
            P(),
        ),
        out_specs=P("ctx", "head"),
        check_vma=False,
    )
```

profile of v0, /device:TPU:278, one launch (start us, length us, event | category | flops | bytes accessed | tf_op | source)
XLA Modules:
  0.0 577.2 jit_solution(16170439540065857675)
XLA Ops:
  0.0 1.7 copy.90
  1.7 7.8 %all-to-all-start.4 = ((bf16[16,32,256]{2,0,1:T(8,128)(2,1)}), bf16[16,32,256]{2,0,1:T(8,128)(2,1)S(1)}, u32[]{:S(2)}, u32[]{:S(2)}) async-start(bf16[16,32,256]{2,0,1:T(8,128)(2,1)} %bitcast.34), calls=%async_computation.4 | async-start | bytes 524288 | tf_op jit(solution)/shard_map/all_to_all | solution.py:77
  10.4 1.7 copy.92
  13.0 4.1 all-to-all-done.4
  17.0 7.5 %all-to-all-start = ((bf16[16,32,256]{2,0,1:T(8,128)(2,1)}), bf16[16,32,256]{2,0,1:T(8,128)(2,1)S(1)}, u32[]{:S(2)}, u32[]{:S(2)}) async-start(bf16[16,32,256]{2,0,1:T(8,128)(2,1)} %bitcast.36), calls=%async_computation | async-start | bytes 524288 | tf_op jit(solution)/shard_map/all_to_all | solution.py:78
  25.8 6.2 %all-to-all-done = bf16[16,32,256]{2,0,1:T(8,128)(2,1)S(1)} async-done(((bf16[16,32,256]{2,0,1:T(8,128)(2,1)}), bf16[16,32,256]{2,0,1:T(8,128)(2,1)S(1)}, u32[]{:S(2)}, u32[]{:S(2)}) %all-to-all-start) | async-done | bytes 262176 | tf_op jit(solution)/shard_map/all_to_all | solution.py:78
  31.9 7.5 %all-to-all-start.2 = ((bf16[16,32,256]{2,0,1:T(8,128)(2,1)}), bf16[16,32,256]{2,0,1:T(8,128)(2,1)S(1)}, u32[]{:S(2)}, u32[]{:S(2)}) async-start(bf16[16,32,256]{2,0,1:T(8,128)(2,1)} %bitcast.35), calls=%async_computation.2 | async-start | bytes 524288 | tf_op jit(solution)/shard_map/all_to_all | solution.py:79
  40.8 6.1 %all-to-all-done.2 = bf16[16,32,256]{2,0,1:T(8,128)(2,1)S(1)} async-done(((bf16[16,32,256]{2,0,1:T(8,128)(2,1)}), bf16[16,32,256]{2,0,1:T(8,128)(2,1)S(1)}, u32[]{:S(2)}, u32[]{:S(2)}) %all-to-all-start.2) | async-done | bytes 262176 | tf_op jit(solution)/shard_map/all_to_all | solution.py:79
  49.0 10.0 %all-to-all-start.1 = ((bf16[16,64,256]{2,1,0:T(8,128)(2,1)}), bf16[16,64,256]{2,1,0:T(8,128)(2,1)S(1)}, u32[]{:S(2)}, u32[]{:S(2)}) async-start(bf16[16,64,256]{2,1,0:T(8,128)(2,1)} %bitcast.1), calls=%async_computation.1 | async-start | bytes 1048576 | tf_op jit(solution)/shard_map/all_to_all | solution.py:116
  59.7 16.5 %all-to-all-done.1 = bf16[16,64,256]{2,1,0:T(8,128)(2,1)S(1)} async-done(((bf16[16,64,256]{2,1,0:T(8,128)(2,1)}), bf16[16,64,256]{2,1,0:T(8,128)(2,1)S(1)}, u32[]{:S(2)}, u32[]{:S(2)}) %all-to-all-start.1) | async-done | bytes 524320 | tf_op jit(solution)/shard_map/all_to_all | solution.py:116
  76.2 8.4 %all-to-all-start.3 = ((bf16[16,64,256]{2,1,0:T(8,128)(2,1)}), bf16[16,64,256]{2,1,0:T(8,128)(2,1)S(1)}, u32[]{:S(2)}, u32[]{:S(2)}) async-start(bf16[16,64,256]{2,1,0:T(8,128)(2,1)} %bitcast.5), calls=%async_computation.3 | async-start | bytes 1048576 | tf_op jit(solution)/shard_map/all_to_all | solution.py:117
  85.2 15.2 %all-to-all-done.3 = bf16[16,64,256]{2,1,0:T(8,128)(2,1)S(1)} async-done(((bf16[16,64,256]{2,1,0:T(8,128)(2,1)}), bf16[16,64,256]{2,1,0:T(8,128)(2,1)S(1)}, u32[]{:S(2)}, u32[]{:S(2)}) %all-to-all-start.3) | async-done | bytes 524320 | tf_op jit(solution)/shard_map/all_to_all | solution.py:117
  100.4 8.3 %all-to-all-start.5 = ((bf16[16,64,256]{2,1,0:T(8,128)(2,1)}), bf16[16,64,256]{2,1,0:T(8,128)(2,1)S(1)}, u32[]{:S(2)}, u32[]{:S(2)}) async-start(bf16[16,64,256]{2,1,0:T(8,128)(2,1)} %bitcast.11), calls=%async_computation.5 | async-start | bytes 1048576 | tf_op jit(solution)/shard_map/all_to_all | solution.py:115
  111.1 13.6 %all-to-all-done.5 = bf16[16,64,256]{2,1,0:T(8,128)(2,1)S(1)} async-done(((bf16[16,64,256]{2,1,0:T(8,128)(2,1)}), bf16[16,64,256]{2,1,0:T(8,128)(2,1)S(1)}, u32[]{:S(2)}, u32[]{:S(2)}) %all-to-all-start.5) | async-done | bytes 524320 | tf_op jit(solution)/shard_map/all_to_all | solution.py:115
  127.3 445.7 %while.23 = (s32[]{:T(128)}, f32[2,512]{1,0:T(2,128)S(1)}, f32[2,512]{1,0:T(2,128)S(1)}, f32[2,512,128]{2,1,0:T(8,128)}, bf16[2,512,256]{1,2,0:T(8,128)(2,1)S(1)...) while((s32[]{:T(128)}, f32[2,512]{1,0:T(2,128)S(1)}, ...), condition=%wide.wide.region_11.14_spmd.clone, body=%wide.wide.region_8.13_spmd.clone.sunk | while | flops 276435968 | bytes 13451656 | solution.py:140
  127.3 3.2 collective-permute-start
  131.9 1.7 fusion.65
  134.2 2.7 convolution_add_fusion.4
  136.9 10.6 %collective-permute-done = bf16[2,512,256]{1,2,0:T(8,128)(2,1)S(1)} collective-permute-done((bf16[2,512,256]{1,2,0:T(8,128)(2,1)S(1)}, bf16[2,512,256]{1,2,0:T(8,128)(2,1)S(1)}, u32[]{:S(2)}, u32[]{:S(2)}) %collective-permute-start) | collective-permute-done | bytes 524320 | tf_op jit(solution)/shard_map/while/body/eval_jaxpr/ppermute | solution.py:12
  147.6 13.3 %collective-permute-start = (bf16[2,512,256]{1,2,0:T(8,128)(2,1)S(1)}, bf16[2,512,256]{1,2,0:T(8,128)(2,1)S(1)}, u32[]{:S(2)}, u32[]{:S(2)}) collective-permute-start(bf16[2,512,256]{1,2,0:T(8,128)(2,1)S(1)} %copy.105), channel_id=1, source_target_pairs={{15,0},{0,1},{1,2},{2,3},{3,4},{4,5},{5,6},{6,7},{7,8},{8,9},{9,10... | collective-permute-start | bytes 1572872 | tf_op jit(solution)/shard_map/while/body/eval_jaxpr/ppermute | solution.py:12
  164.5 2.9 convolution_add_fusion.4
  167.4 14.1 %collective-permute-done = bf16[2,512,256]{1,2,0:T(8,128)(2,1)S(1)} collective-permute-done((bf16[2,512,256]{1,2,0:T(8,128)(2,1)S(1)}, bf16[2,512,256]{1,2,0:T(8,128)(2,1)S(1)}, u32[]{:S(2)}, u32[]{:S(2)}) %collective-permute-start) | collective-permute-done | bytes 524320 | tf_op jit(solution)/shard_map/while/body/eval_jaxpr/ppermute | solution.py:12
  181.5 8.4 %collective-permute-start = (bf16[2,512,256]{1,2,0:T(8,128)(2,1)S(1)}, bf16[2,512,256]{1,2,0:T(8,128)(2,1)S(1)}, u32[]{:S(2)}, u32[]{:S(2)}) collective-permute-start(bf16[2,512,256]{1,2,0:T(8,128)(2,1)S(1)} %copy.105), channel_id=1, source_target_pairs={{15,0},{0,1},{1,2},{2,3},{3,4},{4,5},{5,6},{6,7},{7,8},{8,9},{9,10... | collective-permute-start | bytes 1572872 | tf_op jit(solution)/shard_map/while/body/eval_jaxpr/ppermute | solution.py:12
  193.5 2.9 convolution_add_fusion.4
  196.4 14.8 %collective-permute-done = bf16[2,512,256]{1,2,0:T(8,128)(2,1)S(1)} collective-permute-done((bf16[2,512,256]{1,2,0:T(8,128)(2,1)S(1)}, bf16[2,512,256]{1,2,0:T(8,128)(2,1)S(1)}, u32[]{:S(2)}, u32[]{:S(2)}) %collective-permute-start) | collective-permute-done | bytes 524320 | tf_op jit(solution)/shard_map/while/body/eval_jaxpr/ppermute | solution.py:12
  211.2 3.3 collective-permute-start
  215.8 1.7 fusion.65
  218.1 2.9 convolution_add_fusion.4
  221.0 32.4 %collective-permute-done = bf16[2,512,256]{1,2,0:T(8,128)(2,1)S(1)} collective-permute-done((bf16[2,512,256]{1,2,0:T(8,128)(2,1)S(1)}, bf16[2,512,256]{1,2,0:T(8,128)(2,1)S(1)}, u32[]{:S(2)}, u32[]{:S(2)}) %collective-permute-start) | collective-permute-done | bytes 524320 | tf_op jit(solution)/shard_map/while/body/eval_jaxpr/ppermute | solution.py:12
  253.5 1.9 collective-permute-start
  259.0 2.9 convolution_add_fusion.4
  261.9 24.6 %collective-permute-done = bf16[2,512,256]{1,2,0:T(8,128)(2,1)S(1)} collective-permute-done((bf16[2,512,256]{1,2,0:T(8,128)(2,1)S(1)}, bf16[2,512,256]{1,2,0:T(8,128)(2,1)S(1)}, u32[]{:S(2)}, u32[]{:S(2)}) %collective-permute-start) | collective-permute-done | bytes 524320 | tf_op jit(solution)/shard_map/while/body/eval_jaxpr/ppermute | solution.py:12
  286.6 1.9 collective-permute-start
  289.8 1.7 fusion.65
  292.1 2.9 convolution_add_fusion.4
  295.0 21.7 %collective-permute-done = bf16[2,512,256]{1,2,0:T(8,128)(2,1)S(1)} collective-permute-done((bf16[2,512,256]{1,2,0:T(8,128)(2,1)S(1)}, bf16[2,512,256]{1,2,0:T(8,128)(2,1)S(1)}, u32[]{:S(2)}, u32[]{:S(2)}) %collective-permute-start) | collective-permute-done | bytes 524320 | tf_op jit(solution)/shard_map/while/body/eval_jaxpr/ppermute | solution.py:12
  316.8 1.9 collective-permute-start
  322.3 2.9 convolution_add_fusion.4
  325.2 22.8 %collective-permute-done = bf16[2,512,256]{1,2,0:T(8,128)(2,1)S(1)} collective-permute-done((bf16[2,512,256]{1,2,0:T(8,128)(2,1)S(1)}, bf16[2,512,256]{1,2,0:T(8,128)(2,1)S(1)}, u32[]{:S(2)}, u32[]{:S(2)}) %collective-permute-start) | collective-permute-done | bytes 524320 | tf_op jit(solution)/shard_map/while/body/eval_jaxpr/ppermute | solution.py:12
  348.1 1.9 collective-permute-start
  353.6 2.9 convolution_add_fusion.4
  356.5 20.0 %collective-permute-done = bf16[2,512,256]{1,2,0:T(8,128)(2,1)S(1)} collective-permute-done((bf16[2,512,256]{1,2,0:T(8,128)(2,1)S(1)}, bf16[2,512,256]{1,2,0:T(8,128)(2,1)S(1)}, u32[]{:S(2)}, u32[]{:S(2)}) %collective-permute-start) | collective-permute-done | bytes 524320 | tf_op jit(solution)/shard_map/while/body/eval_jaxpr/ppermute | solution.py:12
  376.5 1.9 collective-permute-start
  382.0 2.9 convolution_add_fusion.4
  384.9 20.1 %collective-permute-done = bf16[2,512,256]{1,2,0:T(8,128)(2,1)S(1)} collective-permute-done((bf16[2,512,256]{1,2,0:T(8,128)(2,1)S(1)}, bf16[2,512,256]{1,2,0:T(8,128)(2,1)S(1)}, u32[]{:S(2)}, u32[]{:S(2)}) %collective-permute-start) | collective-permute-done | bytes 524320 | tf_op jit(solution)/shard_map/while/body/eval_jaxpr/ppermute | solution.py:12
  405.1 2.5 collective-permute-start
  411.2 2.9 convolution_add_fusion.4
  414.1 12.9 %collective-permute-done = bf16[2,512,256]{1,2,0:T(8,128)(2,1)S(1)} collective-permute-done((bf16[2,512,256]{1,2,0:T(8,128)(2,1)S(1)}, bf16[2,512,256]{1,2,0:T(8,128)(2,1)S(1)}, u32[]{:S(2)}, u32[]{:S(2)}) %collective-permute-start) | collective-permute-done | bytes 524320 | tf_op jit(solution)/shard_map/while/body/eval_jaxpr/ppermute | solution.py:12
  427.1 8.0 %collective-permute-start = (bf16[2,512,256]{1,2,0:T(8,128)(2,1)S(1)}, bf16[2,512,256]{1,2,0:T(8,128)(2,1)S(1)}, u32[]{:S(2)}, u32[]{:S(2)}) collective-permute-start(bf16[2,512,256]{1,2,0:T(8,128)(2,1)S(1)} %copy.105), channel_id=1, source_target_pairs={{15,0},{0,1},{1,2},{2,3},{3,4},{4,5},{5,6},{6,7},{7,8},{8,9},{9,10... | collective-permute-start | bytes 1572872 | tf_op jit(solution)/shard_map/while/body/eval_jaxpr/ppermute | solution.py:12
  438.7 2.9 convolution_add_fusion.4
  441.6 10.5 %collective-permute-done = bf16[2,512,256]{1,2,0:T(8,128)(2,1)S(1)} collective-permute-done((bf16[2,512,256]{1,2,0:T(8,128)(2,1)S(1)}, bf16[2,512,256]{1,2,0:T(8,128)(2,1)S(1)}, u32[]{:S(2)}, u32[]{:S(2)}) %collective-permute-start) | collective-permute-done | bytes 524320 | tf_op jit(solution)/shard_map/while/body/eval_jaxpr/ppermute | solution.py:12
  452.1 8.3 %collective-permute-start = (bf16[2,512,256]{1,2,0:T(8,128)(2,1)S(1)}, bf16[2,512,256]{1,2,0:T(8,128)(2,1)S(1)}, u32[]{:S(2)}, u32[]{:S(2)}) collective-permute-start(bf16[2,512,256]{1,2,0:T(8,128)(2,1)S(1)} %copy.105), channel_id=1, source_target_pairs={{15,0},{0,1},{1,2},{2,3},{3,4},{4,5},{5,6},{6,7},{7,8},{8,9},{9,10... | collective-permute-start | bytes 1572872 | tf_op jit(solution)/shard_map/while/body/eval_jaxpr/ppermute | solution.py:12
  461.7 1.7 fusion.65
  464.0 2.9 convolution_add_fusion.4
  466.9 27.1 %collective-permute-done = bf16[2,512,256]{1,2,0:T(8,128)(2,1)S(1)} collective-permute-done((bf16[2,512,256]{1,2,0:T(8,128)(2,1)S(1)}, bf16[2,512,256]{1,2,0:T(8,128)(2,1)S(1)}, u32[]{:S(2)}, u32[]{:S(2)}) %collective-permute-start) | collective-permute-done | bytes 524320 | tf_op jit(solution)/shard_map/while/body/eval_jaxpr/ppermute | solution.py:12
  494.0 1.9 collective-permute-start
  499.5 2.9 convolution_add_fusion.4
  502.4 24.6 %collective-permute-done = bf16[2,512,256]{1,2,0:T(8,128)(2,1)S(1)} collective-permute-done((bf16[2,512,256]{1,2,0:T(8,128)(2,1)S(1)}, bf16[2,512,256]{1,2,0:T(8,128)(2,1)S(1)}, u32[]{:S(2)}, u32[]{:S(2)}) %collective-permute-start) | collective-permute-done | bytes 524320 | tf_op jit(solution)/shard_map/while/body/eval_jaxpr/ppermute | solution.py:12
  527.0 1.9 collective-permute-start
  532.6 2.9 convolution_add_fusion.4
  535.5 20.4 %collective-permute-done = bf16[2,512,256]{1,2,0:T(8,128)(2,1)S(1)} collective-permute-done((bf16[2,512,256]{1,2,0:T(8,128)(2,1)S(1)}, bf16[2,512,256]{1,2,0:T(8,128)(2,1)S(1)}, u32[]{:S(2)}, u32[]{:S(2)}) %collective-permute-start) | collective-permute-done | bytes 524320 | tf_op jit(solution)/shard_map/while/body/eval_jaxpr/ppermute | solution.py:12
  555.9 1.9 collective-permute-start
  561.4 2.9 convolution_add_fusion.4
  564.3 8.7 %collective-permute-done = bf16[2,512,256]{1,2,0:T(8,128)(2,1)S(1)} collective-permute-done((bf16[2,512,256]{1,2,0:T(8,128)(2,1)S(1)}, bf16[2,512,256]{1,2,0:T(8,128)(2,1)S(1)}, u32[]{:S(2)}, u32[]{:S(2)}) %collective-permute-start) | collective-permute-done | bytes 524320 | tf_op jit(solution)/shard_map/while/body/eval_jaxpr/ppermute | solution.py:12
  (219 shorter events, 63.7 us)
Async XLA Ops:
  0.0 25.0 %copy-start.2 = (bf16[16,8192]{1,0:T(8,128)(2,1)S(1)}, bf16[16,8192]{1,0:T(8,128)(2,1)}, u32[]{:S(2)}) copy-start(bf16[16,8192]{1,0:T(8,128)(2,1)} %param.13) | copy-start | bytes 786436
  1.7 15.3 %all-to-all-start.4 = ((bf16[16,32,256]{2,0,1:T(8,128)(2,1)}), bf16[16,32,256]{2,0,1:T(8,128)(2,1)S(1)}, u32[]{:S(2)}, u32[]{:S(2)}) async-start(bf16[16,32,256]{2,0,1:T(8,128)(2,1)} %bitcast.34), calls=%async_computation.4 | async-start | bytes 524288 | tf_op jit(solution)/shard_map/all_to_all | solution.py:77
  17.0 14.9 %all-to-all-start = ((bf16[16,32,256]{2,0,1:T(8,128)(2,1)}), bf16[16,32,256]{2,0,1:T(8,128)(2,1)S(1)}, u32[]{:S(2)}, u32[]{:S(2)}) async-start(bf16[16,32,256]{2,0,1:T(8,128)(2,1)} %bitcast.36), calls=%async_computation | async-start | bytes 524288 | tf_op jit(solution)/shard_map/all_to_all | solution.py:78
  31.9 15.0 %all-to-all-start.2 = ((bf16[16,32,256]{2,0,1:T(8,128)(2,1)}), bf16[16,32,256]{2,0,1:T(8,128)(2,1)S(1)}, u32[]{:S(2)}, u32[]{:S(2)}) async-start(bf16[16,32,256]{2,0,1:T(8,128)(2,1)} %bitcast.35), calls=%async_computation.2 | async-start | bytes 524288 | tf_op jit(solution)/shard_map/all_to_all | solution.py:79
  47.6 11.5 %copy-start.4 = (s32[512]{0:T(512)S(1)}, s32[512]{0:T(512)}, u32[]{:S(2)}) copy-start(s32[512]{0:T(512)} %param.15) | copy-start | bytes 6148
  49.0 35.9 %copy-start.5 = (s32[8]{0:T(128)S(1)}, s32[8]{0:T(128)}, u32[]{:S(2)}) copy-start(s32[8]{0:T(128)} %param.14) | copy-start | bytes 100
  49.0 27.2 %all-to-all-start.1 = ((bf16[16,64,256]{2,1,0:T(8,128)(2,1)}), bf16[16,64,256]{2,1,0:T(8,128)(2,1)S(1)}, u32[]{:S(2)}, u32[]{:S(2)}) async-start(bf16[16,64,256]{2,1,0:T(8,128)(2,1)} %bitcast.1), calls=%async_computation.1 | async-start | bytes 1048576 | tf_op jit(solution)/shard_map/all_to_all | solution.py:116
  76.2 24.2 %all-to-all-start.3 = ((bf16[16,64,256]{2,1,0:T(8,128)(2,1)}), bf16[16,64,256]{2,1,0:T(8,128)(2,1)S(1)}, u32[]{:S(2)}, u32[]{:S(2)}) async-start(bf16[16,64,256]{2,1,0:T(8,128)(2,1)} %bitcast.5), calls=%async_computation.3 | async-start | bytes 1048576 | tf_op jit(solution)/shard_map/all_to_all | solution.py:117
  100.4 24.3 %all-to-all-start.5 = ((bf16[16,64,256]{2,1,0:T(8,128)(2,1)}), bf16[16,64,256]{2,1,0:T(8,128)(2,1)S(1)}, u32[]{:S(2)}, u32[]{:S(2)}) async-start(bf16[16,64,256]{2,1,0:T(8,128)(2,1)} %bitcast.11), calls=%async_computation.5 | async-start | bytes 1048576 | tf_op jit(solution)/shard_map/all_to_all | solution.py:115
  125.4 1.6 copy-start
  127.3 20.2 %collective-permute-start = (bf16[2,512,256]{1,2,0:T(8,128)(2,1)S(1)}, bf16[2,512,256]{1,2,0:T(8,128)(2,1)S(1)}, u32[]{:S(2)}, u32[]{:S(2)}) collective-permute-start(bf16[2,512,256]{1,2,0:T(8,128)(2,1)S(1)} %copy.105), channel_id=1, source_target_pairs={{15,0},{0,1},{1,2},{2,3},{3,4},{4,5},{5,6},{6,7},{7,8},{8,9},{9,10... | collective-permute-start | bytes 1572872 | tf_op jit(solution)/shard_map/while/body/eval_jaxpr/ppermute | solution.py:12
  147.6 33.9 %collective-permute-start = (bf16[2,512,256]{1,2,0:T(8,128)(2,1)S(1)}, bf16[2,512,256]{1,2,0:T(8,128)(2,1)S(1)}, u32[]{:S(2)}, u32[]{:S(2)}) collective-permute-start(bf16[2,512,256]{1,2,0:T(8,128)(2,1)S(1)} %copy.105), channel_id=1, source_target_pairs={{15,0},{0,1},{1,2},{2,3},{3,4},{4,5},{5,6},{6,7},{7,8},{8,9},{9,10... | collective-permute-start | bytes 1572872 | tf_op jit(solution)/shard_map/while/body/eval_jaxpr/ppermute | solution.py:12
  181.5 29.7 %collective-permute-start = (bf16[2,512,256]{1,2,0:T(8,128)(2,1)S(1)}, bf16[2,512,256]{1,2,0:T(8,128)(2,1)S(1)}, u32[]{:S(2)}, u32[]{:S(2)}) collective-permute-start(bf16[2,512,256]{1,2,0:T(8,128)(2,1)S(1)} %copy.105), channel_id=1, source_target_pairs={{15,0},{0,1},{1,2},{2,3},{3,4},{4,5},{5,6},{6,7},{7,8},{8,9},{9,10... | collective-permute-start | bytes 1572872 | tf_op jit(solution)/shard_map/while/body/eval_jaxpr/ppermute | solution.py:12
  211.2 42.2 %collective-permute-start = (bf16[2,512,256]{1,2,0:T(8,128)(2,1)S(1)}, bf16[2,512,256]{1,2,0:T(8,128)(2,1)S(1)}, u32[]{:S(2)}, u32[]{:S(2)}) collective-permute-start(bf16[2,512,256]{1,2,0:T(8,128)(2,1)S(1)} %copy.105), channel_id=1, source_target_pairs={{15,0},{0,1},{1,2},{2,3},{3,4},{4,5},{5,6},{6,7},{7,8},{8,9},{9,10... | collective-permute-start | bytes 1572872 | tf_op jit(solution)/shard_map/while/body/eval_jaxpr/ppermute | solution.py:12
  253.5 33.1 %collective-permute-start = (bf16[2,512,256]{1,2,0:T(8,128)(2,1)S(1)}, bf16[2,512,256]{1,2,0:T(8,128)(2,1)S(1)}, u32[]{:S(2)}, u32[]{:S(2)}) collective-permute-start(bf16[2,512,256]{1,2,0:T(8,128)(2,1)S(1)} %copy.105), channel_id=1, source_target_pairs={{15,0},{0,1},{1,2},{2,3},{3,4},{4,5},{5,6},{6,7},{7,8},{8,9},{9,10... | collective-permute-start | bytes 1572872 | tf_op jit(solution)/shard_map/while/body/eval_jaxpr/ppermute | solution.py:12
  286.6 30.1 %collective-permute-start = (bf16[2,512,256]{1,2,0:T(8,128)(2,1)S(1)}, bf16[2,512,256]{1,2,0:T(8,128)(2,1)S(1)}, u32[]{:S(2)}, u32[]{:S(2)}) collective-permute-start(bf16[2,512,256]{1,2,0:T(8,128)(2,1)S(1)} %copy.105), channel_id=1, source_target_pairs={{15,0},{0,1},{1,2},{2,3},{3,4},{4,5},{5,6},{6,7},{7,8},{8,9},{9,10... | collective-permute-start | bytes 1572872 | tf_op jit(solution)/shard_map/while/body/eval_jaxpr/ppermute | solution.py:12
  316.8 31.2 %collective-permute-start = (bf16[2,512,256]{1,2,0:T(8,128)(2,1)S(1)}, bf16[2,512,256]{1,2,0:T(8,128)(2,1)S(1)}, u32[]{:S(2)}, u32[]{:S(2)}) collective-permute-start(bf16[2,512,256]{1,2,0:T(8,128)(2,1)S(1)} %copy.105), channel_id=1, source_target_pairs={{15,0},{0,1},{1,2},{2,3},{3,4},{4,5},{5,6},{6,7},{7,8},{8,9},{9,10... | collective-permute-start | bytes 1572872 | tf_op jit(solution)/shard_map/while/body/eval_jaxpr/ppermute | solution.py:12
  348.1 28.4 %collective-permute-start = (bf16[2,512,256]{1,2,0:T(8,128)(2,1)S(1)}, bf16[2,512,256]{1,2,0:T(8,128)(2,1)S(1)}, u32[]{:S(2)}, u32[]{:S(2)}) collective-permute-start(bf16[2,512,256]{1,2,0:T(8,128)(2,1)S(1)} %copy.105), channel_id=1, source_target_pairs={{15,0},{0,1},{1,2},{2,3},{3,4},{4,5},{5,6},{6,7},{7,8},{8,9},{9,10... | collective-permute-start | bytes 1572872 | tf_op jit(solution)/shard_map/while/body/eval_jaxpr/ppermute | solution.py:12
  376.5 28.6 %collective-permute-start = (bf16[2,512,256]{1,2,0:T(8,128)(2,1)S(1)}, bf16[2,512,256]{1,2,0:T(8,128)(2,1)S(1)}, u32[]{:S(2)}, u32[]{:S(2)}) collective-permute-start(bf16[2,512,256]{1,2,0:T(8,128)(2,1)S(1)} %copy.105), channel_id=1, source_target_pairs={{15,0},{0,1},{1,2},{2,3},{3,4},{4,5},{5,6},{6,7},{7,8},{8,9},{9,10... | collective-permute-start | bytes 1572872 | tf_op jit(solution)/shard_map/while/body/eval_jaxpr/ppermute | solution.py:12
  405.1 22.0 %collective-permute-start = (bf16[2,512,256]{1,2,0:T(8,128)(2,1)S(1)}, bf16[2,512,256]{1,2,0:T(8,128)(2,1)S(1)}, u32[]{:S(2)}, u32[]{:S(2)}) collective-permute-start(bf16[2,512,256]{1,2,0:T(8,128)(2,1)S(1)} %copy.105), channel_id=1, source_target_pairs={{15,0},{0,1},{1,2},{2,3},{3,4},{4,5},{5,6},{6,7},{7,8},{8,9},{9,10... | collective-permute-start | bytes 1572872 | tf_op jit(solution)/shard_map/while/body/eval_jaxpr/ppermute | solution.py:12
  427.1 24.9 %collective-permute-start = (bf16[2,512,256]{1,2,0:T(8,128)(2,1)S(1)}, bf16[2,512,256]{1,2,0:T(8,128)(2,1)S(1)}, u32[]{:S(2)}, u32[]{:S(2)}) collective-permute-start(bf16[2,512,256]{1,2,0:T(8,128)(2,1)S(1)} %copy.105), channel_id=1, source_target_pairs={{15,0},{0,1},{1,2},{2,3},{3,4},{4,5},{5,6},{6,7},{7,8},{8,9},{9,10... | collective-permute-start | bytes 1572872 | tf_op jit(solution)/shard_map/while/body/eval_jaxpr/ppermute | solution.py:12
  452.1 41.9 %collective-permute-start = (bf16[2,512,256]{1,2,0:T(8,128)(2,1)S(1)}, bf16[2,512,256]{1,2,0:T(8,128)(2,1)S(1)}, u32[]{:S(2)}, u32[]{:S(2)}) collective-permute-start(bf16[2,512,256]{1,2,0:T(8,128)(2,1)S(1)} %copy.105), channel_id=1, source_target_pairs={{15,0},{0,1},{1,2},{2,3},{3,4},{4,5},{5,6},{6,7},{7,8},{8,9},{9,10... | collective-permute-start | bytes 1572872 | tf_op jit(solution)/shard_map/while/body/eval_jaxpr/ppermute | solution.py:12
  494.0 33.0 %collective-permute-start = (bf16[2,512,256]{1,2,0:T(8,128)(2,1)S(1)}, bf16[2,512,256]{1,2,0:T(8,128)(2,1)S(1)}, u32[]{:S(2)}, u32[]{:S(2)}) collective-permute-start(bf16[2,512,256]{1,2,0:T(8,128)(2,1)S(1)} %copy.105), channel_id=1, source_target_pairs={{15,0},{0,1},{1,2},{2,3},{3,4},{4,5},{5,6},{6,7},{7,8},{8,9},{9,10... | collective-permute-start | bytes 1572872 | tf_op jit(solution)/shard_map/while/body/eval_jaxpr/ppermute | solution.py:12
  527.0 28.8 %collective-permute-start = (bf16[2,512,256]{1,2,0:T(8,128)(2,1)S(1)}, bf16[2,512,256]{1,2,0:T(8,128)(2,1)S(1)}, u32[]{:S(2)}, u32[]{:S(2)}) collective-permute-start(bf16[2,512,256]{1,2,0:T(8,128)(2,1)S(1)} %copy.105), channel_id=1, source_target_pairs={{15,0},{0,1},{1,2},{2,3},{3,4},{4,5},{5,6},{6,7},{7,8},{8,9},{9,10... | collective-permute-start | bytes 1572872 | tf_op jit(solution)/shard_map/while/body/eval_jaxpr/ppermute | solution.py:12
  555.9 17.1 %collective-permute-start = (bf16[2,512,256]{1,2,0:T(8,128)(2,1)S(1)}, bf16[2,512,256]{1,2,0:T(8,128)(2,1)S(1)}, u32[]{:S(2)}, u32[]{:S(2)}) collective-permute-start(bf16[2,512,256]{1,2,0:T(8,128)(2,1)S(1)} %copy.105), channel_id=1, source_target_pairs={{15,0},{0,1},{1,2},{2,3},{3,4},{4,5},{5,6},{6,7},{7,8},{8,9},{9,10... | collective-permute-start | bytes 1572872 | tf_op jit(solution)/shard_map/while/body/eval_jaxpr/ppermute | solution.py:12
  573.0 1.3 copy-start.1
  573.0 1.3 copy-start.3
where the time goes:
time: 579 us; the launch traced here: 577 us
  waiting for transfers between devices  347 us (60%)
  starting transfers between devices  112 us (19%)
  matrix products  69.6 us (12%)
  local copies, waits for them, and re-layouts  28.8 us (5%)
  other arithmetic  18.5 us (3%)
    ppermute x15, waiting for transfers between devices, from_behind(): return lax.ppermute(block, axis, route)  285 us
    ppermute x15, starting transfers between devices, from_behind(): return lax.ppermute(block, axis, route)  62.4 us
    dot_general x16, matrix products, attend(): jnp.einsum('hqk,khd->hqd', weights.astype(jnp.bfloat16), value_three, pre...  44.1 us
    dot_general x16, matrix products, attend(): jnp.einsum('qhd,khd->hqk', query_three, key_three, preferred_element_type...  25.6 us
    all_to_all x1, waiting for transfers between devices, per_device(): lax.all_to_all(pack_rows(spread[1]), 'ctx', split_axis=0, concat_axis=0,...  16.5 us
    all_to_all x1, waiting for transfers between devices, per_device(): lax.all_to_all(pack_rows(spread[2]), 'ctx', split_axis=0, concat_axis=0,...  15.2 us
    all_to_all x1, waiting for transfers between devices, per_device(): lax.all_to_all(pack_rows(spread[0]), 'ctx', split_axis=0, concat_axis=0,...  13.6 us
    slice x15, local copies, waits for them, and re-layouts, attend(): value_three = key_value[1].reshape(key_count, head_count, DH)  13 us
  transfers between devices with their start and end apart: 21, of which 21 were waited for; matrix products, arithmetic and copies ran while one was open for 18% of the time, Pallas kernels for 0%

commit v1 on v0

v1 whole, which is shorter than its diff:
```python
import jax
import jax.numpy as jnp
from jax import lax
from jax.experimental import pallas as pl
from jax.experimental.pallas import tpu as pltpu
from jax.sharding import Mesh, PartitionSpec as P

DH = 128
SLAB = 16
TOKENS = 8192
HEADS = 64
TQ = 128
BK = 512
ROWS = 1024
SLABS_HERE = ROWS // SLAB
FOLD = DH ** (-0.5) * 1.4426950408889634
AXES = ("x", "yl", "core", "zh", "zl", "yh")
HEAD_AXES = ("zh", "yl", "zl", "yh")


def split_kernel(q_ref, k_ref, v_ref, out_ref):
    for n in range(HEADS):
        cols = slice(n * DH, (n + 1) * DH)
        out_ref[n, 0:16, :] = q_ref[:, cols]
        out_ref[n, 16:32, :] = k_ref[:, cols]
        out_ref[n, 32:48, :] = v_ref[:, cols]


def split_heads(queries, keys, values):
    vmem = pl.BlockSpec(memory_space=pltpu.VMEM)
    return pl.pallas_call(
        split_kernel,
        out_shape=jax.ShapeDtypeStruct((HEADS, 48, DH), jnp.bfloat16),
        in_specs=[vmem, vmem, vmem],
        out_specs=vmem,
        name="split_heads",
    )(queries, keys, values)


def doc_start(positions, starts):
    first = jnp.zeros_like(positions)
    for start in starts:
        first = jnp.where(positions >= start, start, first)
    return first


def attend_kernel(slab_ref, dst_ref, start_ref, all_ref, out_ref, q_s, k_s, v_s, sem_q, sem_k, sem_v):
    def fetch_query(r, carry):
        j = slab_ref[r]
        h, c = j >> 4, j & 15
        shard = (h >> 3) * 2 + (h & 1)
        pltpu.make_async_copy(
            all_ref.at[shard, c >> 2, (h >> 1) & 3, c & 3, pl.ds(0, SLAB), :],
            q_s.at[pl.ds(pl.multiple_of(r * SLAB, SLAB), SLAB), :],
            sem_q,
        ).start()
        return carry

    lax.fori_loop(0, SLABS_HERE, fetch_query, 0)
    for x in range(4):
        for core in range(2):
            for yl in range(4):
                h = x * 8 + yl * 2 + core
                for buf, lo, sem in ((k_s, 16, sem_k), (v_s, 32, sem_v)):
                    pltpu.make_async_copy(
                        all_ref.at[x * 2 + core, :, yl, :, pl.ds(lo, SLAB), :],
                        buf.at[h],
                        sem,
                    ).start()
    pltpu.make_async_copy(q_s, q_s, sem_q).wait()
    pltpu.make_async_copy(k_s, k_s, sem_k).wait()
    pltpu.make_async_copy(v_s, v_s, sem_v).wait()
    starts = [start_ref[i] for i in range(8)]
    per_tile = TQ // SLAB
    blocks = BK // 256

    def tile(t, carry):
        q = q_s[pl.ds(pl.multiple_of(t * TQ, TQ), TQ), :]
        slabs = [slab_ref[t * per_tile + i] for i in range(per_tile)]
        row = lax.broadcasted_iota(jnp.int32, (SLAB, DH), 0)
        pos = jnp.concatenate([row + j * SLAB for j in slabs], axis=0)
        low = doc_start(pos, starts)
        first_pos = slabs[0] * SLAB
        last_pos = slabs[-1] * SLAB + SLAB - 1
        low_first = doc_start(first_pos, starts)
        low_last = doc_start(last_pos, starts)
        begin = low_first // BK
        end = last_pos // BK + 1
        full_begin = (low_last + BK - 1) // BK
        full_end = jnp.maximum((first_pos + 1) // BK, full_begin)
        full_begin = jnp.minimum(full_begin, end)
        full_end = jnp.minimum(full_end, end)

        def block(masked):
            def body(i, state):
                high, denom, acc = state
                k = k_s[pl.ds(i * blocks, blocks)].reshape(BK, DH)
                v = v_s[pl.ds(i * blocks, blocks)].reshape(BK, DH)
                s = lax.dot_general(
                    q, k, (((1,), (1,)), ((), ())), preferred_element_type=jnp.float32
                )
                if masked:
                    lane = lax.broadcasted_iota(jnp.int32, (TQ, DH), 1) + i * BK
                    parts = []
                    for m in range(BK // DH):
                        u = lane + m * DH
                        ok = (u >= low) & (u <= pos)
                        parts.append(jnp.where(ok, s[:, m * DH:(m + 1) * DH], -1e30))
                else:
                    parts = [s[:, m * DH:(m + 1) * DH] for m in range(BK // DH)]
                top = parts[0]
                for part in parts[1:]:
                    top = jnp.maximum(top, part)
                top = jnp.max(top, axis=1, keepdims=True) * FOLD
                new_high = jnp.maximum(high, jnp.broadcast_to(top, (TQ, DH)))
                scale = jnp.exp2(high - new_high)
                weights = [jnp.exp2(part * FOLD - new_high) for part in parts]
                denom = denom * scale
                for w in weights:
                    denom = denom + w
                p = jnp.concatenate([w.astype(jnp.bfloat16) for w in weights], axis=1)
                acc = acc * scale + jnp.dot(p, v, preferred_element_type=jnp.float32)
                return new_high, denom, acc

            return body

        state = (
            jnp.full((TQ, DH), -1e30, jnp.float32),
            jnp.zeros((TQ, DH), jnp.float32),
            jnp.zeros((TQ, DH), jnp.float32),
        )
        state = lax.fori_loop(begin, full_begin, block(True), state)
        state = lax.fori_loop(full_begin, full_end, block(False), state)
        state = lax.fori_loop(full_end, end, block(True), state)
        high, denom, acc = state
        result = (acc / jnp.sum(denom, axis=1, keepdims=True)).astype(jnp.bfloat16)
        for i in range(per_tile):
            to = pl.multiple_of(dst_ref[t * per_tile + i], SLAB)
            out_ref[pl.ds(to, SLAB), :] = result[i * SLAB:(i + 1) * SLAB]
        return carry

    lax.fori_loop(0, ROWS // TQ, tile, 0)


def attend(slabs, dst, starts, gathered):
    smem = pl.BlockSpec(memory_space=pltpu.SMEM)
    return pl.pallas_call(
        attend_kernel,
        out_shape=jax.ShapeDtypeStruct((ROWS, DH), jnp.bfloat16),
        in_specs=[smem, smem, smem, pl.BlockSpec(memory_space=pl.ANY)],
        out_specs=pl.BlockSpec(memory_space=pltpu.VMEM),
        scratch_shapes=[
            pltpu.VMEM((ROWS, DH), jnp.bfloat16),
            pltpu.VMEM((32, 4, 4, SLAB, DH), jnp.bfloat16),
            pltpu.VMEM((32, 4, 4, SLAB, DH), jnp.bfloat16),
            pltpu.SemaphoreType.DMA,
            pltpu.SemaphoreType.DMA,
            pltpu.SemaphoreType.DMA,
        ],
        compiler_params=pltpu.CompilerParams(vmem_limit_bytes=32 * 1024 * 1024),
        cost_estimate=pl.CostEstimate(flops=2 * 10**9, bytes_accessed=8 * 2**20, transcendentals=2 * 10**6),
        name="attend",
    )(slabs, dst, starts, gathered)


def tables(doc_lengths, slab_owner):
    part = lax.axis_index("x") * 2 + lax.axis_index("core")
    yh = lax.axis_index("yh")
    n = slab_owner.shape[0]
    index = jnp.arange(n, dtype=jnp.int32)
    mine = (slab_owner >> 1) == part
    before = jnp.sum((mine[None, :] & (index[None, :] < index[:, None])).astype(jnp.int32), axis=1)
    here = jnp.arange(SLABS_HERE, dtype=jnp.int32)
    hit = mine[None, :] & (before[None, :] == here[:, None])
    slabs = jnp.sum(jnp.where(hit, index[None, :], 0), axis=1)
    low_owner = jnp.sum(jnp.where(hit, slab_owner[None, :] & 1, 0), axis=1)
    rank = jnp.sum(
        ((low_owner[None, :] == low_owner[:, None]) & (here[None, :] < here[:, None])).astype(jnp.int32),
        axis=1,
    )
    dst = (low_owner ^ yh) * 512 + rank * SLAB
    earlier = jnp.arange(8)[None, :] < jnp.arange(8)[:, None]
    starts = jnp.sum(jnp.where(earlier, doc_lengths[None, :], 0), axis=1)
    return slabs, dst, starts


def to_owner(swap):
    route = []
    for x in range(4):
        for core in range(2):
            for z in range(8):
                for yh in range(2):
                    source = ((x * 2 + core) * 8 + z) * 2 + yh
                    target = (z * 8 + (x * 2 + core)) * 2 + (yh ^ swap)
                    route.append((source, target))
    return route


def per_device(queries, keys, values, doc_lengths, slab_owner):
    slabs, dst, starts = tables(doc_lengths, slab_owner)
    parted = split_heads(queries, keys, values)
    landed = lax.all_to_all(parted, HEAD_AXES, split_axis=0, concat_axis=0, tiled=True)
    gathered = lax.all_gather(landed, ("x", "core"), axis=0, tiled=False)
    gathered = gathered.reshape(8, 4, 4, 4, 48, DH)
    attended = attend(slabs, dst, starts, gathered)
    moved = ("x", "core", "zh", "zl", "yh")
    same = lax.ppermute(attended[:512], moved, to_owner(0))
    other = lax.ppermute(attended[512:], moved, to_owner(1))
    first = lax.axis_index("yh") == 0
    return jnp.concatenate(
        [jnp.where(first, same, other), jnp.where(first, other, same)], axis=1
    )


def solution(mesh):
    fine = Mesh(mesh.devices.reshape(4, 4, 2, 4, 2, 2), AXES)
    rows = P(AXES, None)
    return jax.shard_map(
        per_device,
        mesh=fine,
        in_specs=(rows, rows, rows, P(), P()),
        out_specs=P(("zh", "zl", "yh"), ("x", "yl", "core")),
        check_vma=False,
    )
```

time: 579 us -> 150 us (0.26)
  the two profiles are of different devices: /device:TPU:278 before, /device:TPU:20 now
where the time goes in v1:
time: 150 us; the launch traced here: 149 us
  waiting for transfers between devices  52.8 us (35%)
  blocking collectives  41 us (27%)
  Pallas kernels  20.5 us (14%)
  starting transfers between devices  15.3 us (10%)
  between operations  13.5 us (9%)
  other arithmetic  3.37 us (2%)
  local copies, waits for them, and re-layouts  2.8 us (2%)
    all_to_all x1, blocking collectives, per_device(): lax.all_to_all(parted, HEAD_AXES, split_axis=0, concat_axis=0, tiled=True)  41 us
    all_gather x1, waiting for transfers between devices, per_device(): gathered = lax.all_gather(landed, ('x', 'core'), axis=0, tiled=False)  36.4 us
    pallas_call x1, Pallas kernels, attend(): pl.pallas_call(attend_kernel, out_shape=jax.ShapeDtypeStruct((ROWS, DH),...  18.4 us
    ppermute x1, waiting for transfers between devices, per_device(): other = lax.ppermute(attended[512:], moved, to_owner(1))  16.4 us
    ppermute x1, starting transfers between devices, per_device(): same = lax.ppermute(attended[:512], moved, to_owner(0))  10 us
    ppermute x1, starting transfers between devices, per_device(): other = lax.ppermute(attended[512:], moved, to_owner(1))  5.22 us
  transfers between devices with their start and end apart: 3, of which 2 were waited for; matrix products, arithmetic and copies ran while one was open for 2% of the time, Pallas kernels for 0%

profile of v1, /device:TPU:20, one launch (start us, length us, event | category | flops | bytes accessed | tf_op | source)
XLA Modules:
  0.0 149.3 jit_solution(4017048795689079893)
XLA Ops:
  6.5 0.0 all-gather.3.cloned.1.call-start
  6.5 2.1 %split_heads.1 = bf16[64,48,128]{2,1,0:T(8,128)(2,1)} custom-call(bf16[16,8192]{1,0:T(8,128)(2,1)} %q_ref.1, bf16[16,8192]{1,0:T(8,128)(2,1)} %k_ref.1, bf16[16,8192]{1,0:T(8,128)(2,1)} %v_ref.1), custom_call_target="tpu_custom_call" | custom-call | tf_op jit(solution)/shard_map/split_heads/pallas_call | solution.py:31
  8.7 41.0 %all_to_all.5 = bf16[64,48,128]{2,1,0:T(8,128)(2,1)} all-to-all(bf16[64,48,128]{2,1,0:T(8,128)(2,1)} %split_heads.1), channel_id=1, replica_groups=mesh['x'=4,'yl'=4,'core'=2,'zh'=4,'zl'=2,'yh'=2] {'zh','yl','zl','yh'}, dimensions={0} | all-to-all | bytes 1572864 | tf_op jit(solution)/shard_map/all_to_all | solution.py:202
  49.7 0.0 all-gather.3.cloned.1.call-update
  49.7 0.8 select_reduce_fusion.2.start_ref
  50.5 0.7 shift-right-arithmetic_compare_fusion
  51.2 0.2 convert_reduce_fusion
  51.3 0.7 broadcast_and_fusion
  52.0 0.1 select_reduce_fusion
  52.2 0.2 convert_reduce_fusion.1
  52.4 36.4 %all-gather.3.cloned.1.call-done = bf16[512,48,128]{2,1,0:T(8,128)(2,1)} async-done(((bf16[64,48,128]{2,1,0:T(8,128)(2,1)}), bf16[512,48,128]{2,1,0:T(8,128)(2,1)}) %all-gather.3.cloned.1.call-update) | async-done | bytes 6291472 | tf_op jit(solution)/shard_map/all_gather | solution.py:203
  88.7 0.0 copy-start
  88.7 2.8 %copy-done = bf16[512,48,128]{2,1,0:T(8,128)(2,1)S(1)} copy-done((bf16[512,48,128]{2,1,0:T(8,128)(2,1)S(1)}, bf16[512,48,128]{2,1,0:T(8,128)(2,1)}, u32[]{:S(2)}) %copy-start) | copy-done | bytes 6291480
  91.5 18.4 %attend.1 = bf16[1024,128]{1,0:T(8,128)(2,1)S(1)} custom-call(s32[64]{0:T(128)S(1)} %get-tuple-element.6.slab_ref, s32[64]{0:T(128)S(1)} %multiply_add_fusion.dst_ref, s32[8]{0:T(128)S(1)} %select_reduce_fusion.2.start_ref, bf16[8,4,4,4,48,128]{5,4,3,2,1,0:T(8,128)(2,1)S(1)} %bitcast.1), custom_call_target="tpu_custom_call" | custom-call | flops 2000000000 | bytes 8388608 | tf_op jit(solution)/shard_map/attend/pallas_call | solution.py:147
  109.9 10.0 %collective-permute-start = (bf16[512,128]{1,0:T(8,128)(2,1)S(1)}, bf16[512,128]{1,0:T(8,128)(2,1)S(1)}, u32[]{:S(2)}, u32[]{:S(2)}) collective-permute-start(bf16[512,128]{1,0:T(8,128)(2,1)S(1)} %get-tuple-element.9), channel_id=1, source_target_pairs={{0,0},{1,1},{2,16},{3,17},{4,128},{5,129},{6,144},{7,145},{8,256},... | collective-permute-start | bytes 393224 | tf_op jit(solution)/shard_map/ppermute | solution.py:207
  120.0 5.2 %collective-permute-start.1 = (bf16[512,128]{1,0:T(8,128)(2,1)S(1)}, bf16[512,128]{1,0:T(8,128)(2,1)S(1)}, u32[]{:S(2)}, u32[]{:S(2)}) collective-permute-start(bf16[512,128]{1,0:T(8,128)(2,1)S(1)} %get-tuple-element.10), channel_id=1, source_target_pairs={{0,1},{1,0},{2,17},{3,16},{4,129},{5,128},{6,145},{7,144},{8,257},... | collective-permute-start | bytes 393224 | tf_op jit(solution)/shard_map/ppermute | solution.py:208
  125.2 0.0 collective-permute-done
  125.2 16.4 %collective-permute-done.1 = bf16[512,128]{1,0:T(8,128)(2,1)S(1)} collective-permute-done((bf16[512,128]{1,0:T(8,128)(2,1)S(1)}, bf16[512,128]{1,0:T(8,128)(2,1)S(1)}, u32[]{:S(2)}, u32[]{:S(2)}) %collective-permute-start.1) | collective-permute-done | bytes 131104 | tf_op jit(solution)/shard_map/ppermute | solution.py:208
  141.7 0.7 pad_maximum_fusion
  (3 shorter events, 0.0 us)
Async XLA Ops:
  6.5 82.2 %all-gather.3.cloned.1.call-start = ((), (), s32[]{:S(2)}) async-start(), calls=%async_computation.1 | async-start | bytes 7077888 | tf_op jit(solution)/shard_map/all_gather | solution.py:203
  88.7 2.8 %copy-start = (bf16[512,48,128]{2,1,0:T(8,128)(2,1)S(1)}, bf16[512,48,128]{2,1,0:T(8,128)(2,1)}, u32[]{:S(2)}) copy-start(bf16[512,48,128]{2,1,0:T(8,128)(2,1)} %all-gather.3.cloned.1.call-done) | copy-start | bytes 18874372
  109.9 15.3 %collective-permute-start = (bf16[512,128]{1,0:T(8,128)(2,1)S(1)}, bf16[512,128]{1,0:T(8,128)(2,1)S(1)}, u32[]{:S(2)}, u32[]{:S(2)}) collective-permute-start(bf16[512,128]{1,0:T(8,128)(2,1)S(1)} %get-tuple-element.9), channel_id=1, source_target_pairs={{0,0},{1,1},{2,16},{3,17},{4,128},{5,129},{6,144},{7,145},{8,256},... | collective-permute-start | bytes 393224 | tf_op jit(solution)/shard_map/ppermute | solution.py:207
  120.0 21.7 %collective-permute-start.1 = (bf16[512,128]{1,0:T(8,128)(2,1)S(1)}, bf16[512,128]{1,0:T(8,128)(2,1)S(1)}, u32[]{:S(2)}, u32[]{:S(2)}) collective-permute-start(bf16[512,128]{1,0:T(8,128)(2,1)S(1)} %get-tuple-element.10), channel_id=1, source_target_pairs={{0,1},{1,0},{2,17},{3,16},{4,129},{5,128},{6,145},{7,144},{8,257},... | collective-permute-start | bytes 393224 | tf_op jit(solution)/shard_map/ppermute | solution.py:208
Sparse Core Ops, SparseCore 0:
  49.8 38.8 all-gather.2

commit v2 on v1

--- a/solution.py
+++ b/solution.py
@@ -10,7 +10,7 @@
 TOKENS = 8192
 HEADS = 64
 TQ = 128
-BK = 512
+BK = 2048
 ROWS = 1024
 SLABS_HERE = ROWS // SLAB
 FOLD = DH ** (-0.5) * 1.4426950408889634
@@ -44,29 +44,15 @@
     return first
 
 
-def attend_kernel(slab_ref, dst_ref, start_ref, all_ref, out_ref, q_s, k_s, v_s, sem_q, sem_k, sem_v):
-    def fetch_query(r, carry):
-        j = slab_ref[r]
-        h, c = j >> 4, j & 15
-        shard = (h >> 3) * 2 + (h & 1)
-        pltpu.make_async_copy(
-            all_ref.at[shard, c >> 2, (h >> 1) & 3, c & 3, pl.ds(0, SLAB), :],
-            q_s.at[pl.ds(pl.multiple_of(r * SLAB, SLAB), SLAB), :],
-            sem_q,
-        ).start()
-        return carry
-
-    lax.fori_loop(0, SLABS_HERE, fetch_query, 0)
-    for x in range(4):
-        for core in range(2):
-            for yl in range(4):
-                h = x * 8 + yl * 2 + core
-                for buf, lo, sem in ((k_s, 16, sem_k), (v_s, 32, sem_v)):
-                    pltpu.make_async_copy(
-                        all_ref.at[x * 2 + core, :, yl, :, pl.ds(lo, SLAB), :],
-                        buf.at[h],
-                        sem,
-                    ).start()
+def attend_kernel(slab_ref, dst_ref, start_ref, home_ref, *refs):
+    shards, (out_ref, q_s, k_s, v_s, sem_q, sem_k, sem_v) = refs[:8], refs[8:]
+    for i, shard in enumerate(shards):
+        for yl in range(4):
+            h = home_ref[i] + yl * 2
+            for buf, lo, sem in ((q_s, 0, sem_q), (k_s, 16, sem_k), (v_s, 32, sem_v)):
+                pltpu.make_async_copy(
+                    shard.at[:, yl, :, pl.ds(lo, SLAB), :], buf.at[h], sem
+                ).start()
     pltpu.make_async_copy(q_s, q_s, sem_q).wait()
     pltpu.make_async_copy(k_s, k_s, sem_k).wait()
     pltpu.make_async_copy(v_s, v_s, sem_v).wait()
@@ -75,8 +61,8 @@
     blocks = BK // 256
 
     def tile(t, carry):
-        q = q_s[pl.ds(pl.multiple_of(t * TQ, TQ), TQ), :]
         slabs = [slab_ref[t * per_tile + i] for i in range(per_tile)]
+        q = jnp.concatenate([q_s[j >> 4, (j >> 2) & 3, j & 3] for j in slabs], axis=0)
         row = lax.broadcasted_iota(jnp.int32, (SLAB, DH), 0)
         pos = jnp.concatenate([row + j * SLAB for j in slabs], axis=0)
         low = doc_start(pos, starts)
@@ -84,23 +70,23 @@
         last_pos = slabs[-1] * SLAB + SLAB - 1
         low_first = doc_start(first_pos, starts)
         low_last = doc_start(last_pos, starts)
-        begin = low_first // BK
-        end = last_pos // BK + 1
-        full_begin = (low_last + BK - 1) // BK
-        full_end = jnp.maximum((first_pos + 1) // BK, full_begin)
-        full_begin = jnp.minimum(full_begin, end)
-        full_end = jnp.minimum(full_end, end)
+        begin = low_first >> 8
+        count = (last_pos + 1 - begin * 256 + BK - 1) // BK
+        begin = jnp.minimum(begin, 32 - count * blocks)
+        base = begin * 256
+        full_begin = jnp.minimum((jnp.maximum(low_last - base, 0) + BK - 1) // BK, count)
+        full_end = jnp.clip((first_pos + 1 - base) // BK, full_begin, count)
 
         def block(masked):
             def body(i, state):
                 high, denom, acc = state
-                k = k_s[pl.ds(i * blocks, blocks)].reshape(BK, DH)
-                v = v_s[pl.ds(i * blocks, blocks)].reshape(BK, DH)
+                k = k_s[pl.ds(begin + i * blocks, blocks)].reshape(BK, DH)
+                v = v_s[pl.ds(begin + i * blocks, blocks)].reshape(BK, DH)
                 s = lax.dot_general(
                     q, k, (((1,), (1,)), ((), ())), preferred_element_type=jnp.float32
                 )
                 if masked:
-                    lane = lax.broadcasted_iota(jnp.int32, (TQ, DH), 1) + i * BK
+                    lane = lax.broadcasted_iota(jnp.int32, (TQ, DH), 1) + (base + i * BK)
                     parts = []
                     for m in range(BK // DH):
                         u = lane + m * DH
@@ -129,9 +115,7 @@
             jnp.zeros((TQ, DH), jnp.float32),
             jnp.zeros((TQ, DH), jnp.float32),
         )
-        state = lax.fori_loop(begin, full_begin, block(True), state)
-        state = lax.fori_loop(full_begin, full_end, block(False), state)
-        state = lax.fori_loop(full_end, end, block(True), state)
+        state = lax.fori_loop(0, count, block(True), state)
         high, denom, acc = state
         result = (acc / jnp.sum(denom, axis=1, keepdims=True)).astype(jnp.bfloat16)
         for i in range(per_tile):
@@ -142,25 +126,22 @@
     lax.fori_loop(0, ROWS // TQ, tile, 0)
 
 
-def attend(slabs, dst, starts, gathered):
+def attend(slabs, dst, starts, homes, shards):
     smem = pl.BlockSpec(memory_space=pltpu.SMEM)
+    shards = [shard.reshape(4, 4, 4, 48, DH) for shard in shards]
+    whole = pltpu.VMEM((32, 4, 4, SLAB, DH), jnp.bfloat16)
     return pl.pallas_call(
         attend_kernel,
         out_shape=jax.ShapeDtypeStruct((ROWS, DH), jnp.bfloat16),
-        in_specs=[smem, smem, smem, pl.BlockSpec(memory_space=pl.ANY)],
+        in_specs=[smem] * 4 + [pl.BlockSpec(memory_space=pl.ANY)] * 8,
         out_specs=pl.BlockSpec(memory_space=pltpu.VMEM),
-        scratch_shapes=[
-            pltpu.VMEM((ROWS, DH), jnp.bfloat16),
-            pltpu.VMEM((32, 4, 4, SLAB, DH), jnp.bfloat16),
-            pltpu.VMEM((32, 4, 4, SLAB, DH), jnp.bfloat16),
-            pltpu.SemaphoreType.DMA,
-            pltpu.SemaphoreType.DMA,
-            pltpu.SemaphoreType.DMA,
-        ],
+        scratch_shapes=[whole, whole, whole] + [pltpu.SemaphoreType.DMA] * 3,
         compiler_params=pltpu.CompilerParams(vmem_limit_bytes=32 * 1024 * 1024),
-        cost_estimate=pl.CostEstimate(flops=2 * 10**9, bytes_accessed=8 * 2**20, transcendentals=2 * 10**6),
+        cost_estimate=pl.CostEstimate(
+            flops=2 * 10**9, bytes_accessed=8 * 2**20, transcendentals=2 * 10**6
+        ),
         name="attend",
-    )(slabs, dst, starts, gathered)
+    )(slabs, dst, starts, homes, *shards)
 
 
 def tables(doc_lengths, slab_owner):
@@ -196,13 +177,54 @@
     return route
 
 
+def row_route(turn):
+    route = []
+    for x in range(4):
+        for core in range(2):
+            to_x, to_core = turn(x, core)
+            route.append((x * 2 + core, (to_x % 4) * 2 + to_core))
+    return route
+
+
+def gather_row(mine):
+    row = ("x", "core")
+    ring = row_route(lambda x, core: (x + 1 - 2 * core, core))
+    crossed = row_route(lambda x, core: (x - 1 + 2 * core, 1 - core))
+    swap = row_route(lambda x, core: (x, 1 - core))
+    near = lax.ppermute(mine, row, ring)
+    near_other = lax.ppermute(mine, row, crossed)
+    other = lax.ppermute(mine, row, swap)
+    far = lax.ppermute(near, row, ring)
+    back = lax.ppermute(near, row, swap)
+    back_other = lax.ppermute(near_other, row, swap)
+    far_other = lax.ppermute(far, row, swap)
+    x, core = lax.axis_index("x"), lax.axis_index("core")
+    behind = x - 1 + 2 * core
+    ahead = x + 1 - 2 * core
+    homes = jnp.stack(
+        [
+            (at & 3) * 8 + c
+            for at, c in (
+                (x, core),
+                (x, 1 - core),
+                (behind, core),
+                (behind, 1 - core),
+                (x + 2, core),
+                (ahead, 1 - core),
+                (ahead, core),
+                (x + 2, 1 - core),
+            )
+        ]
+    )
+    return (mine, other, near, near_other, far, back, back_other, far_other), homes
+
+
 def per_device(queries, keys, values, doc_lengths, slab_owner):
     slabs, dst, starts = tables(doc_lengths, slab_owner)
     parted = split_heads(queries, keys, values)
     landed = lax.all_to_all(parted, HEAD_AXES, split_axis=0, concat_axis=0, tiled=True)
-    gathered = lax.all_gather(landed, ("x", "core"), axis=0, tiled=False)
-    gathered = gathered.reshape(8, 4, 4, 4, 48, DH)
-    attended = attend(slabs, dst, starts, gathered)
+    shards, homes = gather_row(landed)
+    attended = attend(slabs, dst, starts, homes, shards)
     moved = ("x", "core", "zh", "zl", "yh")
     same = lax.ppermute(attended[:512], moved, to_owner(0))
     other = lax.ppermute(attended[512:], moved, to_owner(1))

time: 150 us -> 123 us (0.82)
  the two profiles are of different devices: /device:TPU:20 before, /device:TPU:12 now
where the time goes in v2:
time: 123 us; the launch traced here: 122 us
  blocking collectives  42 us (34%)
  waiting for transfers between devices  34.4 us (28%)
  starting transfers between devices  29.6 us (24%)
  Pallas kernels  14 us (11%)
  other arithmetic  1.35 us (1%)
    all_to_all x1, blocking collectives, per_device(): lax.all_to_all(parted, HEAD_AXES, split_axis=0, concat_axis=0, tiled=True)  42 us
    ppermute x1, waiting for transfers between devices, gather_row(): near = lax.ppermute(mine, row, ring)  14.7 us
    ppermute x1, waiting for transfers between devices, per_device(): other = lax.ppermute(attended[512:], moved, to_owner(1))  14.2 us
    pallas_call x1, Pallas kernels, attend(): pl.pallas_call(attend_kernel, out_shape=jax.ShapeDtypeStruct((ROWS, DH),...  11.9 us
    ppermute x1, starting transfers between devices, per_device(): other = lax.ppermute(attended[512:], moved, to_owner(1))  8.02 us
    ppermute x1, starting transfers between devices, per_device(): same = lax.ppermute(attended[:512], moved, to_owner(0))  4.61 us
    ppermute x1, starting transfers between devices, gather_row(): far = lax.ppermute(near, row, ring)  3.81 us
    ppermute x1, starting transfers between devices, gather_row(): near = lax.ppermute(mine, row, ring)  3.09 us
  transfers between devices with their start and end apart: 9, of which 5 were waited for; matrix products, arithmetic and copies ran while one was open for 1% of the time, Pallas kernels for 0%

profile of v2, /device:TPU:12, one launch (start us, length us, event | category | flops | bytes accessed | tf_op | source)
XLA Modules:
  0.0 122.2 jit_solution(15395467940916566173)
XLA Ops:
  0.0 2.1 %split_heads.1 = bf16[64,48,128]{2,1,0:T(8,128)(2,1)} custom-call(bf16[16,8192]{1,0:T(8,128)(2,1)} %q_ref.1, bf16[16,8192]{1,0:T(8,128)(2,1)} %k_ref.1, bf16[16,8192]{1,0:T(8,128)(2,1)} %v_ref.1), custom_call_target="tpu_custom_call" | custom-call | tf_op jit(solution)/shard_map/split_heads/pallas_call | solution.py:31
  2.1 42.0 %all_to_all.5 = bf16[64,48,128]{2,1,0:T(8,128)(2,1)S(1)} all-to-all(bf16[64,48,128]{2,1,0:T(8,128)(2,1)} %split_heads.1), channel_id=1, replica_groups=mesh['x'=4,'yl'=4,'core'=2,'zh'=4,'zl'=2,'yh'=2] {'zh','yl','zl','yh'}, dimensions={0} | all-to-all | bytes 1572864 | tf_op jit(solution)/shard_map/all_to_all | solution.py:225
  44.1 3.1 %collective-permute-start.1 = (bf16[64,48,128]{2,1,0:T(8,128)(2,1)S(1)}, bf16[64,48,128]{2,1,0:T(8,128)(2,1)S(1)}, u32[]{:S(2)}, u32[]{:S(2)}) collective-permute-start(bf16[64,48,128]{2,1,0:T(8,128)(2,1)S(1)} %all_to_all.5), channel_id=1, source_target_pairs={{0,128},{16,400},{128,256},{144,16},{256,384},{272,144},{384,0},{4... | collective-permute-start | bytes 2359304 | tf_op jit(solution)/shard_map/ppermute | solution.py:194
  47.2 1.9 %collective-permute-start.2 = (bf16[64,48,128]{2,1,0:T(8,128)(2,1)S(1)}, bf16[64,48,128]{2,1,0:T(8,128)(2,1)S(1)}, u32[]{:S(2)}, u32[]{:S(2)}) collective-permute-start(bf16[64,48,128]{2,1,0:T(8,128)(2,1)S(1)} %all_to_all.5), channel_id=1, source_target_pairs={{0,400},{16,128},{128,16},{144,256},{256,144},{272,384},{384,272},... | collective-permute-start | bytes 2359304 | tf_op jit(solution)/shard_map/ppermute | solution.py:195
  49.1 14.7 %collective-permute-done.1 = bf16[64,48,128]{2,1,0:T(8,128)(2,1)S(1)} collective-permute-done((bf16[64,48,128]{2,1,0:T(8,128)(2,1)S(1)}, bf16[64,48,128]{2,1,0:T(8,128)(2,1)S(1)}, u32[]{:S(2)}, u32[]{:S(2)}) %collective-permute-start.1) | collective-permute-done | bytes 786464 | tf_op jit(solution)/shard_map/ppermute | solution.py:194
  63.8 3.8 %collective-permute-start.3 = (bf16[64,48,128]{2,1,0:T(8,128)(2,1)S(1)}, bf16[64,48,128]{2,1,0:T(8,128)(2,1)S(1)}, u32[]{:S(2)}, u32[]{:S(2)}) collective-permute-start(bf16[64,48,128]{2,1,0:T(8,128)(2,1)S(1)} %collective-permute-done.1), channel_id=1, source_target_pairs={{0,128},{16,400},{128,256},{144,16},{256,384},{272,144},{384,0},{4... | collective-permute-start | bytes 2359304 | tf_op jit(solution)/shard_map/ppermute | solution.py:197
  67.6 0.0 copy-start
  67.6 0.1 stack.35.home_ref
  67.7 0.6 copy-done
  68.3 0.0 copy-start.1
  68.3 0.1 convert_reduce_fusion
  68.5 1.9 %collective-permute-start = (bf16[64,48,128]{2,1,0:T(8,128)(2,1)S(1)}, bf16[64,48,128]{2,1,0:T(8,128)(2,1)S(1)}, u32[]{:S(2)}, u32[]{:S(2)}) collective-permute-start(bf16[64,48,128]{2,1,0:T(8,128)(2,1)S(1)} %all_to_all.5), channel_id=1, source_target_pairs={{0,16},{16,0},{128,144},{144,128},{256,272},{272,256},{384,400},{4... | collective-permute-start | bytes 2359304 | tf_op jit(solution)/shard_map/ppermute | solution.py:196
  70.4 2.4 %collective-permute-start.4 = (bf16[64,48,128]{2,1,0:T(8,128)(2,1)S(1)}, bf16[64,48,128]{2,1,0:T(8,128)(2,1)S(1)}, u32[]{:S(2)}, u32[]{:S(2)}) collective-permute-start(bf16[64,48,128]{2,1,0:T(8,128)(2,1)S(1)} %collective-permute-done.1), channel_id=1, source_target_pairs={{0,16},{16,0},{128,144},{144,128},{256,272},{272,256},{384,400},{4... | collective-permute-start | bytes 2359304 | tf_op jit(solution)/shard_map/ppermute | solution.py:198
  72.8 0.0 collective-permute-done.2
  72.8 1.9 %collective-permute-start.5 = (bf16[64,48,128]{2,1,0:T(8,128)(2,1)S(1)}, bf16[64,48,128]{2,1,0:T(8,128)(2,1)S(1)}, u32[]{:S(2)}, u32[]{:S(2)}) collective-permute-start(bf16[64,48,128]{2,1,0:T(8,128)(2,1)S(1)} %collective-permute-done.2), channel_id=1, source_target_pairs={{0,16},{16,0},{128,144},{144,128},{256,272},{272,256},{384,400},{4... | collective-permute-start | bytes 2359304 | tf_op jit(solution)/shard_map/ppermute | solution.py:199
  74.7 2.9 %collective-permute-done.3 = bf16[64,48,128]{2,1,0:T(8,128)(2,1)S(1)} collective-permute-done((bf16[64,48,128]{2,1,0:T(8,128)(2,1)S(1)}, bf16[64,48,128]{2,1,0:T(8,128)(2,1)S(1)}, u32[]{:S(2)}, u32[]{:S(2)}) %collective-permute-start.3) | collective-permute-done | bytes 786464 | tf_op jit(solution)/shard_map/ppermute | solution.py:197
  77.6 1.9 %collective-permute-start.6 = (bf16[64,48,128]{2,1,0:T(8,128)(2,1)S(1)}, bf16[64,48,128]{2,1,0:T(8,128)(2,1)S(1)}, u32[]{:S(2)}, u32[]{:S(2)}) collective-permute-start(bf16[64,48,128]{2,1,0:T(8,128)(2,1)S(1)} %collective-permute-done.3), channel_id=1, source_target_pairs={{0,16},{16,0},{128,144},{144,128},{256,272},{272,256},{384,400},{4... | collective-permute-start | bytes 2359304 | tf_op jit(solution)/shard_map/ppermute | solution.py:200
  79.6 0.0 copy-done.1
  79.6 0.1 select_reduce_fusion.2.start_ref
  79.7 0.1 select_reduce_fusion
  79.8 0.2 convert_reduce_fusion.1
  80.0 0.0 collective-permute-done
  80.0 0.0 collective-permute-done.5
  80.0 0.0 collective-permute-done.4
  80.0 1.8 %collective-permute-done.6 = bf16[64,48,128]{2,1,0:T(8,128)(2,1)S(1)} collective-permute-done((bf16[64,48,128]{2,1,0:T(8,128)(2,1)S(1)}, bf16[64,48,128]{2,1,0:T(8,128)(2,1)S(1)}, u32[]{:S(2)}, u32[]{:S(2)}) %collective-permute-start.6) | collective-permute-done | bytes 786464 | tf_op jit(solution)/shard_map/ppermute | solution.py:200
  81.8 11.9 %attend.1 = bf16[1024,128]{1,0:T(8,128)(2,1)S(1)} custom-call(s32[64]{0:T(128)S(1)} %get-tuple-element.6.slab_ref, s32[64]{0:T(128)S(1)} %multiply_add_fusion.dst_ref, s32[8]{0:T(128)S(1)} %select_reduce_fusion.2.start_ref, s32[8]{0:T(128)S(1)} %stack.35.home_ref, bf16[4,4,4,48,128]{4,3,2,1,0:T(8,128)(2,1)S(1)} %bitcast.16, ...), custom_call_target="tpu_custom_call" | custom-call | flops 2000000000 | bytes 8388608 | tf_op jit(solution)/shard_map/attend/pallas_call | solution.py:133
  93.8 4.6 %collective-permute-start.7 = (bf16[512,128]{1,0:T(8,128)(2,1)S(1)}, bf16[512,128]{1,0:T(8,128)(2,1)S(1)}, u32[]{:S(2)}, u32[]{:S(2)}) collective-permute-start(bf16[512,128]{1,0:T(8,128)(2,1)S(1)} %get-tuple-element.9), channel_id=1, source_target_pairs={{0,0},{1,1},{2,16},{3,17},{4,128},{5,129},{6,144},{7,145},{8,256},... | collective-permute-start | bytes 393224 | tf_op jit(solution)/shard_map/ppermute | solution.py:229
  98.4 8.0 %collective-permute-start.8 = (bf16[512,128]{1,0:T(8,128)(2,1)S(1)}, bf16[512,128]{1,0:T(8,128)(2,1)S(1)}, u32[]{:S(2)}, u32[]{:S(2)}) collective-permute-start(bf16[512,128]{1,0:T(8,128)(2,1)S(1)} %get-tuple-element.10), channel_id=1, source_target_pairs={{0,1},{1,0},{2,17},{3,16},{4,129},{5,128},{6,145},{7,144},{8,257},... | collective-permute-start | bytes 393224 | tf_op jit(solution)/shard_map/ppermute | solution.py:230
  106.4 0.8 collective-permute-done.7
  107.2 14.2 %collective-permute-done.8 = bf16[512,128]{1,0:T(8,128)(2,1)S(1)} collective-permute-done((bf16[512,128]{1,0:T(8,128)(2,1)S(1)}, bf16[512,128]{1,0:T(8,128)(2,1)S(1)}, u32[]{:S(2)}, u32[]{:S(2)}) %collective-permute-start.8) | collective-permute-done | bytes 131104 | tf_op jit(solution)/shard_map/ppermute | solution.py:230
  121.4 0.7 pad_maximum_fusion
  (5 shorter events, 0.1 us)
Async XLA Ops:
  44.1 19.7 %collective-permute-start.1 = (bf16[64,48,128]{2,1,0:T(8,128)(2,1)S(1)}, bf16[64,48,128]{2,1,0:T(8,128)(2,1)S(1)}, u32[]{:S(2)}, u32[]{:S(2)}) collective-permute-start(bf16[64,48,128]{2,1,0:T(8,128)(2,1)S(1)} %all_to_all.5), channel_id=1, source_target_pairs={{0,128},{16,400},{128,256},{144,16},{256,384},{272,144},{384,0},{4... | collective-permute-start | bytes 2359304 | tf_op jit(solution)/shard_map/ppermute | solution.py:194
  47.2 25.6 %collective-permute-start.2 = (bf16[64,48,128]{2,1,0:T(8,128)(2,1)S(1)}, bf16[64,48,128]{2,1,0:T(8,128)(2,1)S(1)}, u32[]{:S(2)}, u32[]{:S(2)}) collective-permute-start(bf16[64,48,128]{2,1,0:T(8,128)(2,1)S(1)} %all_to_all.5), channel_id=1, source_target_pairs={{0,400},{16,128},{128,16},{144,256},{256,144},{272,384},{384,272},... | collective-permute-start | bytes 2359304 | tf_op jit(solution)/shard_map/ppermute | solution.py:195
  63.8 13.9 %collective-permute-start.3 = (bf16[64,48,128]{2,1,0:T(8,128)(2,1)S(1)}, bf16[64,48,128]{2,1,0:T(8,128)(2,1)S(1)}, u32[]{:S(2)}, u32[]{:S(2)}) collective-permute-start(bf16[64,48,128]{2,1,0:T(8,128)(2,1)S(1)} %collective-permute-done.1), channel_id=1, source_target_pairs={{0,128},{16,400},{128,256},{144,16},{256,384},{272,144},{384,0},{4... | collective-permute-start | bytes 2359304 | tf_op jit(solution)/shard_map/ppermute | solution.py:197
  67.6 0.7 copy-start
  68.3 11.3 %copy-start.1 = (s32[8]{0:T(128)S(1)}, s32[8]{0:T(128)}, u32[]{:S(2)}) copy-start(s32[8]{0:T(128)} %param.8) | copy-start | bytes 100
  68.5 11.6 %collective-permute-start = (bf16[64,48,128]{2,1,0:T(8,128)(2,1)S(1)}, bf16[64,48,128]{2,1,0:T(8,128)(2,1)S(1)}, u32[]{:S(2)}, u32[]{:S(2)}) collective-permute-start(bf16[64,48,128]{2,1,0:T(8,128)(2,1)S(1)} %all_to_all.5), channel_id=1, source_target_pairs={{0,16},{16,0},{128,144},{144,128},{256,272},{272,256},{384,400},{4... | collective-permute-start | bytes 2359304 | tf_op jit(solution)/shard_map/ppermute | solution.py:196
  70.4 9.7 %collective-permute-start.4 = (bf16[64,48,128]{2,1,0:T(8,128)(2,1)S(1)}, bf16[64,48,128]{2,1,0:T(8,128)(2,1)S(1)}, u32[]{:S(2)}, u32[]{:S(2)}) collective-permute-start(bf16[64,48,128]{2,1,0:T(8,128)(2,1)S(1)} %collective-permute-done.1), channel_id=1, source_target_pairs={{0,16},{16,0},{128,144},{144,128},{256,272},{272,256},{384,400},{4... | collective-permute-start | bytes 2359304 | tf_op jit(solution)/shard_map/ppermute | solution.py:198
  72.8 7.2 %collective-permute-start.5 = (bf16[64,48,128]{2,1,0:T(8,128)(2,1)S(1)}, bf16[64,48,128]{2,1,0:T(8,128)(2,1)S(1)}, u32[]{:S(2)}, u32[]{:S(2)}) collective-permute-start(bf16[64,48,128]{2,1,0:T(8,128)(2,1)S(1)} %collective-permute-done.2), channel_id=1, source_target_pairs={{0,16},{16,0},{128,144},{144,128},{256,272},{272,256},{384,400},{4... | collective-permute-start | bytes 2359304 | tf_op jit(solution)/shard_map/ppermute | solution.py:199
  77.6 4.2 %collective-permute-start.6 = (bf16[64,48,128]{2,1,0:T(8,128)(2,1)S(1)}, bf16[64,48,128]{2,1,0:T(8,128)(2,1)S(1)}, u32[]{:S(2)}, u32[]{:S(2)}) collective-permute-start(bf16[64,48,128]{2,1,0:T(8,128)(2,1)S(1)} %collective-permute-done.3), channel_id=1, source_target_pairs={{0,16},{16,0},{128,144},{144,128},{256,272},{272,256},{384,400},{4... | collective-permute-start | bytes 2359304 | tf_op jit(solution)/shard_map/ppermute | solution.py:200
  93.8 13.4 %collective-permute-start.7 = (bf16[512,128]{1,0:T(8,128)(2,1)S(1)}, bf16[512,128]{1,0:T(8,128)(2,1)S(1)}, u32[]{:S(2)}, u32[]{:S(2)}) collective-permute-start(bf16[512,128]{1,0:T(8,128)(2,1)S(1)} %get-tuple-element.9), channel_id=1, source_target_pairs={{0,0},{1,1},{2,16},{3,17},{4,128},{5,129},{6,144},{7,145},{8,256},... | collective-permute-start | bytes 393224 | tf_op jit(solution)/shard_map/ppermute | solution.py:229
  98.4 23.0 %collective-permute-start.8 = (bf16[512,128]{1,0:T(8,128)(2,1)S(1)}, bf16[512,128]{1,0:T(8,128)(2,1)S(1)}, u32[]{:S(2)}, u32[]{:S(2)}) collective-permute-start(bf16[512,128]{1,0:T(8,128)(2,1)S(1)} %get-tuple-element.10), channel_id=1, source_target_pairs={{0,1},{1,0},{2,17},{3,16},{4,129},{5,128},{6,145},{7,144},{8,257},... | collective-permute-start | bytes 393224 | tf_op jit(solution)/shard_map/ppermute | solution.py:230

commit v3 on v2

--- a/solution.py
+++ b/solution.py
@@ -15,15 +15,20 @@
 SLABS_HERE = ROWS // SLAB
 FOLD = DH ** (-0.5) * 1.4426950408889634
 AXES = ("x", "yl", "core", "zh", "zl", "yh")
-HEAD_AXES = ("zh", "yl", "zl", "yh")
+HEAD_AXES = ("yl", "zh", "zl", "yh")
 
 
 def split_kernel(q_ref, k_ref, v_ref, out_ref):
-    for n in range(HEADS):
-        cols = slice(n * DH, (n + 1) * DH)
-        out_ref[n, 0:16, :] = q_ref[:, cols]
-        out_ref[n, 16:32, :] = k_ref[:, cols]
-        out_ref[n, 32:48, :] = v_ref[:, cols]
+    for yl in range(4):
+        for zh in range(2):
+            for zl in range(4):
+                for yh in range(2):
+                    to = yl * 16 + zh * 8 + zl * 2 + yh
+                    head = zl * 16 + yl * 4 + zh * 2 + yh
+                    cols = slice(head * DH, (head + 1) * DH)
+                    out_ref[to, 0:16, :] = q_ref[:, cols]
+                    out_ref[to, 16:32, :] = k_ref[:, cols]
+                    out_ref[to, 32:48, :] = v_ref[:, cols]
 
 
 def split_heads(queries, keys, values):
@@ -51,7 +56,7 @@
             h = home_ref[i] + yl * 2
             for buf, lo, sem in ((q_s, 0, sem_q), (k_s, 16, sem_k), (v_s, 32, sem_v)):
                 pltpu.make_async_copy(
-                    shard.at[:, yl, :, pl.ds(lo, SLAB), :], buf.at[h], sem
+                    shard.at[yl, :, pl.ds(lo, SLAB), :], buf.at[h], sem
                 ).start()
     pltpu.make_async_copy(q_s, q_s, sem_q).wait()
     pltpu.make_async_copy(k_s, k_s, sem_k).wait()
@@ -62,61 +67,51 @@
 
     def tile(t, carry):
         slabs = [slab_ref[t * per_tile + i] for i in range(per_tile)]
-        q = jnp.concatenate([q_s[j >> 4, (j >> 2) & 3, j & 3] for j in slabs], axis=0)
+        q = jnp.concatenate([q_s[j >> 4, j & 15] for j in slabs], axis=0)
         row = lax.broadcasted_iota(jnp.int32, (SLAB, DH), 0)
         pos = jnp.concatenate([row + j * SLAB for j in slabs], axis=0)
         low = doc_start(pos, starts)
-        first_pos = slabs[0] * SLAB
         last_pos = slabs[-1] * SLAB + SLAB - 1
-        low_first = doc_start(first_pos, starts)
-        low_last = doc_start(last_pos, starts)
+        since = lax.broadcasted_iota(jnp.int32, (TQ, DH), 1) - low
+        width = (pos - low).astype(jnp.uint32)
+        low_first = doc_start(slabs[0] * SLAB, starts)
         begin = low_first >> 8
         count = (last_pos + 1 - begin * 256 + BK - 1) // BK
         begin = jnp.minimum(begin, 32 - count * blocks)
         base = begin * 256
-        full_begin = jnp.minimum((jnp.maximum(low_last - base, 0) + BK - 1) // BK, count)
-        full_end = jnp.clip((first_pos + 1 - base) // BK, full_begin, count)
-
-        def block(masked):
-            def body(i, state):
-                high, denom, acc = state
-                k = k_s[pl.ds(begin + i * blocks, blocks)].reshape(BK, DH)
-                v = v_s[pl.ds(begin + i * blocks, blocks)].reshape(BK, DH)
-                s = lax.dot_general(
-                    q, k, (((1,), (1,)), ((), ())), preferred_element_type=jnp.float32
-                )
-                if masked:
-                    lane = lax.broadcasted_iota(jnp.int32, (TQ, DH), 1) + (base + i * BK)
-                    parts = []
-                    for m in range(BK // DH):
-                        u = lane + m * DH
-                        ok = (u >= low) & (u <= pos)
-                        parts.append(jnp.where(ok, s[:, m * DH:(m + 1) * DH], -1e30))
-                else:
-                    parts = [s[:, m * DH:(m + 1) * DH] for m in range(BK // DH)]
-                top = parts[0]
-                for part in parts[1:]:
-                    top = jnp.maximum(top, part)
-                top = jnp.max(top, axis=1, keepdims=True) * FOLD
-                new_high = jnp.maximum(high, jnp.broadcast_to(top, (TQ, DH)))
-                scale = jnp.exp2(high - new_high)
-                weights = [jnp.exp2(part * FOLD - new_high) for part in parts]
-                denom = denom * scale
-                for w in weights:
-                    denom = denom + w
-                p = jnp.concatenate([w.astype(jnp.bfloat16) for w in weights], axis=1)
-                acc = acc * scale + jnp.dot(p, v, preferred_element_type=jnp.float32)
-                return new_high, denom, acc
-
-            return body
+
+        def block(i, state):
+            high, denom, acc = state
+            k = k_s[pl.ds(begin + i * blocks, blocks)].reshape(BK, DH)
+            v = v_s[pl.ds(begin + i * blocks, blocks)].reshape(BK, DH)
+            s = lax.dot_general(
+                q, k, (((1,), (1,)), ((), ())), preferred_element_type=jnp.float32
+            )
+            gap = since + (base + i * BK)
+            parts = []
+            for m in range(BK // DH):
+                ok = (gap + m * DH).astype(jnp.uint32) <= width
+                parts.append(jnp.where(ok, s[:, m * DH:(m + 1) * DH], -1e30))
+            top = parts[0]
+            for part in parts[1:]:
+                top = jnp.maximum(top, part)
+            top = jnp.max(top, axis=1, keepdims=True) * FOLD
+            new_high = jnp.maximum(high, jnp.broadcast_to(top, (TQ, DH)))
+            scale = jnp.exp2(high - new_high)
+            weights = [jnp.exp2(part * FOLD - new_high) for part in parts]
+            denom = denom * scale
+            for w in weights:
+                denom = denom + w
+            p = jnp.concatenate([w.astype(jnp.bfloat16) for w in weights], axis=1)
+            acc = acc * scale + jnp.dot(p, v, preferred_element_type=jnp.float32)
+            return new_high, denom, acc
 
         state = (
             jnp.full((TQ, DH), -1e30, jnp.float32),
             jnp.zeros((TQ, DH), jnp.float32),
             jnp.zeros((TQ, DH), jnp.float32),
         )
-        state = lax.fori_loop(0, count, block(True), state)
-        high, denom, acc = state
+        high, denom, acc = lax.fori_loop(0, count, block, state)
         result = (acc / jnp.sum(denom, axis=1, keepdims=True)).astype(jnp.bfloat16)
         for i in range(per_tile):
             to = pl.multiple_of(dst_ref[t * per_tile + i], SLAB)
@@ -128,8 +123,8 @@
 
 def attend(slabs, dst, starts, homes, shards):
     smem = pl.BlockSpec(memory_space=pltpu.SMEM)
-    shards = [shard.reshape(4, 4, 4, 48, DH) for shard in shards]
-    whole = pltpu.VMEM((32, 4, 4, SLAB, DH), jnp.bfloat16)
+    shards = [shard.reshape(4, 16, 48, DH) for shard in shards]
+    whole = pltpu.VMEM((32, 16, SLAB, DH), jnp.bfloat16)
     return pl.pallas_call(
         attend_kernel,
         out_shape=jax.ShapeDtypeStruct((ROWS, DH), jnp.bfloat16),
@@ -145,7 +140,7 @@
 
 
 def tables(doc_lengths, slab_owner):
-    part = lax.axis_index("x") * 2 + lax.axis_index("core")
+    part = lax.axis_index("core") * 4 + lax.axis_index("x")
     yh = lax.axis_index("yh")
     n = slab_owner.shape[0]
     index = jnp.arange(n, dtype=jnp.int32)
@@ -169,11 +164,12 @@
     route = []
     for x in range(4):
         for core in range(2):
-            for z in range(8):
-                for yh in range(2):
-                    source = ((x * 2 + core) * 8 + z) * 2 + yh
-                    target = (z * 8 + (x * 2 + core)) * 2 + (yh ^ swap)
-                    route.append((source, target))
+            for zh in range(2):
+                for zl in range(4):
+                    for yh in range(2):
+                        source = (((x * 2 + core) * 2 + zh) * 4 + zl) * 2 + yh
+                        target = (((zl * 2 + zh) * 2 + core) * 4 + x) * 2 + (yh ^ swap)
+                        route.append((source, target))
     return route
 
 
@@ -235,7 +231,7 @@
 
 
 def solution(mesh):
-    fine = Mesh(mesh.devices.reshape(4, 4, 2, 4, 2, 2), AXES)
+    fine = Mesh(mesh.devices.reshape(4, 4, 2, 2, 4, 2), AXES)
     rows = P(AXES, None)
     return jax.shard_map(
         per_device,

time: 123 us -> 119 us (0.967)
  the two profiles are of different devices: /device:TPU:12 before, /device:TPU:1 now
where the time goes in v3:
time: 119 us
  starting transfers between devices  44.2 us (37%)
  blocking collectives  39.8 us (33%)
  waiting for transfers between devices  19.6 us (16%)
  Pallas kernels  12.9 us (11%)
  other arithmetic  1.35 us (1%)
    all_to_all x1, blocking collectives, per_device(): lax.all_to_all(parted, HEAD_AXES, split_axis=0, concat_axis=0, tiled=True)  39.8 us
    ppermute x1, waiting for transfers between devices, per_device(): other = lax.ppermute(attended[512:], moved, to_owner(1))  11.3 us
    pallas_call x1, Pallas kernels, attend(): pl.pallas_call(attend_kernel, out_shape=jax.ShapeDtypeStruct((ROWS, DH),...  10.8 us
    ppermute x1, starting transfers between devices, gather_row(): far_other = lax.ppermute(far, row, swap)  7.65 us
    ppermute x1, starting transfers between devices, per_device(): other = lax.ppermute(attended[512:], moved, to_owner(1))  7.22 us
    ppermute x1, waiting for transfers between devices, gather_row(): near = lax.ppermute(mine, row, ring)  6.88 us
    ppermute x1, starting transfers between devices, gather_row(): other = lax.ppermute(mine, row, swap)  6.39 us
    ppermute x1, starting transfers between devices, gather_row(): near_other = lax.ppermute(mine, row, crossed)  5.64 us
  transfers between devices with their start and end apart: 9, of which 3 were waited for; matrix products, arithmetic and copies ran while one was open for 1% of the time, Pallas kernels for 0%

profile of v3, /device:TPU:1, one launch (start us, length us, event | category | flops | bytes accessed | tf_op | source)
XLA Modules:
  0.0 118.7 jit_solution(10820675815856842685)
XLA Ops:
  0.0 2.1 %split_heads.1 = bf16[64,48,128]{2,1,0:T(8,128)(2,1)} custom-call(bf16[16,8192]{1,0:T(8,128)(2,1)} %q_ref.1, bf16[16,8192]{1,0:T(8,128)(2,1)} %k_ref.1, bf16[16,8192]{1,0:T(8,128)(2,1)} %v_ref.1), custom_call_target="tpu_custom_call" | custom-call | tf_op jit(solution)/shard_map/split_heads/pallas_call | solution.py:36
  2.1 39.8 %all_to_all.5 = bf16[64,48,128]{2,1,0:T(8,128)(2,1)S(1)} all-to-all(bf16[64,48,128]{2,1,0:T(8,128)(2,1)} %split_heads.1), channel_id=1, replica_groups=mesh['x'=4,'yl'=4,'core'=2,'zh'=2,'zl'=4,'yh'=2] {'yl','zh','zl','yh'}, dimensions={0} | all-to-all | bytes 1572864 | tf_op jit(solution)/shard_map/all_to_all | solution.py:221
  41.9 4.4 %collective-permute-start.1 = (bf16[64,48,128]{2,1,0:T(8,128)(2,1)S(1)}, bf16[64,48,128]{2,1,0:T(8,128)(2,1)S(1)}, u32[]{:S(2)}, u32[]{:S(2)}) collective-permute-start(bf16[64,48,128]{2,1,0:T(8,128)(2,1)S(1)} %all_to_all.5), channel_id=1, source_target_pairs={{0,128},{16,400},{128,256},{144,16},{256,384},{272,144},{384,0},{4... | collective-permute-start | bytes 2359304 | tf_op jit(solution)/shard_map/ppermute | solution.py:190
  46.3 5.6 %collective-permute-start.2 = (bf16[64,48,128]{2,1,0:T(8,128)(2,1)S(1)}, bf16[64,48,128]{2,1,0:T(8,128)(2,1)S(1)}, u32[]{:S(2)}, u32[]{:S(2)}) collective-permute-start(bf16[64,48,128]{2,1,0:T(8,128)(2,1)S(1)} %all_to_all.5), channel_id=1, source_target_pairs={{0,400},{16,128},{128,16},{144,256},{256,144},{272,384},{384,272},... | collective-permute-start | bytes 2359304 | tf_op jit(solution)/shard_map/ppermute | solution.py:191
  51.9 6.9 %collective-permute-done.1 = bf16[64,48,128]{2,1,0:T(8,128)(2,1)S(1)} collective-permute-done((bf16[64,48,128]{2,1,0:T(8,128)(2,1)S(1)}, bf16[64,48,128]{2,1,0:T(8,128)(2,1)S(1)}, u32[]{:S(2)}, u32[]{:S(2)}) %collective-permute-start.1) | collective-permute-done | bytes 786464 | tf_op jit(solution)/shard_map/ppermute | solution.py:190
  58.8 5.0 %collective-permute-start.3 = (bf16[64,48,128]{2,1,0:T(8,128)(2,1)S(1)}, bf16[64,48,128]{2,1,0:T(8,128)(2,1)S(1)}, u32[]{:S(2)}, u32[]{:S(2)}) collective-permute-start(bf16[64,48,128]{2,1,0:T(8,128)(2,1)S(1)} %collective-permute-done.1), channel_id=1, source_target_pairs={{0,128},{16,400},{128,256},{144,16},{256,384},{272,144},{384,0},{4... | collective-permute-start | bytes 2359304 | tf_op jit(solution)/shard_map/ppermute | solution.py:193
  63.9 0.0 copy-start
  63.9 0.1 stack.35.home_ref
  64.0 0.6 copy-done
  64.6 0.0 copy-start.1
  64.6 0.1 convert_reduce_fusion
  64.7 6.4 %collective-permute-start = (bf16[64,48,128]{2,1,0:T(8,128)(2,1)S(1)}, bf16[64,48,128]{2,1,0:T(8,128)(2,1)S(1)}, u32[]{:S(2)}, u32[]{:S(2)}) collective-permute-start(bf16[64,48,128]{2,1,0:T(8,128)(2,1)S(1)} %all_to_all.5), channel_id=1, source_target_pairs={{0,16},{16,0},{128,144},{144,128},{256,272},{272,256},{384,400},{4... | collective-permute-start | bytes 2359304 | tf_op jit(solution)/shard_map/ppermute | solution.py:192
  71.1 1.9 %collective-permute-start.4 = (bf16[64,48,128]{2,1,0:T(8,128)(2,1)S(1)}, bf16[64,48,128]{2,1,0:T(8,128)(2,1)S(1)}, u32[]{:S(2)}, u32[]{:S(2)}) collective-permute-start(bf16[64,48,128]{2,1,0:T(8,128)(2,1)S(1)} %collective-permute-done.1), channel_id=1, source_target_pairs={{0,16},{16,0},{128,144},{144,128},{256,272},{272,256},{384,400},{4... | collective-permute-start | bytes 2359304 | tf_op jit(solution)/shard_map/ppermute | solution.py:194
  73.0 0.0 collective-permute-done.2
  73.1 2.4 %collective-permute-start.5 = (bf16[64,48,128]{2,1,0:T(8,128)(2,1)S(1)}, bf16[64,48,128]{2,1,0:T(8,128)(2,1)S(1)}, u32[]{:S(2)}, u32[]{:S(2)}) collective-permute-start(bf16[64,48,128]{2,1,0:T(8,128)(2,1)S(1)} %collective-permute-done.2), channel_id=1, source_target_pairs={{0,16},{16,0},{128,144},{144,128},{256,272},{272,256},{384,400},{4... | collective-permute-start | bytes 2359304 | tf_op jit(solution)/shard_map/ppermute | solution.py:195
  75.5 0.0 collective-permute-done.3
  75.5 7.6 %collective-permute-start.6 = (bf16[64,48,128]{2,1,0:T(8,128)(2,1)S(1)}, bf16[64,48,128]{2,1,0:T(8,128)(2,1)S(1)}, u32[]{:S(2)}, u32[]{:S(2)}) collective-permute-start(bf16[64,48,128]{2,1,0:T(8,128)(2,1)S(1)} %collective-permute-done.3), channel_id=1, source_target_pairs={{0,16},{16,0},{128,144},{144,128},{256,272},{272,256},{384,400},{4... | collective-permute-start | bytes 2359304 | tf_op jit(solution)/shard_map/ppermute | solution.py:196
  83.1 0.0 copy-done.1
  83.1 0.1 select_reduce_fusion.2.start_ref
  83.3 0.1 select_reduce_fusion
  83.4 0.2 convert_reduce_fusion.1
  83.6 0.0 collective-permute-done
  83.6 0.0 collective-permute-done.5
  83.6 0.0 collective-permute-done.4
  83.6 1.4 %collective-permute-done.6 = bf16[64,48,128]{2,1,0:T(8,128)(2,1)S(1)} collective-permute-done((bf16[64,48,128]{2,1,0:T(8,128)(2,1)S(1)}, bf16[64,48,128]{2,1,0:T(8,128)(2,1)S(1)}, u32[]{:S(2)}, u32[]{:S(2)}) %collective-permute-start.6) | collective-permute-done | bytes 786464 | tf_op jit(solution)/shard_map/ppermute | solution.py:196
  85.0 10.8 %attend.1 = bf16[1024,128]{1,0:T(8,128)(2,1)S(1)} custom-call(s32[64]{0:T(128)S(1)} %get-tuple-element.6.slab_ref, s32[64]{0:T(128)S(1)} %multiply_add_fusion.dst_ref, s32[8]{0:T(128)S(1)} %select_reduce_fusion.2.start_ref, s32[8]{0:T(128)S(1)} %stack.35.home_ref, bf16[4,16,48,128]{3,2,1,0:T(8,128)(2,1)S(1)} %bitcast.16, ...), custom_call_target="tpu_custom_call" | custom-call | flops 2000000000 | bytes 8388608 | tf_op jit(solution)/shard_map/attend/pallas_call | solution.py:128
  95.8 3.5 %collective-permute-start.7 = (bf16[512,128]{1,0:T(8,128)(2,1)S(1)}, bf16[512,128]{1,0:T(8,128)(2,1)S(1)}, u32[]{:S(2)}, u32[]{:S(2)}) collective-permute-start(bf16[512,128]{1,0:T(8,128)(2,1)S(1)} %get-tuple-element.9), channel_id=1, source_target_pairs={{0,0},{1,1},{2,128},{3,129},{4,256},{5,257},{6,384},{7,385},{8,16}... | collective-permute-start | bytes 393224 | tf_op jit(solution)/shard_map/ppermute | solution.py:225
  99.4 7.2 %collective-permute-start.8 = (bf16[512,128]{1,0:T(8,128)(2,1)S(1)}, bf16[512,128]{1,0:T(8,128)(2,1)S(1)}, u32[]{:S(2)}, u32[]{:S(2)}) collective-permute-start(bf16[512,128]{1,0:T(8,128)(2,1)S(1)} %get-tuple-element.10), channel_id=1, source_target_pairs={{0,1},{1,0},{2,129},{3,128},{4,257},{5,256},{6,385},{7,384},{8,17}... | collective-permute-start | bytes 393224 | tf_op jit(solution)/shard_map/ppermute | solution.py:226
  106.6 0.0 collective-permute-done.7
  106.6 11.3 %collective-permute-done.8 = bf16[512,128]{1,0:T(8,128)(2,1)S(1)} collective-permute-done((bf16[512,128]{1,0:T(8,128)(2,1)S(1)}, bf16[512,128]{1,0:T(8,128)(2,1)S(1)}, u32[]{:S(2)}, u32[]{:S(2)}) %collective-permute-start.8) | collective-permute-done | bytes 131104 | tf_op jit(solution)/shard_map/ppermute | solution.py:226
  117.9 0.7 pad_maximum_fusion
  (5 shorter events, 0.1 us)
Async XLA Ops:
  41.9 16.9 %collective-permute-start.1 = (bf16[64,48,128]{2,1,0:T(8,128)(2,1)S(1)}, bf16[64,48,128]{2,1,0:T(8,128)(2,1)S(1)}, u32[]{:S(2)}, u32[]{:S(2)}) collective-permute-start(bf16[64,48,128]{2,1,0:T(8,128)(2,1)S(1)} %all_to_all.5), channel_id=1, source_target_pairs={{0,128},{16,400},{128,256},{144,16},{256,384},{272,144},{384,0},{4... | collective-permute-start | bytes 2359304 | tf_op jit(solution)/shard_map/ppermute | solution.py:190
  46.3 26.7 %collective-permute-start.2 = (bf16[64,48,128]{2,1,0:T(8,128)(2,1)S(1)}, bf16[64,48,128]{2,1,0:T(8,128)(2,1)S(1)}, u32[]{:S(2)}, u32[]{:S(2)}) collective-permute-start(bf16[64,48,128]{2,1,0:T(8,128)(2,1)S(1)} %all_to_all.5), channel_id=1, source_target_pairs={{0,400},{16,128},{128,16},{144,256},{256,144},{272,384},{384,272},... | collective-permute-start | bytes 2359304 | tf_op jit(solution)/shard_map/ppermute | solution.py:191
  58.8 16.6 %collective-permute-start.3 = (bf16[64,48,128]{2,1,0:T(8,128)(2,1)S(1)}, bf16[64,48,128]{2,1,0:T(8,128)(2,1)S(1)}, u32[]{:S(2)}, u32[]{:S(2)}) collective-permute-start(bf16[64,48,128]{2,1,0:T(8,128)(2,1)S(1)} %collective-permute-done.1), channel_id=1, source_target_pairs={{0,128},{16,400},{128,256},{144,16},{256,384},{272,144},{384,0},{4... | collective-permute-start | bytes 2359304 | tf_op jit(solution)/shard_map/ppermute | solution.py:193
  63.9 0.7 copy-start
  64.6 18.6 %copy-start.1 = (s32[8]{0:T(128)S(1)}, s32[8]{0:T(128)}, u32[]{:S(2)}) copy-start(s32[8]{0:T(128)} %param.8) | copy-start | bytes 100
  64.7 18.9 %collective-permute-start = (bf16[64,48,128]{2,1,0:T(8,128)(2,1)S(1)}, bf16[64,48,128]{2,1,0:T(8,128)(2,1)S(1)}, u32[]{:S(2)}, u32[]{:S(2)}) collective-permute-start(bf16[64,48,128]{2,1,0:T(8,128)(2,1)S(1)} %all_to_all.5), channel_id=1, source_target_pairs={{0,16},{16,0},{128,144},{144,128},{256,272},{272,256},{384,400},{4... | collective-permute-start | bytes 2359304 | tf_op jit(solution)/shard_map/ppermute | solution.py:192
  71.1 12.5 %collective-permute-start.4 = (bf16[64,48,128]{2,1,0:T(8,128)(2,1)S(1)}, bf16[64,48,128]{2,1,0:T(8,128)(2,1)S(1)}, u32[]{:S(2)}, u32[]{:S(2)}) collective-permute-start(bf16[64,48,128]{2,1,0:T(8,128)(2,1)S(1)} %collective-permute-done.1), channel_id=1, source_target_pairs={{0,16},{16,0},{128,144},{144,128},{256,272},{272,256},{384,400},{4... | collective-permute-start | bytes 2359304 | tf_op jit(solution)/shard_map/ppermute | solution.py:194
  73.1 10.6 %collective-permute-start.5 = (bf16[64,48,128]{2,1,0:T(8,128)(2,1)S(1)}, bf16[64,48,128]{2,1,0:T(8,128)(2,1)S(1)}, u32[]{:S(2)}, u32[]{:S(2)}) collective-permute-start(bf16[64,48,128]{2,1,0:T(8,128)(2,1)S(1)} %collective-permute-done.2), channel_id=1, source_target_pairs={{0,16},{16,0},{128,144},{144,128},{256,272},{272,256},{384,400},{4... | collective-permute-start | bytes 2359304 | tf_op jit(solution)/shard_map/ppermute | solution.py:195
  75.5 9.5 %collective-permute-start.6 = (bf16[64,48,128]{2,1,0:T(8,128)(2,1)S(1)}, bf16[64,48,128]{2,1,0:T(8,128)(2,1)S(1)}, u32[]{:S(2)}, u32[]{:S(2)}) collective-permute-start(bf16[64,48,128]{2,1,0:T(8,128)(2,1)S(1)} %collective-permute-done.3), channel_id=1, source_target_pairs={{0,16},{16,0},{128,144},{144,128},{256,272},{272,256},{384,400},{4... | collective-permute-start | bytes 2359304 | tf_op jit(solution)/shard_map/ppermute | solution.py:196
  95.8 10.8 %collective-permute-start.7 = (bf16[512,128]{1,0:T(8,128)(2,1)S(1)}, bf16[512,128]{1,0:T(8,128)(2,1)S(1)}, u32[]{:S(2)}, u32[]{:S(2)}) collective-permute-start(bf16[512,128]{1,0:T(8,128)(2,1)S(1)} %get-tuple-element.9), channel_id=1, source_target_pairs={{0,0},{1,1},{2,128},{3,129},{4,256},{5,257},{6,384},{7,385},{8,16}... | collective-permute-start | bytes 393224 | tf_op jit(solution)/shard_map/ppermute | solution.py:225
  99.4 18.5 %collective-permute-start.8 = (bf16[512,128]{1,0:T(8,128)(2,1)S(1)}, bf16[512,128]{1,0:T(8,128)(2,1)S(1)}, u32[]{:S(2)}, u32[]{:S(2)}) collective-permute-start(bf16[512,128]{1,0:T(8,128)(2,1)S(1)} %get-tuple-element.10), channel_id=1, source_target_pairs={{0,1},{1,0},{2,129},{3,128},{4,257},{5,256},{6,385},{7,384},{8,17}... | collective-permute-start | bytes 393224 | tf_op jit(solution)/shard_map/ppermute | solution.py:226

commit v4 on v3

--- a/solution.py
+++ b/solution.py
@@ -11,6 +11,8 @@
 HEADS = 64
 TQ = 128
 BK = 2048
+HALF = 1024
+TOGETHER = 2
 ROWS = 1024
 SLABS_HERE = ROWS // SLAB
 FOLD = DH ** (-0.5) * 1.4426950408889634
@@ -65,60 +67,81 @@
     per_tile = TQ // SLAB
     blocks = BK // 256
 
-    def tile(t, carry):
+    def setup(t):
         slabs = [slab_ref[t * per_tile + i] for i in range(per_tile)]
         q = jnp.concatenate([q_s[j >> 4, j & 15] for j in slabs], axis=0)
         row = lax.broadcasted_iota(jnp.int32, (SLAB, DH), 0)
         pos = jnp.concatenate([row + j * SLAB for j in slabs], axis=0)
         low = doc_start(pos, starts)
-        last_pos = slabs[-1] * SLAB + SLAB - 1
         since = lax.broadcasted_iota(jnp.int32, (TQ, DH), 1) - low
         width = (pos - low).astype(jnp.uint32)
-        low_first = doc_start(slabs[0] * SLAB, starts)
-        begin = low_first >> 8
-        count = (last_pos + 1 - begin * 256 + BK - 1) // BK
-        begin = jnp.minimum(begin, 32 - count * blocks)
-        base = begin * 256
-
-        def block(i, state):
-            high, denom, acc = state
-            k = k_s[pl.ds(begin + i * blocks, blocks)].reshape(BK, DH)
-            v = v_s[pl.ds(begin + i * blocks, blocks)].reshape(BK, DH)
-            s = lax.dot_general(
-                q, k, (((1,), (1,)), ((), ())), preferred_element_type=jnp.float32
-            )
-            gap = since + (base + i * BK)
-            parts = []
-            for m in range(BK // DH):
-                ok = (gap + m * DH).astype(jnp.uint32) <= width
-                parts.append(jnp.where(ok, s[:, m * DH:(m + 1) * DH], -1e30))
-            top = parts[0]
-            for part in parts[1:]:
-                top = jnp.maximum(top, part)
-            top = jnp.max(top, axis=1, keepdims=True) * FOLD
-            new_high = jnp.maximum(high, jnp.broadcast_to(top, (TQ, DH)))
-            scale = jnp.exp2(high - new_high)
-            weights = [jnp.exp2(part * FOLD - new_high) for part in parts]
-            denom = denom * scale
-            for w in weights:
-                denom = denom + w
-            p = jnp.concatenate([w.astype(jnp.bfloat16) for w in weights], axis=1)
-            acc = acc * scale + jnp.dot(p, v, preferred_element_type=jnp.float32)
-            return new_high, denom, acc
-
-        state = (
+        begin = doc_start(slabs[0] * SLAB, starts) >> 8
+        end = slabs[-1] * SLAB + SLAB
+        return q, since, width, begin, (end - begin * 256 + HALF - 1) // HALF
+
+    def some(group, carry):
+        tiles = [setup(group * TOGETHER + g) for g in range(TOGETHER)]
+        count = tiles[0][4]
+        for tile in tiles[1:]:
+            count = jnp.maximum(count, tile[4])
+        begins = [jnp.minimum(tile[3], 32 - count * (HALF // 256)) for tile in tiles]
+
+        def block(start, size, states):
+            some_blocks = size // 256
+            scores = []
+            for tile, begin in zip(tiles, begins):
+                k = k_s[pl.ds(begin + start, some_blocks)].reshape(size, DH)
+                scores.append(
+                    lax.dot_general(
+                        tile[0], k, (((1,), (1,)), ((), ())), preferred_element_type=jnp.float32
+                    )
+                )
+            held = []
+            for tile, begin, s, state in zip(tiles, begins, scores, states):
+                high, denom, acc = state
+                gap = tile[1] + (begin + start) * 256
+                parts = []
+                for m in range(size // DH):
+                    ok = (gap + m * DH).astype(jnp.uint32) <= tile[2]
+                    parts.append(jnp.where(ok, s[:, m * DH:(m + 1) * DH], -1e30))
+                top = parts[0]
+                for part in parts[1:]:
+                    top = jnp.maximum(top, part)
+                top = jnp.max(top, axis=1, keepdims=True) * FOLD
+                new_high = jnp.maximum(high, jnp.broadcast_to(top, (TQ, DH)))
+                scale = jnp.exp2(high - new_high)
+                weights = [jnp.exp2(part * FOLD - new_high) for part in parts]
+                denom = denom * scale
+                for w in weights:
+                    denom = denom + w
+                p = jnp.concatenate([w.astype(jnp.bfloat16) for w in weights], axis=1)
+                held.append((p, begin, scale, acc, new_high, denom))
+            after = []
+            for p, begin, scale, acc, new_high, denom in held:
+                v = v_s[pl.ds(begin + start, some_blocks)].reshape(size, DH)
+                acc = acc * scale + jnp.dot(p, v, preferred_element_type=jnp.float32)
+                after.append((new_high, denom, acc))
+            return after
+
+        empty = (
             jnp.full((TQ, DH), -1e30, jnp.float32),
             jnp.zeros((TQ, DH), jnp.float32),
             jnp.zeros((TQ, DH), jnp.float32),
         )
-        high, denom, acc = lax.fori_loop(0, count, block, state)
-        result = (acc / jnp.sum(denom, axis=1, keepdims=True)).astype(jnp.bfloat16)
-        for i in range(per_tile):
-            to = pl.multiple_of(dst_ref[t * per_tile + i], SLAB)
-            out_ref[pl.ds(to, SLAB), :] = result[i * SLAB:(i + 1) * SLAB]
+        states = lax.fori_loop(
+            0, count >> 1, lambda i, states: block(i * blocks, BK, states), [empty] * TOGETHER
+        )
+        states = lax.fori_loop(
+            0, count & 1, lambda i, states: block((count >> 1) * blocks, HALF, states), states
+        )
+        for g, (high, denom, acc) in enumerate(states):
+            result = (acc / jnp.sum(denom, axis=1, keepdims=True)).astype(jnp.bfloat16)
+            for i in range(per_tile):
+                to = dst_ref[(group * TOGETHER + g) * per_tile + i]
+                out_ref[pl.ds(pl.multiple_of(to, SLAB), SLAB), :] = result[i * SLAB:(i + 1) * SLAB]
         return carry
 
-    lax.fori_loop(0, ROWS // TQ, tile, 0)
+    lax.fori_loop(0, ROWS // TQ // TOGETHER, some, 0)
 
 
 def attend(slabs, dst, starts, homes, shards):

time: 119 us -> 117 us (0.983)
  Pallas kernels: 12.9 us -> 11 us
    pallas_call x1, Pallas kernels: 10.8 us -> 8.84 us  [attend(): pl.pallas_call(attend_kernel, out_shape=jax.ShapeDtypeStruct((ROWS, DH),...]
where the time goes in v4:
time: 117 us
  starting transfers between devices  44.2 us (38%)
  blocking collectives  39.8 us (34%)
  waiting for transfers between devices  19.6 us (17%)
  Pallas kernels  11 us (9%)
  other arithmetic  1.35 us (1%)
    all_to_all x1, blocking collectives, per_device(): lax.all_to_all(parted, HEAD_AXES, split_axis=0, concat_axis=0, tiled=True)  39.8 us
    ppermute x1, waiting for transfers between devices, per_device(): other = lax.ppermute(attended[512:], moved, to_owner(1))  11.3 us
    pallas_call x1, Pallas kernels, attend(): pl.pallas_call(attend_kernel, out_shape=jax.ShapeDtypeStruct((ROWS, DH),...  8.84 us
    ppermute x1, starting transfers between devices, gather_row(): far_other = lax.ppermute(far, row, swap)  7.65 us
    ppermute x1, starting transfers between devices, per_device(): other = lax.ppermute(attended[512:], moved, to_owner(1))  7.22 us
    ppermute x1, waiting for transfers between devices, gather_row(): near = lax.ppermute(mine, row, ring)  6.88 us
    ppermute x1, starting transfers between devices, gather_row(): other = lax.ppermute(mine, row, swap)  6.39 us
    ppermute x1, starting transfers between devices, gather_row(): near_other = lax.ppermute(mine, row, crossed)  5.64 us
  transfers between devices with their start and end apart: 9, of which 3 were waited for; matrix products, arithmetic and copies ran while one was open for 1% of the time, Pallas kernels for 0%

profile of v4, /device:TPU:1, one launch (start us, length us, event | category | flops | bytes accessed | tf_op | source)
XLA Modules:
  0.0 116.7 jit_solution(15902824324829915455)
XLA Ops:
  0.0 2.1 %split_heads.1 = bf16[64,48,128]{2,1,0:T(8,128)(2,1)} custom-call(bf16[16,8192]{1,0:T(8,128)(2,1)} %q_ref.1, bf16[16,8192]{1,0:T(8,128)(2,1)} %k_ref.1, bf16[16,8192]{1,0:T(8,128)(2,1)} %v_ref.1), custom_call_target="tpu_custom_call" | custom-call | tf_op jit(solution)/shard_map/split_heads/pallas_call | solution.py:38
  2.1 39.8 %all_to_all.5 = bf16[64,48,128]{2,1,0:T(8,128)(2,1)S(1)} all-to-all(bf16[64,48,128]{2,1,0:T(8,128)(2,1)} %split_heads.1), channel_id=1, replica_groups=mesh['x'=4,'yl'=4,'core'=2,'zh'=2,'zl'=4,'yh'=2] {'yl','zh','zl','yh'}, dimensions={0} | all-to-all | bytes 1572864 | tf_op jit(solution)/shard_map/all_to_all | solution.py:244
  41.9 4.4 %collective-permute-start.1 = (bf16[64,48,128]{2,1,0:T(8,128)(2,1)S(1)}, bf16[64,48,128]{2,1,0:T(8,128)(2,1)S(1)}, u32[]{:S(2)}, u32[]{:S(2)}) collective-permute-start(bf16[64,48,128]{2,1,0:T(8,128)(2,1)S(1)} %all_to_all.5), channel_id=1, source_target_pairs={{0,128},{16,400},{128,256},{144,16},{256,384},{272,144},{384,0},{4... | collective-permute-start | bytes 2359304 | tf_op jit(solution)/shard_map/ppermute | solution.py:213
  46.3 5.6 %collective-permute-start.2 = (bf16[64,48,128]{2,1,0:T(8,128)(2,1)S(1)}, bf16[64,48,128]{2,1,0:T(8,128)(2,1)S(1)}, u32[]{:S(2)}, u32[]{:S(2)}) collective-permute-start(bf16[64,48,128]{2,1,0:T(8,128)(2,1)S(1)} %all_to_all.5), channel_id=1, source_target_pairs={{0,400},{16,128},{128,16},{144,256},{256,144},{272,384},{384,272},... | collective-permute-start | bytes 2359304 | tf_op jit(solution)/shard_map/ppermute | solution.py:214
  51.9 6.9 %collective-permute-done.1 = bf16[64,48,128]{2,1,0:T(8,128)(2,1)S(1)} collective-permute-done((bf16[64,48,128]{2,1,0:T(8,128)(2,1)S(1)}, bf16[64,48,128]{2,1,0:T(8,128)(2,1)S(1)}, u32[]{:S(2)}, u32[]{:S(2)}) %collective-permute-start.1) | collective-permute-done | bytes 786464 | tf_op jit(solution)/shard_map/ppermute | solution.py:213
  58.8 5.0 %collective-permute-start.3 = (bf16[64,48,128]{2,1,0:T(8,128)(2,1)S(1)}, bf16[64,48,128]{2,1,0:T(8,128)(2,1)S(1)}, u32[]{:S(2)}, u32[]{:S(2)}) collective-permute-start(bf16[64,48,128]{2,1,0:T(8,128)(2,1)S(1)} %collective-permute-done.1), channel_id=1, source_target_pairs={{0,128},{16,400},{128,256},{144,16},{256,384},{272,144},{384,0},{4... | collective-permute-start | bytes 2359304 | tf_op jit(solution)/shard_map/ppermute | solution.py:216
  63.9 0.0 copy-start
  63.9 0.1 stack.35.home_ref
  64.0 0.6 copy-done
  64.6 0.0 copy-start.1
  64.6 0.1 convert_reduce_fusion
  64.7 6.4 %collective-permute-start = (bf16[64,48,128]{2,1,0:T(8,128)(2,1)S(1)}, bf16[64,48,128]{2,1,0:T(8,128)(2,1)S(1)}, u32[]{:S(2)}, u32[]{:S(2)}) collective-permute-start(bf16[64,48,128]{2,1,0:T(8,128)(2,1)S(1)} %all_to_all.5), channel_id=1, source_target_pairs={{0,16},{16,0},{128,144},{144,128},{256,272},{272,256},{384,400},{4... | collective-permute-start | bytes 2359304 | tf_op jit(solution)/shard_map/ppermute | solution.py:215
  71.1 1.9 %collective-permute-start.4 = (bf16[64,48,128]{2,1,0:T(8,128)(2,1)S(1)}, bf16[64,48,128]{2,1,0:T(8,128)(2,1)S(1)}, u32[]{:S(2)}, u32[]{:S(2)}) collective-permute-start(bf16[64,48,128]{2,1,0:T(8,128)(2,1)S(1)} %collective-permute-done.1), channel_id=1, source_target_pairs={{0,16},{16,0},{128,144},{144,128},{256,272},{272,256},{384,400},{4... | collective-permute-start | bytes 2359304 | tf_op jit(solution)/shard_map/ppermute | solution.py:217
  73.0 0.0 collective-permute-done.2
  73.1 2.4 %collective-permute-start.5 = (bf16[64,48,128]{2,1,0:T(8,128)(2,1)S(1)}, bf16[64,48,128]{2,1,0:T(8,128)(2,1)S(1)}, u32[]{:S(2)}, u32[]{:S(2)}) collective-permute-start(bf16[64,48,128]{2,1,0:T(8,128)(2,1)S(1)} %collective-permute-done.2), channel_id=1, source_target_pairs={{0,16},{16,0},{128,144},{144,128},{256,272},{272,256},{384,400},{4... | collective-permute-start | bytes 2359304 | tf_op jit(solution)/shard_map/ppermute | solution.py:218
  75.5 0.0 collective-permute-done.3
  75.5 7.6 %collective-permute-start.6 = (bf16[64,48,128]{2,1,0:T(8,128)(2,1)S(1)}, bf16[64,48,128]{2,1,0:T(8,128)(2,1)S(1)}, u32[]{:S(2)}, u32[]{:S(2)}) collective-permute-start(bf16[64,48,128]{2,1,0:T(8,128)(2,1)S(1)} %collective-permute-done.3), channel_id=1, source_target_pairs={{0,16},{16,0},{128,144},{144,128},{256,272},{272,256},{384,400},{4... | collective-permute-start | bytes 2359304 | tf_op jit(solution)/shard_map/ppermute | solution.py:219
  83.1 0.0 copy-done.1
  83.1 0.1 select_reduce_fusion.2.start_ref
  83.3 0.1 select_reduce_fusion
  83.4 0.2 convert_reduce_fusion.1
  83.6 0.0 collective-permute-done
  83.6 0.0 collective-permute-done.5
  83.6 0.0 collective-permute-done.4
  83.6 1.4 %collective-permute-done.6 = bf16[64,48,128]{2,1,0:T(8,128)(2,1)S(1)} collective-permute-done((bf16[64,48,128]{2,1,0:T(8,128)(2,1)S(1)}, bf16[64,48,128]{2,1,0:T(8,128)(2,1)S(1)}, u32[]{:S(2)}, u32[]{:S(2)}) %collective-permute-start.6) | collective-permute-done | bytes 786464 | tf_op jit(solution)/shard_map/ppermute | solution.py:219
  85.0 8.8 %attend.1 = bf16[1024,128]{1,0:T(8,128)(2,1)S(1)} custom-call(s32[64]{0:T(128)S(1)} %get-tuple-element.6.slab_ref, s32[64]{0:T(128)S(1)} %multiply_add_fusion.dst_ref, s32[8]{0:T(128)S(1)} %select_reduce_fusion.2.start_ref, s32[8]{0:T(128)S(1)} %stack.35.home_ref, bf16[4,16,48,128]{3,2,1,0:T(8,128)(2,1)S(1)} %bitcast.16, ...), custom_call_target="tpu_custom_call" | custom-call | flops 2000000000 | bytes 8388608 | tf_op jit(solution)/shard_map/attend/pallas_call | solution.py:151
  93.9 3.6 %collective-permute-start.7 = (bf16[512,128]{1,0:T(8,128)(2,1)S(1)}, bf16[512,128]{1,0:T(8,128)(2,1)S(1)}, u32[]{:S(2)}, u32[]{:S(2)}) collective-permute-start(bf16[512,128]{1,0:T(8,128)(2,1)S(1)} %get-tuple-element.9), channel_id=1, source_target_pairs={{0,0},{1,1},{2,128},{3,129},{4,256},{5,257},{6,384},{7,385},{8,16}... | collective-permute-start | bytes 393224 | tf_op jit(solution)/shard_map/ppermute | solution.py:248
  97.5 7.2 %collective-permute-start.8 = (bf16[512,128]{1,0:T(8,128)(2,1)S(1)}, bf16[512,128]{1,0:T(8,128)(2,1)S(1)}, u32[]{:S(2)}, u32[]{:S(2)}) collective-permute-start(bf16[512,128]{1,0:T(8,128)(2,1)S(1)} %get-tuple-element.10), channel_id=1, source_target_pairs={{0,1},{1,0},{2,129},{3,128},{4,257},{5,256},{6,385},{7,384},{8,17}... | collective-permute-start | bytes 393224 | tf_op jit(solution)/shard_map/ppermute | solution.py:249
  104.7 0.0 collective-permute-done.7
  104.7 11.3 %collective-permute-done.8 = bf16[512,128]{1,0:T(8,128)(2,1)S(1)} collective-permute-done((bf16[512,128]{1,0:T(8,128)(2,1)S(1)}, bf16[512,128]{1,0:T(8,128)(2,1)S(1)}, u32[]{:S(2)}, u32[]{:S(2)}) %collective-permute-start.8) | collective-permute-done | bytes 131104 | tf_op jit(solution)/shard_map/ppermute | solution.py:249
  116.0 0.7 pad_maximum_fusion
  (5 shorter events, 0.1 us)
Async XLA Ops:
  41.9 16.9 %collective-permute-start.1 = (bf16[64,48,128]{2,1,0:T(8,128)(2,1)S(1)}, bf16[64,48,128]{2,1,0:T(8,128)(2,1)S(1)}, u32[]{:S(2)}, u32[]{:S(2)}) collective-permute-start(bf16[64,48,128]{2,1,0:T(8,128)(2,1)S(1)} %all_to_all.5), channel_id=1, source_target_pairs={{0,128},{16,400},{128,256},{144,16},{256,384},{272,144},{384,0},{4... | collective-permute-start | bytes 2359304 | tf_op jit(solution)/shard_map/ppermute | solution.py:213
  46.3 26.7 %collective-permute-start.2 = (bf16[64,48,128]{2,1,0:T(8,128)(2,1)S(1)}, bf16[64,48,128]{2,1,0:T(8,128)(2,1)S(1)}, u32[]{:S(2)}, u32[]{:S(2)}) collective-permute-start(bf16[64,48,128]{2,1,0:T(8,128)(2,1)S(1)} %all_to_all.5), channel_id=1, source_target_pairs={{0,400},{16,128},{128,16},{144,256},{256,144},{272,384},{384,272},... | collective-permute-start | bytes 2359304 | tf_op jit(solution)/shard_map/ppermute | solution.py:214
  58.8 16.6 %collective-permute-start.3 = (bf16[64,48,128]{2,1,0:T(8,128)(2,1)S(1)}, bf16[64,48,128]{2,1,0:T(8,128)(2,1)S(1)}, u32[]{:S(2)}, u32[]{:S(2)}) collective-permute-start(bf16[64,48,128]{2,1,0:T(8,128)(2,1)S(1)} %collective-permute-done.1), channel_id=1, source_target_pairs={{0,128},{16,400},{128,256},{144,16},{256,384},{272,144},{384,0},{4... | collective-permute-start | bytes 2359304 | tf_op jit(solution)/shard_map/ppermute | solution.py:216
  63.9 0.7 copy-start
  64.6 18.6 %copy-start.1 = (s32[8]{0:T(128)S(1)}, s32[8]{0:T(128)}, u32[]{:S(2)}) copy-start(s32[8]{0:T(128)} %param.8) | copy-start | bytes 100
  64.7 18.9 %collective-permute-start = (bf16[64,48,128]{2,1,0:T(8,128)(2,1)S(1)}, bf16[64,48,128]{2,1,0:T(8,128)(2,1)S(1)}, u32[]{:S(2)}, u32[]{:S(2)}) collective-permute-start(bf16[64,48,128]{2,1,0:T(8,128)(2,1)S(1)} %all_to_all.5), channel_id=1, source_target_pairs={{0,16},{16,0},{128,144},{144,128},{256,272},{272,256},{384,400},{4... | collective-permute-start | bytes 2359304 | tf_op jit(solution)/shard_map/ppermute | solution.py:215
  71.1 12.5 %collective-permute-start.4 = (bf16[64,48,128]{2,1,0:T(8,128)(2,1)S(1)}, bf16[64,48,128]{2,1,0:T(8,128)(2,1)S(1)}, u32[]{:S(2)}, u32[]{:S(2)}) collective-permute-start(bf16[64,48,128]{2,1,0:T(8,128)(2,1)S(1)} %collective-permute-done.1), channel_id=1, source_target_pairs={{0,16},{16,0},{128,144},{144,128},{256,272},{272,256},{384,400},{4... | collective-permute-start | bytes 2359304 | tf_op jit(solution)/shard_map/ppermute | solution.py:217
  73.1 10.6 %collective-permute-start.5 = (bf16[64,48,128]{2,1,0:T(8,128)(2,1)S(1)}, bf16[64,48,128]{2,1,0:T(8,128)(2,1)S(1)}, u32[]{:S(2)}, u32[]{:S(2)}) collective-permute-start(bf16[64,48,128]{2,1,0:T(8,128)(2,1)S(1)} %collective-permute-done.2), channel_id=1, source_target_pairs={{0,16},{16,0},{128,144},{144,128},{256,272},{272,256},{384,400},{4... | collective-permute-start | bytes 2359304 | tf_op jit(solution)/shard_map/ppermute | solution.py:218
  75.5 9.5 %collective-permute-start.6 = (bf16[64,48,128]{2,1,0:T(8,128)(2,1)S(1)}, bf16[64,48,128]{2,1,0:T(8,128)(2,1)S(1)}, u32[]{:S(2)}, u32[]{:S(2)}) collective-permute-start(bf16[64,48,128]{2,1,0:T(8,128)(2,1)S(1)} %collective-permute-done.3), channel_id=1, source_target_pairs={{0,16},{16,0},{128,144},{144,128},{256,272},{272,256},{384,400},{4... | collective-permute-start | bytes 2359304 | tf_op jit(solution)/shard_map/ppermute | solution.py:219
  93.9 10.8 %collective-permute-start.7 = (bf16[512,128]{1,0:T(8,128)(2,1)S(1)}, bf16[512,128]{1,0:T(8,128)(2,1)S(1)}, u32[]{:S(2)}, u32[]{:S(2)}) collective-permute-start(bf16[512,128]{1,0:T(8,128)(2,1)S(1)} %get-tuple-element.9), channel_id=1, source_target_pairs={{0,0},{1,1},{2,128},{3,129},{4,256},{5,257},{6,384},{7,385},{8,16}... | collective-permute-start | bytes 393224 | tf_op jit(solution)/shard_map/ppermute | solution.py:248
  97.5 18.5 %collective-permute-start.8 = (bf16[512,128]{1,0:T(8,128)(2,1)S(1)}, bf16[512,128]{1,0:T(8,128)(2,1)S(1)}, u32[]{:S(2)}, u32[]{:S(2)}) collective-permute-start(bf16[512,128]{1,0:T(8,128)(2,1)S(1)} %get-tuple-element.10), channel_id=1, source_target_pairs={{0,1},{1,0},{2,129},{3,128},{4,257},{5,256},{6,385},{7,384},{8,17}... | collective-permute-start | bytes 393224 | tf_op jit(solution)/shard_map/ppermute | solution.py:249

commit v5 on v4

--- a/solution.py
+++ b/solution.py
@@ -54,12 +54,13 @@
 def attend_kernel(slab_ref, dst_ref, start_ref, home_ref, *refs):
     shards, (out_ref, q_s, k_s, v_s, sem_q, sem_k, sem_v) = refs[:8], refs[8:]
     for i, shard in enumerate(shards):
-        for yl in range(4):
-            h = home_ref[i] + yl * 2
-            for buf, lo, sem in ((q_s, 0, sem_q), (k_s, 16, sem_k), (v_s, 32, sem_v)):
-                pltpu.make_async_copy(
-                    shard.at[yl, :, pl.ds(lo, SLAB), :], buf.at[h], sem
-                ).start()
+        x, core = home_ref[i] >> 3, home_ref[i] & 1
+        for buf, lo, sem in ((q_s, 0, sem_q), (k_s, 16, sem_k), (v_s, 32, sem_v)):
+            pltpu.make_async_copy(
+                shard.at[:, :, pl.ds(lo, SLAB), :],
+                buf.reshape(4, 4, 2, 16, SLAB, DH).at[x, :, core],
+                sem,
+            ).start()
     pltpu.make_async_copy(q_s, q_s, sem_q).wait()
     pltpu.make_async_copy(k_s, k_s, sem_k).wait()
     pltpu.make_async_copy(v_s, v_s, sem_v).wait()

time: 117 us -> 116 us (level)
  no operation moved by 1% of the time
where the time goes in v5:
time: 116 us
  starting transfers between devices  44.2 us (38%)
  blocking collectives  39.8 us (34%)
  waiting for transfers between devices  19.6 us (17%)
  Pallas kernels  10 us (9%)
  other arithmetic  1.35 us (1%)
    all_to_all x1, blocking collectives, per_device(): lax.all_to_all(parted, HEAD_AXES, split_axis=0, concat_axis=0, tiled=True)  39.8 us
    ppermute x1, waiting for transfers between devices, per_device(): other = lax.ppermute(attended[512:], moved, to_owner(1))  11.3 us
    pallas_call x1, Pallas kernels, attend(): pl.pallas_call(attend_kernel, out_shape=jax.ShapeDtypeStruct((ROWS, DH),...  7.91 us
    ppermute x1, starting transfers between devices, gather_row(): far_other = lax.ppermute(far, row, swap)  7.65 us
    ppermute x1, starting transfers between devices, per_device(): other = lax.ppermute(attended[512:], moved, to_owner(1))  7.22 us
    ppermute x1, waiting for transfers between devices, gather_row(): near = lax.ppermute(mine, row, ring)  6.88 us
    ppermute x1, starting transfers between devices, gather_row(): other = lax.ppermute(mine, row, swap)  6.39 us
    ppermute x1, starting transfers between devices, gather_row(): near_other = lax.ppermute(mine, row, crossed)  5.64 us
  transfers between devices with their start and end apart: 9, of which 3 were waited for; matrix products, arithmetic and copies ran while one was open for 1% of the time, Pallas kernels for 0%

profile of v5, /device:TPU:1, one launch (start us, length us, event | category | flops | bytes accessed | tf_op | source)
XLA Modules:
  0.0 115.8 jit_solution(17804742209895797525)
XLA Ops:
  0.0 2.1 %split_heads.1 = bf16[64,48,128]{2,1,0:T(8,128)(2,1)} custom-call(bf16[16,8192]{1,0:T(8,128)(2,1)} %q_ref.1, bf16[16,8192]{1,0:T(8,128)(2,1)} %k_ref.1, bf16[16,8192]{1,0:T(8,128)(2,1)} %v_ref.1), custom_call_target="tpu_custom_call" | custom-call | tf_op jit(solution)/shard_map/split_heads/pallas_call | solution.py:38
  2.1 39.8 %all_to_all.5 = bf16[64,48,128]{2,1,0:T(8,128)(2,1)S(1)} all-to-all(bf16[64,48,128]{2,1,0:T(8,128)(2,1)} %split_heads.1), channel_id=1, replica_groups=mesh['x'=4,'yl'=4,'core'=2,'zh'=2,'zl'=4,'yh'=2] {'yl','zh','zl','yh'}, dimensions={0} | all-to-all | bytes 1572864 | tf_op jit(solution)/shard_map/all_to_all | solution.py:245
  41.9 4.4 %collective-permute-start.1 = (bf16[64,48,128]{2,1,0:T(8,128)(2,1)S(1)}, bf16[64,48,128]{2,1,0:T(8,128)(2,1)S(1)}, u32[]{:S(2)}, u32[]{:S(2)}) collective-permute-start(bf16[64,48,128]{2,1,0:T(8,128)(2,1)S(1)} %all_to_all.5), channel_id=1, source_target_pairs={{0,128},{16,400},{128,256},{144,16},{256,384},{272,144},{384,0},{4... | collective-permute-start | bytes 2359304 | tf_op jit(solution)/shard_map/ppermute | solution.py:214
  46.3 5.6 %collective-permute-start.2 = (bf16[64,48,128]{2,1,0:T(8,128)(2,1)S(1)}, bf16[64,48,128]{2,1,0:T(8,128)(2,1)S(1)}, u32[]{:S(2)}, u32[]{:S(2)}) collective-permute-start(bf16[64,48,128]{2,1,0:T(8,128)(2,1)S(1)} %all_to_all.5), channel_id=1, source_target_pairs={{0,400},{16,128},{128,16},{144,256},{256,144},{272,384},{384,272},... | collective-permute-start | bytes 2359304 | tf_op jit(solution)/shard_map/ppermute | solution.py:215
  51.9 6.9 %collective-permute-done.1 = bf16[64,48,128]{2,1,0:T(8,128)(2,1)S(1)} collective-permute-done((bf16[64,48,128]{2,1,0:T(8,128)(2,1)S(1)}, bf16[64,48,128]{2,1,0:T(8,128)(2,1)S(1)}, u32[]{:S(2)}, u32[]{:S(2)}) %collective-permute-start.1) | collective-permute-done | bytes 786464 | tf_op jit(solution)/shard_map/ppermute | solution.py:214
  58.8 5.0 %collective-permute-start.3 = (bf16[64,48,128]{2,1,0:T(8,128)(2,1)S(1)}, bf16[64,48,128]{2,1,0:T(8,128)(2,1)S(1)}, u32[]{:S(2)}, u32[]{:S(2)}) collective-permute-start(bf16[64,48,128]{2,1,0:T(8,128)(2,1)S(1)} %collective-permute-done.1), channel_id=1, source_target_pairs={{0,128},{16,400},{128,256},{144,16},{256,384},{272,144},{384,0},{4... | collective-permute-start | bytes 2359304 | tf_op jit(solution)/shard_map/ppermute | solution.py:217
  63.9 0.0 copy-start
  63.9 0.1 stack.35.home_ref
  64.0 0.6 copy-done
  64.6 0.0 copy-start.1
  64.6 0.1 convert_reduce_fusion
  64.7 6.4 %collective-permute-start = (bf16[64,48,128]{2,1,0:T(8,128)(2,1)S(1)}, bf16[64,48,128]{2,1,0:T(8,128)(2,1)S(1)}, u32[]{:S(2)}, u32[]{:S(2)}) collective-permute-start(bf16[64,48,128]{2,1,0:T(8,128)(2,1)S(1)} %all_to_all.5), channel_id=1, source_target_pairs={{0,16},{16,0},{128,144},{144,128},{256,272},{272,256},{384,400},{4... | collective-permute-start | bytes 2359304 | tf_op jit(solution)/shard_map/ppermute | solution.py:216
  71.1 1.9 %collective-permute-start.4 = (bf16[64,48,128]{2,1,0:T(8,128)(2,1)S(1)}, bf16[64,48,128]{2,1,0:T(8,128)(2,1)S(1)}, u32[]{:S(2)}, u32[]{:S(2)}) collective-permute-start(bf16[64,48,128]{2,1,0:T(8,128)(2,1)S(1)} %collective-permute-done.1), channel_id=1, source_target_pairs={{0,16},{16,0},{128,144},{144,128},{256,272},{272,256},{384,400},{4... | collective-permute-start | bytes 2359304 | tf_op jit(solution)/shard_map/ppermute | solution.py:218
  73.0 0.0 collective-permute-done.2
  73.1 2.4 %collective-permute-start.5 = (bf16[64,48,128]{2,1,0:T(8,128)(2,1)S(1)}, bf16[64,48,128]{2,1,0:T(8,128)(2,1)S(1)}, u32[]{:S(2)}, u32[]{:S(2)}) collective-permute-start(bf16[64,48,128]{2,1,0:T(8,128)(2,1)S(1)} %collective-permute-done.2), channel_id=1, source_target_pairs={{0,16},{16,0},{128,144},{144,128},{256,272},{272,256},{384,400},{4... | collective-permute-start | bytes 2359304 | tf_op jit(solution)/shard_map/ppermute | solution.py:219
  75.5 0.0 collective-permute-done.3
  75.5 7.6 %collective-permute-start.6 = (bf16[64,48,128]{2,1,0:T(8,128)(2,1)S(1)}, bf16[64,48,128]{2,1,0:T(8,128)(2,1)S(1)}, u32[]{:S(2)}, u32[]{:S(2)}) collective-permute-start(bf16[64,48,128]{2,1,0:T(8,128)(2,1)S(1)} %collective-permute-done.3), channel_id=1, source_target_pairs={{0,16},{16,0},{128,144},{144,128},{256,272},{272,256},{384,400},{4... | collective-permute-start | bytes 2359304 | tf_op jit(solution)/shard_map/ppermute | solution.py:220
  83.1 0.0 copy-done.1
  83.1 0.1 select_reduce_fusion.2.start_ref
  83.3 0.1 select_reduce_fusion
  83.4 0.2 convert_reduce_fusion.1
  83.6 0.0 collective-permute-done
  83.6 0.0 collective-permute-done.5
  83.6 0.0 collective-permute-done.4
  83.6 1.4 %collective-permute-done.6 = bf16[64,48,128]{2,1,0:T(8,128)(2,1)S(1)} collective-permute-done((bf16[64,48,128]{2,1,0:T(8,128)(2,1)S(1)}, bf16[64,48,128]{2,1,0:T(8,128)(2,1)S(1)}, u32[]{:S(2)}, u32[]{:S(2)}) %collective-permute-start.6) | collective-permute-done | bytes 786464 | tf_op jit(solution)/shard_map/ppermute | solution.py:220
  85.0 7.9 %attend.1 = bf16[1024,128]{1,0:T(8,128)(2,1)S(1)} custom-call(s32[64]{0:T(128)S(1)} %get-tuple-element.6.slab_ref, s32[64]{0:T(128)S(1)} %multiply_add_fusion.dst_ref, s32[8]{0:T(128)S(1)} %select_reduce_fusion.2.start_ref, s32[8]{0:T(128)S(1)} %stack.35.home_ref, bf16[4,16,48,128]{3,2,1,0:T(8,128)(2,1)S(1)} %bitcast.16, ...), custom_call_target="tpu_custom_call" | custom-call | flops 2000000000 | bytes 8388608 | tf_op jit(solution)/shard_map/attend/pallas_call | solution.py:152
  93.0 3.6 %collective-permute-start.7 = (bf16[512,128]{1,0:T(8,128)(2,1)S(1)}, bf16[512,128]{1,0:T(8,128)(2,1)S(1)}, u32[]{:S(2)}, u32[]{:S(2)}) collective-permute-start(bf16[512,128]{1,0:T(8,128)(2,1)S(1)} %get-tuple-element.9), channel_id=1, source_target_pairs={{0,0},{1,1},{2,128},{3,129},{4,256},{5,257},{6,384},{7,385},{8,16}... | collective-permute-start | bytes 393224 | tf_op jit(solution)/shard_map/ppermute | solution.py:249
  96.5 7.2 %collective-permute-start.8 = (bf16[512,128]{1,0:T(8,128)(2,1)S(1)}, bf16[512,128]{1,0:T(8,128)(2,1)S(1)}, u32[]{:S(2)}, u32[]{:S(2)}) collective-permute-start(bf16[512,128]{1,0:T(8,128)(2,1)S(1)} %get-tuple-element.10), channel_id=1, source_target_pairs={{0,1},{1,0},{2,129},{3,128},{4,257},{5,256},{6,385},{7,384},{8,17}... | collective-permute-start | bytes 393224 | tf_op jit(solution)/shard_map/ppermute | solution.py:250
  103.8 0.0 collective-permute-done.7
  103.8 11.3 %collective-permute-done.8 = bf16[512,128]{1,0:T(8,128)(2,1)S(1)} collective-permute-done((bf16[512,128]{1,0:T(8,128)(2,1)S(1)}, bf16[512,128]{1,0:T(8,128)(2,1)S(1)}, u32[]{:S(2)}, u32[]{:S(2)}) %collective-permute-start.8) | collective-permute-done | bytes 131104 | tf_op jit(solution)/shard_map/ppermute | solution.py:250
  115.1 0.7 pad_maximum_fusion
  (5 shorter events, 0.1 us)
Async XLA Ops:
  41.9 16.9 %collective-permute-start.1 = (bf16[64,48,128]{2,1,0:T(8,128)(2,1)S(1)}, bf16[64,48,128]{2,1,0:T(8,128)(2,1)S(1)}, u32[]{:S(2)}, u32[]{:S(2)}) collective-permute-start(bf16[64,48,128]{2,1,0:T(8,128)(2,1)S(1)} %all_to_all.5), channel_id=1, source_target_pairs={{0,128},{16,400},{128,256},{144,16},{256,384},{272,144},{384,0},{4... | collective-permute-start | bytes 2359304 | tf_op jit(solution)/shard_map/ppermute | solution.py:214
  46.3 26.7 %collective-permute-start.2 = (bf16[64,48,128]{2,1,0:T(8,128)(2,1)S(1)}, bf16[64,48,128]{2,1,0:T(8,128)(2,1)S(1)}, u32[]{:S(2)}, u32[]{:S(2)}) collective-permute-start(bf16[64,48,128]{2,1,0:T(8,128)(2,1)S(1)} %all_to_all.5), channel_id=1, source_target_pairs={{0,400},{16,128},{128,16},{144,256},{256,144},{272,384},{384,272},... | collective-permute-start | bytes 2359304 | tf_op jit(solution)/shard_map/ppermute | solution.py:215
  58.8 16.6 %collective-permute-start.3 = (bf16[64,48,128]{2,1,0:T(8,128)(2,1)S(1)}, bf16[64,48,128]{2,1,0:T(8,128)(2,1)S(1)}, u32[]{:S(2)}, u32[]{:S(2)}) collective-permute-start(bf16[64,48,128]{2,1,0:T(8,128)(2,1)S(1)} %collective-permute-done.1), channel_id=1, source_target_pairs={{0,128},{16,400},{128,256},{144,16},{256,384},{272,144},{384,0},{4... | collective-permute-start | bytes 2359304 | tf_op jit(solution)/shard_map/ppermute | solution.py:217
  63.9 0.7 copy-start
  64.6 18.6 %copy-start.1 = (s32[8]{0:T(128)S(1)}, s32[8]{0:T(128)}, u32[]{:S(2)}) copy-start(s32[8]{0:T(128)} %param.8) | copy-start | bytes 100
  64.7 18.9 %collective-permute-start = (bf16[64,48,128]{2,1,0:T(8,128)(2,1)S(1)}, bf16[64,48,128]{2,1,0:T(8,128)(2,1)S(1)}, u32[]{:S(2)}, u32[]{:S(2)}) collective-permute-start(bf16[64,48,128]{2,1,0:T(8,128)(2,1)S(1)} %all_to_all.5), channel_id=1, source_target_pairs={{0,16},{16,0},{128,144},{144,128},{256,272},{272,256},{384,400},{4... | collective-permute-start | bytes 2359304 | tf_op jit(solution)/shard_map/ppermute | solution.py:216
  71.1 12.5 %collective-permute-start.4 = (bf16[64,48,128]{2,1,0:T(8,128)(2,1)S(1)}, bf16[64,48,128]{2,1,0:T(8,128)(2,1)S(1)}, u32[]{:S(2)}, u32[]{:S(2)}) collective-permute-start(bf16[64,48,128]{2,1,0:T(8,128)(2,1)S(1)} %collective-permute-done.1), channel_id=1, source_target_pairs={{0,16},{16,0},{128,144},{144,128},{256,272},{272,256},{384,400},{4... | collective-permute-start | bytes 2359304 | tf_op jit(solution)/shard_map/ppermute | solution.py:218
  73.1 10.6 %collective-permute-start.5 = (bf16[64,48,128]{2,1,0:T(8,128)(2,1)S(1)}, bf16[64,48,128]{2,1,0:T(8,128)(2,1)S(1)}, u32[]{:S(2)}, u32[]{:S(2)}) collective-permute-start(bf16[64,48,128]{2,1,0:T(8,128)(2,1)S(1)} %collective-permute-done.2), channel_id=1, source_target_pairs={{0,16},{16,0},{128,144},{144,128},{256,272},{272,256},{384,400},{4... | collective-permute-start | bytes 2359304 | tf_op jit(solution)/shard_map/ppermute | solution.py:219
  75.5 9.5 %collective-permute-start.6 = (bf16[64,48,128]{2,1,0:T(8,128)(2,1)S(1)}, bf16[64,48,128]{2,1,0:T(8,128)(2,1)S(1)}, u32[]{:S(2)}, u32[]{:S(2)}) collective-permute-start(bf16[64,48,128]{2,1,0:T(8,128)(2,1)S(1)} %collective-permute-done.3), channel_id=1, source_target_pairs={{0,16},{16,0},{128,144},{144,128},{256,272},{272,256},{384,400},{4... | collective-permute-start | bytes 2359304 | tf_op jit(solution)/shard_map/ppermute | solution.py:220
  93.0 10.8 %collective-permute-start.7 = (bf16[512,128]{1,0:T(8,128)(2,1)S(1)}, bf16[512,128]{1,0:T(8,128)(2,1)S(1)}, u32[]{:S(2)}, u32[]{:S(2)}) collective-permute-start(bf16[512,128]{1,0:T(8,128)(2,1)S(1)} %get-tuple-element.9), channel_id=1, source_target_pairs={{0,0},{1,1},{2,128},{3,129},{4,256},{5,257},{6,384},{7,385},{8,16}... | collective-permute-start | bytes 393224 | tf_op jit(solution)/shard_map/ppermute | solution.py:249
  96.5 18.5 %collective-permute-start.8 = (bf16[512,128]{1,0:T(8,128)(2,1)S(1)}, bf16[512,128]{1,0:T(8,128)(2,1)S(1)}, u32[]{:S(2)}, u32[]{:S(2)}) collective-permute-start(bf16[512,128]{1,0:T(8,128)(2,1)S(1)} %get-tuple-element.10), channel_id=1, source_target_pairs={{0,1},{1,0},{2,129},{3,128},{4,257},{5,256},{6,385},{7,384},{8,17}... | collective-permute-start | bytes 393224 | tf_op jit(solution)/shard_map/ppermute | solution.py:250

commit v6 on v5

--- a/solution.py
+++ b/solution.py
@@ -13,7 +13,7 @@
 BK = 2048
 HALF = 1024
 TOGETHER = 2
-ROWS = 1024
+ROWS = 512
 SLABS_HERE = ROWS // SLAB
 FOLD = DH ** (-0.5) * 1.4426950408889634
 AXES = ("x", "yl", "core", "zh", "zl", "yh")
@@ -51,7 +51,7 @@
     return first
 
 
-def attend_kernel(slab_ref, dst_ref, start_ref, home_ref, *refs):
+def attend_kernel(slab_ref, start_ref, home_ref, *refs):
     shards, (out_ref, q_s, k_s, v_s, sem_q, sem_k, sem_v) = refs[:8], refs[8:]
     for i, shard in enumerate(shards):
         x, core = home_ref[i] >> 3, home_ref[i] & 1
@@ -137,22 +137,22 @@
         )
         for g, (high, denom, acc) in enumerate(states):
             result = (acc / jnp.sum(denom, axis=1, keepdims=True)).astype(jnp.bfloat16)
-            for i in range(per_tile):
-                to = dst_ref[(group * TOGETHER + g) * per_tile + i]
-                out_ref[pl.ds(pl.multiple_of(to, SLAB), SLAB), :] = result[i * SLAB:(i + 1) * SLAB]
+            out_ref[pl.ds(pl.multiple_of((group * TOGETHER + g) * TQ, TQ), TQ), :] = result
         return carry
 
+    if out_ref.shape[0] > ROWS:
+        out_ref[ROWS:, :] = jnp.zeros((out_ref.shape[0] - ROWS, DH), jnp.bfloat16)
     lax.fori_loop(0, ROWS // TQ // TOGETHER, some, 0)
 
 
-def attend(slabs, dst, starts, homes, shards):
+def attend(slabs, starts, homes, shards, extra):
     smem = pl.BlockSpec(memory_space=pltpu.SMEM)
     shards = [shard.reshape(4, 16, 48, DH) for shard in shards]
     whole = pltpu.VMEM((32, 16, SLAB, DH), jnp.bfloat16)
     return pl.pallas_call(
         attend_kernel,
-        out_shape=jax.ShapeDtypeStruct((ROWS, DH), jnp.bfloat16),
-        in_specs=[smem] * 4 + [pl.BlockSpec(memory_space=pl.ANY)] * 8,
+        out_shape=jax.ShapeDtypeStruct((ROWS + extra, DH), jnp.bfloat16),
+        in_specs=[smem] * 3 + [pl.BlockSpec(memory_space=pl.ANY)] * 8,
         out_specs=pl.BlockSpec(memory_space=pltpu.VMEM),
         scratch_shapes=[whole, whole, whole] + [pltpu.SemaphoreType.DMA] * 3,
         compiler_params=pltpu.CompilerParams(vmem_limit_bytes=32 * 1024 * 1024),
@@ -160,28 +160,22 @@
             flops=2 * 10**9, bytes_accessed=8 * 2**20, transcendentals=2 * 10**6
         ),
         name="attend",
-    )(slabs, dst, starts, homes, *shards)
-
-
-def tables(doc_lengths, slab_owner):
+    )(slabs, starts, homes, *shards)
+
+
+def tables(doc_lengths, slab_owner, flip):
     part = lax.axis_index("core") * 4 + lax.axis_index("x")
-    yh = lax.axis_index("yh")
+    owner = part * 2 + (lax.axis_index("yh") ^ flip)
     n = slab_owner.shape[0]
     index = jnp.arange(n, dtype=jnp.int32)
-    mine = (slab_owner >> 1) == part
+    mine = slab_owner == owner
     before = jnp.sum((mine[None, :] & (index[None, :] < index[:, None])).astype(jnp.int32), axis=1)
     here = jnp.arange(SLABS_HERE, dtype=jnp.int32)
     hit = mine[None, :] & (before[None, :] == here[:, None])
     slabs = jnp.sum(jnp.where(hit, index[None, :], 0), axis=1)
-    low_owner = jnp.sum(jnp.where(hit, slab_owner[None, :] & 1, 0), axis=1)
-    rank = jnp.sum(
-        ((low_owner[None, :] == low_owner[:, None]) & (here[None, :] < here[:, None])).astype(jnp.int32),
-        axis=1,
-    )
-    dst = (low_owner ^ yh) * 512 + rank * SLAB
     earlier = jnp.arange(8)[None, :] < jnp.arange(8)[:, None]
     starts = jnp.sum(jnp.where(earlier, doc_lengths[None, :], 0), axis=1)
-    return slabs, dst, starts
+    return slabs, starts
 
 
 def to_owner(swap):
@@ -240,14 +234,16 @@
 
 
 def per_device(queries, keys, values, doc_lengths, slab_owner):
-    slabs, dst, starts = tables(doc_lengths, slab_owner)
+    far_slabs, starts = tables(doc_lengths, slab_owner, 1)
+    near_slabs, _ = tables(doc_lengths, slab_owner, 0)
     parted = split_heads(queries, keys, values)
     landed = lax.all_to_all(parted, HEAD_AXES, split_axis=0, concat_axis=0, tiled=True)
     shards, homes = gather_row(landed)
-    attended = attend(slabs, dst, starts, homes, shards)
     moved = ("x", "core", "zh", "zl", "yh")
-    same = lax.ppermute(attended[:512], moved, to_owner(0))
-    other = lax.ppermute(attended[512:], moved, to_owner(1))
+    crossing = attend(far_slabs, starts, homes, shards, 16)
+    other = lax.ppermute(crossing, moved, to_owner(1))[:512]
+    staying = attend(near_slabs, starts, homes, shards, 0)
+    same = lax.ppermute(staying, moved, to_owner(0))
     first = lax.axis_index("yh") == 0
     return jnp.concatenate(
         [jnp.where(first, same, other), jnp.where(first, other, same)], axis=1

time: 116 us -> 117 us (level)
  the two profiles are of different devices: /device:TPU:1 before, /device:TPU:15 now
where the time goes in v6:
time: 117 us; the launch traced here: 116 us
  starting transfers between devices  41.4 us (35%)
  blocking collectives  38.6 us (33%)
  waiting for transfers between devices  19.1 us (16%)
  Pallas kernels  15.5 us (13%)
  other arithmetic  1.43 us (1%)
    all_to_all x1, blocking collectives, per_device(): lax.all_to_all(parted, HEAD_AXES, split_axis=0, concat_axis=0, tiled=True)  38.6 us
    pallas_call x2, Pallas kernels, attend(): pl.pallas_call(attend_kernel, out_shape=jax.ShapeDtypeStruct((ROWS + extr...  13.3 us
    ppermute x1, waiting for transfers between devices, gather_row(): near = lax.ppermute(mine, row, ring)  9.14 us
    ppermute x1, waiting for transfers between devices, per_device(): same = lax.ppermute(staying, moved, to_owner(0))  8.79 us
    ppermute x1, starting transfers between devices, gather_row(): other = lax.ppermute(mine, row, swap)  8.44 us
    ppermute x1, starting transfers between devices, gather_row(): far_other = lax.ppermute(far, row, swap)  6.79 us
    ppermute x1, starting transfers between devices, gather_row(): near_other = lax.ppermute(mine, row, crossed)  6.25 us
    ppermute x1, starting transfers between devices, per_device(): other = lax.ppermute(crossing, moved, to_owner(1))[:512]  6.21 us
  transfers between devices with their start and end apart: 9, of which 3 were waited for; matrix products, arithmetic and copies ran while one was open for 1% of the time, Pallas kernels for 6%

profile of v6, /device:TPU:15, one launch (start us, length us, event | category | flops | bytes accessed | tf_op | source)
XLA Modules:
  0.0 116.3 jit_solution(1927741681476587345)
XLA Ops:
  0.0 2.1 %split_heads.1 = bf16[64,48,128]{2,1,0:T(8,128)(2,1)} custom-call(bf16[16,8192]{1,0:T(8,128)(2,1)} %q_ref.1, bf16[16,8192]{1,0:T(8,128)(2,1)} %k_ref.1, bf16[16,8192]{1,0:T(8,128)(2,1)} %v_ref.1), custom_call_target="tpu_custom_call" | custom-call | tf_op jit(solution)/shard_map/split_heads/pallas_call | solution.py:38
  2.1 38.6 %all_to_all.5 = bf16[64,48,128]{2,1,0:T(8,128)(2,1)S(1)} all-to-all(bf16[64,48,128]{2,1,0:T(8,128)(2,1)} %split_heads.1), channel_id=1, replica_groups=mesh['x'=4,'yl'=4,'core'=2,'zh'=2,'zl'=4,'yh'=2] {'yl','zh','zl','yh'}, dimensions={0} | all-to-all | bytes 1572864 | tf_op jit(solution)/shard_map/all_to_all | solution.py:240
  40.7 2.4 %collective-permute-start.1 = (bf16[64,48,128]{2,1,0:T(8,128)(2,1)S(1)}, bf16[64,48,128]{2,1,0:T(8,128)(2,1)S(1)}, u32[]{:S(2)}, u32[]{:S(2)}) collective-permute-start(bf16[64,48,128]{2,1,0:T(8,128)(2,1)S(1)} %all_to_all.5), channel_id=1, source_target_pairs={{0,128},{16,400},{128,256},{144,16},{256,384},{272,144},{384,0},{4... | collective-permute-start | bytes 2359304 | tf_op jit(solution)/shard_map/ppermute | solution.py:208
  43.2 6.3 %collective-permute-start.2 = (bf16[64,48,128]{2,1,0:T(8,128)(2,1)S(1)}, bf16[64,48,128]{2,1,0:T(8,128)(2,1)S(1)}, u32[]{:S(2)}, u32[]{:S(2)}) collective-permute-start(bf16[64,48,128]{2,1,0:T(8,128)(2,1)S(1)} %all_to_all.5), channel_id=1, source_target_pairs={{0,400},{16,128},{128,16},{144,256},{256,144},{272,384},{384,272},... | collective-permute-start | bytes 2359304 | tf_op jit(solution)/shard_map/ppermute | solution.py:209
  49.5 9.1 %collective-permute-done.1 = bf16[64,48,128]{2,1,0:T(8,128)(2,1)S(1)} collective-permute-done((bf16[64,48,128]{2,1,0:T(8,128)(2,1)S(1)}, bf16[64,48,128]{2,1,0:T(8,128)(2,1)S(1)}, u32[]{:S(2)}, u32[]{:S(2)}) %collective-permute-start.1) | collective-permute-done | bytes 786464 | tf_op jit(solution)/shard_map/ppermute | solution.py:208
  58.6 1.9 %collective-permute-start.3 = (bf16[64,48,128]{2,1,0:T(8,128)(2,1)S(1)}, bf16[64,48,128]{2,1,0:T(8,128)(2,1)S(1)}, u32[]{:S(2)}, u32[]{:S(2)}) collective-permute-start(bf16[64,48,128]{2,1,0:T(8,128)(2,1)S(1)} %collective-permute-done.1), channel_id=1, source_target_pairs={{0,128},{16,400},{128,256},{144,16},{256,384},{272,144},{384,0},{4... | collective-permute-start | bytes 2359304 | tf_op jit(solution)/shard_map/ppermute | solution.py:211
  60.5 0.0 copy-start.1
  60.6 0.0 copy-start
  60.6 0.1 stack.35.home_ref
  60.6 8.4 %collective-permute-start = (bf16[64,48,128]{2,1,0:T(8,128)(2,1)S(1)}, bf16[64,48,128]{2,1,0:T(8,128)(2,1)S(1)}, u32[]{:S(2)}, u32[]{:S(2)}) collective-permute-start(bf16[64,48,128]{2,1,0:T(8,128)(2,1)S(1)} %all_to_all.5), channel_id=1, source_target_pairs={{0,16},{16,0},{128,144},{144,128},{256,272},{272,256},{384,400},{4... | collective-permute-start | bytes 2359304 | tf_op jit(solution)/shard_map/ppermute | solution.py:210
  69.1 1.9 %collective-permute-start.4 = (bf16[64,48,128]{2,1,0:T(8,128)(2,1)S(1)}, bf16[64,48,128]{2,1,0:T(8,128)(2,1)S(1)}, u32[]{:S(2)}, u32[]{:S(2)}) collective-permute-start(bf16[64,48,128]{2,1,0:T(8,128)(2,1)S(1)} %collective-permute-done.1), channel_id=1, source_target_pairs={{0,16},{16,0},{128,144},{144,128},{256,272},{272,256},{384,400},{4... | collective-permute-start | bytes 2359304 | tf_op jit(solution)/shard_map/ppermute | solution.py:212
  71.0 0.0 collective-permute-done.2
  71.0 2.4 %collective-permute-start.5 = (bf16[64,48,128]{2,1,0:T(8,128)(2,1)S(1)}, bf16[64,48,128]{2,1,0:T(8,128)(2,1)S(1)}, u32[]{:S(2)}, u32[]{:S(2)}) collective-permute-start(bf16[64,48,128]{2,1,0:T(8,128)(2,1)S(1)} %collective-permute-done.2), channel_id=1, source_target_pairs={{0,16},{16,0},{128,144},{144,128},{256,272},{272,256},{384,400},{4... | collective-permute-start | bytes 2359304 | tf_op jit(solution)/shard_map/ppermute | solution.py:213
  73.5 0.0 collective-permute-done.3
  73.5 6.8 %collective-permute-start.6 = (bf16[64,48,128]{2,1,0:T(8,128)(2,1)S(1)}, bf16[64,48,128]{2,1,0:T(8,128)(2,1)S(1)}, u32[]{:S(2)}, u32[]{:S(2)}) collective-permute-start(bf16[64,48,128]{2,1,0:T(8,128)(2,1)S(1)} %collective-permute-done.3), channel_id=1, source_target_pairs={{0,16},{16,0},{128,144},{144,128},{256,272},{272,256},{384,400},{4... | collective-permute-start | bytes 2359304 | tf_op jit(solution)/shard_map/ppermute | solution.py:214
  80.3 0.0 copy-done.1
  80.3 0.1 select_reduce_fusion.2.start_ref
  80.4 0.0 copy-done
  80.4 0.1 convert_reduce_fusion
  80.5 0.1 select_reduce_fusion.slab_ref
  80.7 0.2 convert_reduce_fusion.1
  80.8 0.1 select_reduce_fusion.1.slab_ref
  81.0 0.0 collective-permute-done
  81.0 0.0 collective-permute-done.5
  81.0 0.0 collective-permute-done.4
  81.0 1.2 collective-permute-done.6
  82.1 6.7 %attend.3 = bf16[528,128]{1,0:T(8,128)(2,1)S(1)} custom-call(s32[32]{0:T(128)S(1)} %select_reduce_fusion.slab_ref, s32[8]{0:T(128)S(1)} %select_reduce_fusion.2.start_ref, s32[8]{0:T(128)S(1)} %stack.35.home_ref, bf16[4,16,48,128]{3,2,1,0:T(8,128)(2,1)S(1)} %bitcast.16, bf16[4,16,48,128]{3,2,1,0:T(8,128)(2,1)S(1)} %bitcast.24, ...), custom_call_target="tpu_custom_call" | custom-call | flops 2000000000 | bytes 8388608 | tf_op jit(solution)/shard_map/attend/pallas_call | solution.py:152
  88.8 6.2 %collective-permute-start.8 = (bf16[528,128]{1,0:T(8,128)(2,1)S(1)}, bf16[528,128]{1,0:T(8,128)(2,1)S(1)}, u32[]{:S(2)}, u32[]{:S(2)}) collective-permute-start(bf16[528,128]{1,0:T(8,128)(2,1)S(1)} %attend.3), channel_id=1, source_target_pairs={{0,1},{1,0},{2,129},{3,128},{4,257},{5,256},{6,385},{7,384},{8,17}... | collective-permute-start | bytes 405512 | tf_op jit(solution)/shard_map/ppermute | solution.py:244
  95.0 6.7 %attend.2 = bf16[512,128]{1,0:T(8,128)(2,1)S(1)} custom-call(s32[32]{0:T(128)S(1)} %select_reduce_fusion.1.slab_ref, s32[8]{0:T(128)S(1)} %select_reduce_fusion.2.start_ref, s32[8]{0:T(128)S(1)} %stack.35.home_ref, bf16[4,16,48,128]{3,2,1,0:T(8,128)(2,1)S(1)} %bitcast.17, bf16[4,16,48,128]{3,2,1,0:T(8,128)(2,1)S(1)} %bitcast.25, ...), custom_call_target="tpu_custom_call" | custom-call | flops 2000000000 | bytes 8388608 | tf_op jit(solution)/shard_map/attend/pallas_call | solution.py:152
  101.7 5.0 %collective-permute-start.7 = (bf16[512,128]{1,0:T(8,128)(2,1)S(1)}, bf16[512,128]{1,0:T(8,128)(2,1)S(1)}, u32[]{:S(2)}, u32[]{:S(2)}) collective-permute-start(bf16[512,128]{1,0:T(8,128)(2,1)S(1)} %attend.2), channel_id=1, source_target_pairs={{0,0},{1,1},{2,128},{3,129},{4,256},{5,257},{6,384},{7,385},{8,16}... | collective-permute-start | bytes 393224 | tf_op jit(solution)/shard_map/ppermute | solution.py:246
  106.8 8.8 %collective-permute-done.7 = bf16[512,128]{1,0:T(8,128)(2,1)S(1)} collective-permute-done((bf16[512,128]{1,0:T(8,128)(2,1)S(1)}, bf16[512,128]{1,0:T(8,128)(2,1)S(1)}, u32[]{:S(2)}, u32[]{:S(2)}) %collective-permute-start.7) | collective-permute-done | bytes 131104 | tf_op jit(solution)/shard_map/ppermute | solution.py:246
  115.5 0.0 collective-permute-done.8
  115.6 0.7 pad_maximum_fusion
  (2 shorter events, 0.0 us)
Async XLA Ops:
  40.7 17.9 %collective-permute-start.1 = (bf16[64,48,128]{2,1,0:T(8,128)(2,1)S(1)}, bf16[64,48,128]{2,1,0:T(8,128)(2,1)S(1)}, u32[]{:S(2)}, u32[]{:S(2)}) collective-permute-start(bf16[64,48,128]{2,1,0:T(8,128)(2,1)S(1)} %all_to_all.5), channel_id=1, source_target_pairs={{0,128},{16,400},{128,256},{144,16},{256,384},{272,144},{384,0},{4... | collective-permute-start | bytes 2359304 | tf_op jit(solution)/shard_map/ppermute | solution.py:208
  43.2 27.8 %collective-permute-start.2 = (bf16[64,48,128]{2,1,0:T(8,128)(2,1)S(1)}, bf16[64,48,128]{2,1,0:T(8,128)(2,1)S(1)}, u32[]{:S(2)}, u32[]{:S(2)}) collective-permute-start(bf16[64,48,128]{2,1,0:T(8,128)(2,1)S(1)} %all_to_all.5), channel_id=1, source_target_pairs={{0,400},{16,128},{128,16},{144,256},{256,144},{272,384},{384,272},... | collective-permute-start | bytes 2359304 | tf_op jit(solution)/shard_map/ppermute | solution.py:209
  58.6 14.9 %collective-permute-start.3 = (bf16[64,48,128]{2,1,0:T(8,128)(2,1)S(1)}, bf16[64,48,128]{2,1,0:T(8,128)(2,1)S(1)}, u32[]{:S(2)}, u32[]{:S(2)}) collective-permute-start(bf16[64,48,128]{2,1,0:T(8,128)(2,1)S(1)} %collective-permute-done.1), channel_id=1, source_target_pairs={{0,128},{16,400},{128,256},{144,16},{256,384},{272,144},{384,0},{4... | collective-permute-start | bytes 2359304 | tf_op jit(solution)/shard_map/ppermute | solution.py:211
  60.5 19.7 %copy-start.1 = (s32[8]{0:T(128)S(1)}, s32[8]{0:T(128)}, u32[]{:S(2)}) copy-start(s32[8]{0:T(128)} %param.8) | copy-start | bytes 100
  60.6 19.8 %copy-start = (s32[512]{0:T(512)S(1)}, s32[512]{0:T(512)}, u32[]{:S(2)}) copy-start(s32[512]{0:T(512)} %param.9) | copy-start | bytes 6148
  60.6 20.3 %collective-permute-start = (bf16[64,48,128]{2,1,0:T(8,128)(2,1)S(1)}, bf16[64,48,128]{2,1,0:T(8,128)(2,1)S(1)}, u32[]{:S(2)}, u32[]{:S(2)}) collective-permute-start(bf16[64,48,128]{2,1,0:T(8,128)(2,1)S(1)} %all_to_all.5), channel_id=1, source_target_pairs={{0,16},{16,0},{128,144},{144,128},{256,272},{272,256},{384,400},{4... | collective-permute-start | bytes 2359304 | tf_op jit(solution)/shard_map/ppermute | solution.py:210
  69.1 11.9 %collective-permute-start.4 = (bf16[64,48,128]{2,1,0:T(8,128)(2,1)S(1)}, bf16[64,48,128]{2,1,0:T(8,128)(2,1)S(1)}, u32[]{:S(2)}, u32[]{:S(2)}) collective-permute-start(bf16[64,48,128]{2,1,0:T(8,128)(2,1)S(1)} %collective-permute-done.1), channel_id=1, source_target_pairs={{0,16},{16,0},{128,144},{144,128},{256,272},{272,256},{384,400},{4... | collective-permute-start | bytes 2359304 | tf_op jit(solution)/shard_map/ppermute | solution.py:212
  71.0 9.9 %collective-permute-start.5 = (bf16[64,48,128]{2,1,0:T(8,128)(2,1)S(1)}, bf16[64,48,128]{2,1,0:T(8,128)(2,1)S(1)}, u32[]{:S(2)}, u32[]{:S(2)}) collective-permute-start(bf16[64,48,128]{2,1,0:T(8,128)(2,1)S(1)} %collective-permute-done.2), channel_id=1, source_target_pairs={{0,16},{16,0},{128,144},{144,128},{256,272},{272,256},{384,400},{4... | collective-permute-start | bytes 2359304 | tf_op jit(solution)/shard_map/ppermute | solution.py:213
  73.5 8.7 %collective-permute-start.6 = (bf16[64,48,128]{2,1,0:T(8,128)(2,1)S(1)}, bf16[64,48,128]{2,1,0:T(8,128)(2,1)S(1)}, u32[]{:S(2)}, u32[]{:S(2)}) collective-permute-start(bf16[64,48,128]{2,1,0:T(8,128)(2,1)S(1)} %collective-permute-done.3), channel_id=1, source_target_pairs={{0,16},{16,0},{128,144},{144,128},{256,272},{272,256},{384,400},{4... | collective-permute-start | bytes 2359304 | tf_op jit(solution)/shard_map/ppermute | solution.py:214
  88.8 26.7 %collective-permute-start.8 = (bf16[528,128]{1,0:T(8,128)(2,1)S(1)}, bf16[528,128]{1,0:T(8,128)(2,1)S(1)}, u32[]{:S(2)}, u32[]{:S(2)}) collective-permute-start(bf16[528,128]{1,0:T(8,128)(2,1)S(1)} %attend.3), channel_id=1, source_target_pairs={{0,1},{1,0},{2,129},{3,128},{4,257},{5,256},{6,385},{7,384},{8,17}... | collective-permute-start | bytes 405512 | tf_op jit(solution)/shard_map/ppermute | solution.py:244
  101.7 13.8 %collective-permute-start.7 = (bf16[512,128]{1,0:T(8,128)(2,1)S(1)}, bf16[512,128]{1,0:T(8,128)(2,1)S(1)}, u32[]{:S(2)}, u32[]{:S(2)}) collective-permute-start(bf16[512,128]{1,0:T(8,128)(2,1)S(1)} %attend.2), channel_id=1, source_target_pairs={{0,0},{1,1},{2,128},{3,129},{4,256},{5,257},{6,384},{7,385},{8,16}... | collective-permute-start | bytes 393224 | tf_op jit(solution)/shard_map/ppermute | solution.py:246

commit v7 on v6

--- a/solution.py
+++ b/solution.py
@@ -20,28 +20,46 @@
 HEAD_AXES = ("yl", "zh", "zl", "yh")
 
 
-def split_kernel(q_ref, k_ref, v_ref, out_ref):
-    for yl in range(4):
-        for zh in range(2):
-            for zl in range(4):
-                for yh in range(2):
-                    to = yl * 16 + zh * 8 + zl * 2 + yh
-                    head = zl * 16 + yl * 4 + zh * 2 + yh
-                    cols = slice(head * DH, (head + 1) * DH)
-                    out_ref[to, 0:16, :] = q_ref[:, cols]
-                    out_ref[to, 16:32, :] = k_ref[:, cols]
-                    out_ref[to, 32:48, :] = v_ref[:, cols]
+def split_kernel(q_ref, k_ref, v_ref, out_ref, in_s, out_s, in_sem, out_sem):
+    width = HEADS * DH // 4
+    loads = [
+        pltpu.make_async_copy(
+            ref.at[:, pl.ds(zl * width, width)], in_s.at[t, zl], in_sem.at[zl * 3 + t]
+        )
+        for zl in range(4)
+        for t, ref in enumerate((q_ref, k_ref, v_ref))
+    ]
+    for load in loads:
+        load.start()
+    stores = []
+    for zl in range(4):
+        for t in range(3):
+            loads[zl * 3 + t].wait()
+        for n in range(16):
+            yl, zh, yh = n >> 2, (n >> 1) & 1, n & 1
+            for t in range(3):
+                out_s[zl, yl, zh, yh, t * 16:(t + 1) * 16, :] = in_s[t, zl, :, n * DH:(n + 1) * DH]
+        stores.append(pltpu.make_async_copy(out_s.at[zl], out_ref.at[:, :, zl], out_sem.at[zl]))
+        stores[-1].start()
+    for store in stores:
+        store.wait()
 
 
 def split_heads(queries, keys, values):
-    vmem = pl.BlockSpec(memory_space=pltpu.VMEM)
+    hbm = pl.BlockSpec(memory_space=pl.ANY)
     return pl.pallas_call(
         split_kernel,
-        out_shape=jax.ShapeDtypeStruct((HEADS, 48, DH), jnp.bfloat16),
-        in_specs=[vmem, vmem, vmem],
-        out_specs=vmem,
+        out_shape=jax.ShapeDtypeStruct((4, 2, 4, 2, 48, DH), jnp.bfloat16),
+        in_specs=[hbm, hbm, hbm],
+        out_specs=hbm,
+        scratch_shapes=[
+            pltpu.VMEM((3, 4, SLAB, HEADS * DH // 4), jnp.bfloat16),
+            pltpu.VMEM((4, 4, 2, 2, 48, DH), jnp.bfloat16),
+            pltpu.SemaphoreType.DMA((12,)),
+            pltpu.SemaphoreType.DMA((4,)),
+        ],
         name="split_heads",
-    )(queries, keys, values)
+    )(queries, keys, values).reshape(HEADS, 48, DH)
 
 
 def doc_start(positions, starts):

time: 117 us -> 116 us (level)
  the two profiles are of different devices: /device:TPU:15 before, /device:TPU:72 now
where the time goes in v7:
time: 116 us
  blocking collectives  41 us (35%)
  waiting for transfers between devices  34.6 us (30%)
  starting transfers between devices  23.3 us (20%)
  Pallas kernels  15.4 us (13%)
  other arithmetic  1.43 us (1%)
    all_to_all x1, blocking collectives, per_device(): lax.all_to_all(parted, HEAD_AXES, split_axis=0, concat_axis=0, tiled=True)  41 us
    ppermute x1, waiting for transfers between devices, gather_row(): near = lax.ppermute(mine, row, ring)  15.3 us
    pallas_call x2, Pallas kernels, attend(): pl.pallas_call(attend_kernel, out_shape=jax.ShapeDtypeStruct((ROWS + extr...  13.3 us
    ppermute x1, waiting for transfers between devices, per_device(): same = lax.ppermute(staying, moved, to_owner(0))  11.3 us
    ppermute x1, waiting for transfers between devices, gather_row(): far = lax.ppermute(near, row, ring)  6.49 us
    ppermute x1, starting transfers between devices, per_device(): same = lax.ppermute(staying, moved, to_owner(0))  4.97 us
    ppermute x1, starting transfers between devices, gather_row(): near = lax.ppermute(mine, row, ring)  3.39 us
    ppermute x1, starting transfers between devices, per_device(): other = lax.ppermute(crossing, moved, to_owner(1))[:512]  2.7 us
  transfers between devices with their start and end apart: 9, of which 4 were waited for; matrix products, arithmetic and copies ran while one was open for 1% of the time, Pallas kernels for 6%

profile of v7, /device:TPU:72, one launch (start us, length us, event | category | flops | bytes accessed | tf_op | source)
XLA Modules:
  0.0 116.0 jit_solution(12619543093601935495)
XLA Ops:
  0.0 2.1 %split_heads.1 = bf16[4,2,4,2,48,128]{5,4,3,2,1,0:T(8,128)(2,1)} custom-call(bf16[16,8192]{1,0:T(8,128)(2,1)} %q_ref.1, bf16[16,8192]{1,0:T(8,128)(2,1)} %k_ref.1, bf16[16,8192]{1,0:T(8,128)(2,1)} %v_ref.1), custom_call_target="tpu_custom_call" | custom-call | tf_op jit(solution)/shard_map/split_heads/pallas_call | solution.py:50
  2.1 41.0 %all_to_all.5 = bf16[64,48,128]{2,1,0:T(8,128)(2,1)S(1)} all-to-all(bf16[64,48,128]{2,1,0:T(8,128)(2,1)} %bitcast.33), channel_id=1, replica_groups=mesh['x'=4,'yl'=4,'core'=2,'zh'=2,'zl'=4,'yh'=2] {'yl','zh','zl','yh'}, dimensions={0} | all-to-all | bytes 1572864 | tf_op jit(solution)/shard_map/all_to_all | solution.py:258
  43.1 3.4 %collective-permute-start.1 = (bf16[64,48,128]{2,1,0:T(8,128)(2,1)S(1)}, bf16[64,48,128]{2,1,0:T(8,128)(2,1)S(1)}, u32[]{:S(2)}, u32[]{:S(2)}) collective-permute-start(bf16[64,48,128]{2,1,0:T(8,128)(2,1)S(1)} %all_to_all.5), channel_id=1, source_target_pairs={{0,128},{16,400},{128,256},{144,16},{256,384},{272,144},{384,0},{4... | collective-permute-start | bytes 2359304 | tf_op jit(solution)/shard_map/ppermute | solution.py:226
  46.5 1.9 %collective-permute-start.2 = (bf16[64,48,128]{2,1,0:T(8,128)(2,1)S(1)}, bf16[64,48,128]{2,1,0:T(8,128)(2,1)S(1)}, u32[]{:S(2)}, u32[]{:S(2)}) collective-permute-start(bf16[64,48,128]{2,1,0:T(8,128)(2,1)S(1)} %all_to_all.5), channel_id=1, source_target_pairs={{0,400},{16,128},{128,16},{144,256},{256,144},{272,384},{384,272},... | collective-permute-start | bytes 2359304 | tf_op jit(solution)/shard_map/ppermute | solution.py:227
  48.4 15.3 %collective-permute-done.1 = bf16[64,48,128]{2,1,0:T(8,128)(2,1)S(1)} collective-permute-done((bf16[64,48,128]{2,1,0:T(8,128)(2,1)S(1)}, bf16[64,48,128]{2,1,0:T(8,128)(2,1)S(1)}, u32[]{:S(2)}, u32[]{:S(2)}) %collective-permute-start.1) | collective-permute-done | bytes 786464 | tf_op jit(solution)/shard_map/ppermute | solution.py:226
  63.7 2.2 %collective-permute-start.3 = (bf16[64,48,128]{2,1,0:T(8,128)(2,1)S(1)}, bf16[64,48,128]{2,1,0:T(8,128)(2,1)S(1)}, u32[]{:S(2)}, u32[]{:S(2)}) collective-permute-start(bf16[64,48,128]{2,1,0:T(8,128)(2,1)S(1)} %collective-permute-done.1), channel_id=1, source_target_pairs={{0,128},{16,400},{128,256},{144,16},{256,384},{272,144},{384,0},{4... | collective-permute-start | bytes 2359304 | tf_op jit(solution)/shard_map/ppermute | solution.py:229
  65.9 0.0 copy-start.1
  65.9 0.0 copy-start
  65.9 0.1 stack.35.home_ref
  66.0 1.9 %collective-permute-start = (bf16[64,48,128]{2,1,0:T(8,128)(2,1)S(1)}, bf16[64,48,128]{2,1,0:T(8,128)(2,1)S(1)}, u32[]{:S(2)}, u32[]{:S(2)}) collective-permute-start(bf16[64,48,128]{2,1,0:T(8,128)(2,1)S(1)} %all_to_all.5), channel_id=1, source_target_pairs={{0,16},{16,0},{128,144},{144,128},{256,272},{272,256},{384,400},{4... | collective-permute-start | bytes 2359304 | tf_op jit(solution)/shard_map/ppermute | solution.py:228
  67.9 2.4 %collective-permute-start.4 = (bf16[64,48,128]{2,1,0:T(8,128)(2,1)S(1)}, bf16[64,48,128]{2,1,0:T(8,128)(2,1)S(1)}, u32[]{:S(2)}, u32[]{:S(2)}) collective-permute-start(bf16[64,48,128]{2,1,0:T(8,128)(2,1)S(1)} %collective-permute-done.1), channel_id=1, source_target_pairs={{0,16},{16,0},{128,144},{144,128},{256,272},{272,256},{384,400},{4... | collective-permute-start | bytes 2359304 | tf_op jit(solution)/shard_map/ppermute | solution.py:230
  70.3 0.0 collective-permute-done.2
  70.3 1.9 %collective-permute-start.5 = (bf16[64,48,128]{2,1,0:T(8,128)(2,1)S(1)}, bf16[64,48,128]{2,1,0:T(8,128)(2,1)S(1)}, u32[]{:S(2)}, u32[]{:S(2)}) collective-permute-start(bf16[64,48,128]{2,1,0:T(8,128)(2,1)S(1)} %collective-permute-done.2), channel_id=1, source_target_pairs={{0,16},{16,0},{128,144},{144,128},{256,272},{272,256},{384,400},{4... | collective-permute-start | bytes 2359304 | tf_op jit(solution)/shard_map/ppermute | solution.py:231
  72.3 6.5 %collective-permute-done.3 = bf16[64,48,128]{2,1,0:T(8,128)(2,1)S(1)} collective-permute-done((bf16[64,48,128]{2,1,0:T(8,128)(2,1)S(1)}, bf16[64,48,128]{2,1,0:T(8,128)(2,1)S(1)}, u32[]{:S(2)}, u32[]{:S(2)}) %collective-permute-start.3) | collective-permute-done | bytes 786464 | tf_op jit(solution)/shard_map/ppermute | solution.py:229
  78.8 1.9 %collective-permute-start.6 = (bf16[64,48,128]{2,1,0:T(8,128)(2,1)S(1)}, bf16[64,48,128]{2,1,0:T(8,128)(2,1)S(1)}, u32[]{:S(2)}, u32[]{:S(2)}) collective-permute-start(bf16[64,48,128]{2,1,0:T(8,128)(2,1)S(1)} %collective-permute-done.3), channel_id=1, source_target_pairs={{0,16},{16,0},{128,144},{144,128},{256,272},{272,256},{384,400},{4... | collective-permute-start | bytes 2359304 | tf_op jit(solution)/shard_map/ppermute | solution.py:232
  80.7 0.0 copy-done.1
  80.7 0.1 select_reduce_fusion.2.start_ref
  80.8 0.0 copy-done
  80.8 0.1 convert_reduce_fusion
  81.0 0.1 select_reduce_fusion.slab_ref
  81.1 0.2 convert_reduce_fusion.1
  81.2 0.1 select_reduce_fusion.1.slab_ref
  81.4 0.0 collective-permute-done
  81.4 0.0 collective-permute-done.5
  81.4 0.0 collective-permute-done.4
  81.4 1.5 %collective-permute-done.6 = bf16[64,48,128]{2,1,0:T(8,128)(2,1)S(1)} collective-permute-done((bf16[64,48,128]{2,1,0:T(8,128)(2,1)S(1)}, bf16[64,48,128]{2,1,0:T(8,128)(2,1)S(1)}, u32[]{:S(2)}, u32[]{:S(2)}) %collective-permute-start.6) | collective-permute-done | bytes 786464 | tf_op jit(solution)/shard_map/ppermute | solution.py:232
  82.9 6.7 %attend.3 = bf16[528,128]{1,0:T(8,128)(2,1)S(1)} custom-call(s32[32]{0:T(128)S(1)} %select_reduce_fusion.slab_ref, s32[8]{0:T(128)S(1)} %select_reduce_fusion.2.start_ref, s32[8]{0:T(128)S(1)} %stack.35.home_ref, bf16[4,16,48,128]{3,2,1,0:T(8,128)(2,1)S(1)} %bitcast.17, bf16[4,16,48,128]{3,2,1,0:T(8,128)(2,1)S(1)} %bitcast.25, ...), custom_call_target="tpu_custom_call" | custom-call | flops 2000000000 | bytes 8388608 | tf_op jit(solution)/shard_map/attend/pallas_call | solution.py:170
  89.6 2.7 %collective-permute-start.8 = (bf16[528,128]{1,0:T(8,128)(2,1)S(1)}, bf16[528,128]{1,0:T(8,128)(2,1)S(1)}, u32[]{:S(2)}, u32[]{:S(2)}) collective-permute-start(bf16[528,128]{1,0:T(8,128)(2,1)S(1)} %attend.3), channel_id=1, source_target_pairs={{0,1},{1,0},{2,129},{3,128},{4,257},{5,256},{6,385},{7,384},{8,17}... | collective-permute-start | bytes 405512 | tf_op jit(solution)/shard_map/ppermute | solution.py:262
  92.3 6.7 %attend.2 = bf16[512,128]{1,0:T(8,128)(2,1)S(1)} custom-call(s32[32]{0:T(128)S(1)} %select_reduce_fusion.1.slab_ref, s32[8]{0:T(128)S(1)} %select_reduce_fusion.2.start_ref, s32[8]{0:T(128)S(1)} %stack.35.home_ref, bf16[4,16,48,128]{3,2,1,0:T(8,128)(2,1)S(1)} %bitcast.18, bf16[4,16,48,128]{3,2,1,0:T(8,128)(2,1)S(1)} %bitcast.26, ...), custom_call_target="tpu_custom_call" | custom-call | flops 2000000000 | bytes 8388608 | tf_op jit(solution)/shard_map/attend/pallas_call | solution.py:170
  99.0 5.0 %collective-permute-start.7 = (bf16[512,128]{1,0:T(8,128)(2,1)S(1)}, bf16[512,128]{1,0:T(8,128)(2,1)S(1)}, u32[]{:S(2)}, u32[]{:S(2)}) collective-permute-start(bf16[512,128]{1,0:T(8,128)(2,1)S(1)} %attend.2), channel_id=1, source_target_pairs={{0,0},{1,1},{2,128},{3,129},{4,256},{5,257},{6,384},{7,385},{8,16}... | collective-permute-start | bytes 393224 | tf_op jit(solution)/shard_map/ppermute | solution.py:264
  104.0 11.3 %collective-permute-done.7 = bf16[512,128]{1,0:T(8,128)(2,1)S(1)} collective-permute-done((bf16[512,128]{1,0:T(8,128)(2,1)S(1)}, bf16[512,128]{1,0:T(8,128)(2,1)S(1)}, u32[]{:S(2)}, u32[]{:S(2)}) %collective-permute-start.7) | collective-permute-done | bytes 131104 | tf_op jit(solution)/shard_map/ppermute | solution.py:264
  115.2 0.0 collective-permute-done.8
  115.3 0.7 pad_maximum_fusion
  (2 shorter events, 0.0 us)
Async XLA Ops:
  43.1 20.6 %collective-permute-start.1 = (bf16[64,48,128]{2,1,0:T(8,128)(2,1)S(1)}, bf16[64,48,128]{2,1,0:T(8,128)(2,1)S(1)}, u32[]{:S(2)}, u32[]{:S(2)}) collective-permute-start(bf16[64,48,128]{2,1,0:T(8,128)(2,1)S(1)} %all_to_all.5), channel_id=1, source_target_pairs={{0,128},{16,400},{128,256},{144,16},{256,384},{272,144},{384,0},{4... | collective-permute-start | bytes 2359304 | tf_op jit(solution)/shard_map/ppermute | solution.py:226
  46.5 23.9 %collective-permute-start.2 = (bf16[64,48,128]{2,1,0:T(8,128)(2,1)S(1)}, bf16[64,48,128]{2,1,0:T(8,128)(2,1)S(1)}, u32[]{:S(2)}, u32[]{:S(2)}) collective-permute-start(bf16[64,48,128]{2,1,0:T(8,128)(2,1)S(1)} %all_to_all.5), channel_id=1, source_target_pairs={{0,400},{16,128},{128,16},{144,256},{256,144},{272,384},{384,272},... | collective-permute-start | bytes 2359304 | tf_op jit(solution)/shard_map/ppermute | solution.py:227
  63.7 15.1 %collective-permute-start.3 = (bf16[64,48,128]{2,1,0:T(8,128)(2,1)S(1)}, bf16[64,48,128]{2,1,0:T(8,128)(2,1)S(1)}, u32[]{:S(2)}, u32[]{:S(2)}) collective-permute-start(bf16[64,48,128]{2,1,0:T(8,128)(2,1)S(1)} %collective-permute-done.1), channel_id=1, source_target_pairs={{0,128},{16,400},{128,256},{144,16},{256,384},{272,144},{384,0},{4... | collective-permute-start | bytes 2359304 | tf_op jit(solution)/shard_map/ppermute | solution.py:229
  65.9 14.8 %copy-start.1 = (s32[8]{0:T(128)S(1)}, s32[8]{0:T(128)}, u32[]{:S(2)}) copy-start(s32[8]{0:T(128)} %param.8) | copy-start | bytes 100
  65.9 14.9 %copy-start = (s32[512]{0:T(512)S(1)}, s32[512]{0:T(512)}, u32[]{:S(2)}) copy-start(s32[512]{0:T(512)} %param.9) | copy-start | bytes 6148
  66.0 15.4 %collective-permute-start = (bf16[64,48,128]{2,1,0:T(8,128)(2,1)S(1)}, bf16[64,48,128]{2,1,0:T(8,128)(2,1)S(1)}, u32[]{:S(2)}, u32[]{:S(2)}) collective-permute-start(bf16[64,48,128]{2,1,0:T(8,128)(2,1)S(1)} %all_to_all.5), channel_id=1, source_target_pairs={{0,16},{16,0},{128,144},{144,128},{256,272},{272,256},{384,400},{4... | collective-permute-start | bytes 2359304 | tf_op jit(solution)/shard_map/ppermute | solution.py:228
  67.9 13.5 %collective-permute-start.4 = (bf16[64,48,128]{2,1,0:T(8,128)(2,1)S(1)}, bf16[64,48,128]{2,1,0:T(8,128)(2,1)S(1)}, u32[]{:S(2)}, u32[]{:S(2)}) collective-permute-start(bf16[64,48,128]{2,1,0:T(8,128)(2,1)S(1)} %collective-permute-done.1), channel_id=1, source_target_pairs={{0,16},{16,0},{128,144},{144,128},{256,272},{272,256},{384,400},{4... | collective-permute-start | bytes 2359304 | tf_op jit(solution)/shard_map/ppermute | solution.py:230
  70.3 11.0 %collective-permute-start.5 = (bf16[64,48,128]{2,1,0:T(8,128)(2,1)S(1)}, bf16[64,48,128]{2,1,0:T(8,128)(2,1)S(1)}, u32[]{:S(2)}, u32[]{:S(2)}) collective-permute-start(bf16[64,48,128]{2,1,0:T(8,128)(2,1)S(1)} %collective-permute-done.2), channel_id=1, source_target_pairs={{0,16},{16,0},{128,144},{144,128},{256,272},{272,256},{384,400},{4... | collective-permute-start | bytes 2359304 | tf_op jit(solution)/shard_map/ppermute | solution.py:231
  78.8 4.2 %collective-permute-start.6 = (bf16[64,48,128]{2,1,0:T(8,128)(2,1)S(1)}, bf16[64,48,128]{2,1,0:T(8,128)(2,1)S(1)}, u32[]{:S(2)}, u32[]{:S(2)}) collective-permute-start(bf16[64,48,128]{2,1,0:T(8,128)(2,1)S(1)} %collective-permute-done.3), channel_id=1, source_target_pairs={{0,16},{16,0},{128,144},{144,128},{256,272},{272,256},{384,400},{4... | collective-permute-start | bytes 2359304 | tf_op jit(solution)/shard_map/ppermute | solution.py:232
  89.6 25.6 %collective-permute-start.8 = (bf16[528,128]{1,0:T(8,128)(2,1)S(1)}, bf16[528,128]{1,0:T(8,128)(2,1)S(1)}, u32[]{:S(2)}, u32[]{:S(2)}) collective-permute-start(bf16[528,128]{1,0:T(8,128)(2,1)S(1)} %attend.3), channel_id=1, source_target_pairs={{0,1},{1,0},{2,129},{3,128},{4,257},{5,256},{6,385},{7,384},{8,17}... | collective-permute-start | bytes 405512 | tf_op jit(solution)/shard_map/ppermute | solution.py:262
  99.0 16.3 %collective-permute-start.7 = (bf16[512,128]{1,0:T(8,128)(2,1)S(1)}, bf16[512,128]{1,0:T(8,128)(2,1)S(1)}, u32[]{:S(2)}, u32[]{:S(2)}) collective-permute-start(bf16[512,128]{1,0:T(8,128)(2,1)S(1)} %attend.2), channel_id=1, source_target_pairs={{0,0},{1,1},{2,128},{3,129},{4,256},{5,257},{6,384},{7,385},{8,16}... | collective-permute-start | bytes 393224 | tf_op jit(solution)/shard_map/ppermute | solution.py:264
